TPU v7x, 512 devices: a whole 4x4x16 slice. The times are simulated.
512 devices in a mesh: seq: 32 (over z, core), head: 16 (over x, y).
Axes of the slice: x: 4, y: 4, z: 16, core: 2. Of those that a mesh axis runs over, the one named last changes fastest.
Arguments:
- queries: bfloat16 [12288, 12288], P('seq', 'head'), may hold values from -2.5 to 2.5
- key_states: bfloat16 [12288, 1024], P('seq'), may hold values from -2.5 to 2.5
- value_states: bfloat16 [12288, 1024], P('seq'), may hold values from -4 to 4
- attn_out: bfloat16 [12288, 12288], P('seq', 'head'), may hold values from -4 to 4
- grad_out: bfloat16 [12288, 12288], P('seq', 'head'), may hold values from -4 to 4
- log_norm: bfloat16 [96, 12288], P('head', 'seq'), may hold values from 0.1 to 9
- lengths: int32 [30], replicated, may hold values from 1 to 1153, as said below
- block_plan: int32 [96], replicated, may hold values from 0 to 95, as said below
Outputs:
- query_grad: bfloat16 [12288, 12288], P('seq', 'head')
- key_grad: bfloat16 [12288, 1024], P('seq', 'head')
- value_grad: bfloat16 [12288, 1024], P('seq', 'head')
Inputs may be any that keep to these rules, and one draw needn't show every extreme that they name: The documents' lengths in their order along the sequence; they sum to 12288, and exactly one of them has 1153 tokens. `block_plan`: a permutation of the 96 blocks of 128 query tokens; slot s belongs to the device of index s // 3 along seq and names a block that lies on that device or on the device half the axis away.
All inputs are finite; a program needn't handle non-finite values.
Results may differ from a plain program's by a relative error of at most 0.015.
Values may be sent and summed in bfloat16 or wider, within the bound.
No kernel may reach another device: no remote copies, remote signals or barrier semaphores. Data moves between devices by JAX's collectives and lax.ppermute only.
A program may use at most 128 MiB of HBM per device.

v0:
```python
import jax
import jax.numpy as jnp
from jax import lax
from jax.sharding import PartitionSpec as P

HEAD_DIM = 128
BLOCK = 128


back_shards = 3


def from_behind(value, axis, steps):
    count = lax.axis_size(axis)
    first, last = (max(0, -steps), min(count, count - steps))
    return lax.ppermute(value, axis, [(source, source + steps) for source in range(first, last)])


def swapped(array, axis, apart):
    return lax.ppermute(array, axis, [(i, i ^ 1 << apart) for i in range(lax.axis_size(axis))])


def doc_index(positions, doc_ends):
    return jnp.sum((positions[:, None] >= doc_ends[None, :]).astype(jnp.int32), axis=1)


def tile_grads(
    query_rows,
    outgrad_rows,
    norm_rows,
    delta_rows,
    key_rows,
    value_rows,
    query_pos,
    key_pos,
    doc_ends,
    scaling,
):
    scores = (
        jnp.einsum("qhd,kd->hqk", query_rows, key_rows, preferred_element_type=jnp.float32)
        * scaling
    )
    allowed = (
        (doc_index(query_pos, doc_ends)[:, None] == doc_index(key_pos, doc_ends)[None, :])
        & (key_pos[None, :] <= query_pos[:, None])
        & (key_pos[None, :] >= 0)
    )
    weights = jnp.where(allowed[None], jnp.exp(scores - norm_rows[:, :, None]), 0.0)
    weights_half = weights.astype(jnp.bfloat16)
    prob_grad = jnp.einsum(
        "qhd,kd->hqk", outgrad_rows, value_rows, preferred_element_type=jnp.float32
    )
    score_grad = (weights * (prob_grad - delta_rows[:, :, None])).astype(jnp.bfloat16)
    query_grad = (
        jnp.einsum("hqk,kd->qhd", score_grad, key_rows, preferred_element_type=jnp.float32)
        * scaling
    )
    key_grad = (
        jnp.einsum("hqk,qhd->kd", score_grad, query_rows, preferred_element_type=jnp.float32)
        * scaling
    )
    value_grad = jnp.einsum(
        "hqk,qhd->kd", weights_half, outgrad_rows, preferred_element_type=jnp.float32
    )
    return (query_grad, key_grad, value_grad)


def block_grads(
    query_blocks,
    outgrad_blocks,
    norm_blocks,
    delta_blocks,
    key_blocks,
    value_blocks,
    query_pos,
    key_pos,
    doc_ends,
    scaling,
):
    mapped = jax.vmap(tile_grads, in_axes=(0, 0, 0, 0, 0, 0, 0, 0, None, None))
    return mapped(
        query_blocks,
        outgrad_blocks,
        norm_blocks,
        delta_blocks,
        key_blocks,
        value_blocks,
        query_pos,
        key_pos,
        doc_ends,
        scaling,
    )


def on_device(queries, key_states, value_states, attn_out, grad_out, log_norm, lengths, block_plan):
    tokens_dev = queries.shape[0]
    heads_dev = queries.shape[1] // HEAD_DIM
    feature = heads_dev * HEAD_DIM
    block_rows = BLOCK
    per_device = tokens_dev // block_rows
    window_rows = (back_shards + 1) * tokens_dev
    scaling = HEAD_DIM ** (-0.5)
    seq_index = lax.axis_index("seq")
    head_index = lax.axis_index("head")
    top_bit = lax.axis_size("seq").bit_length() - 2
    kv_group = head_index // 2
    own_keys = lax.dynamic_slice_in_dim(key_states, kv_group * HEAD_DIM, HEAD_DIM, 1)
    own_values = lax.dynamic_slice_in_dim(value_states, kv_group * HEAD_DIM, HEAD_DIM, 1)
    earlier = []
    for distance in range(back_shards, 0, -1):
        earlier.append(from_behind((own_keys, own_values), "seq", distance))
    key_win = jnp.concatenate([shifted_pair[0] for shifted_pair in earlier] + [own_keys], axis=0)
    value_win = jnp.concatenate(
        [shifted_pair[1] for shifted_pair in earlier] + [own_values], axis=0
    )
    doc_ends = jnp.cumsum(lengths)
    offsets = jnp.arange(block_rows, dtype=jnp.int32)
    window_offsets = jnp.arange(window_rows, dtype=jnp.int32) - back_shards * tokens_dev
    slot_blocks = lax.dynamic_slice_in_dim(block_plan, seq_index * per_device, per_device)
    source_dev = slot_blocks // per_device
    local_block = slot_blocks % per_device
    from_partner = (source_dev != seq_index).astype(jnp.int32)
    block_shape = (per_device, block_rows, heads_dev, HEAD_DIM)
    query_blocks = queries.reshape(block_shape)
    outgrad_blocks = grad_out.reshape(block_shape)
    attn_blocks = attn_out.reshape(block_shape)
    delta_blocks = jnp.sum(
        outgrad_blocks.astype(jnp.float32) * attn_blocks.astype(jnp.float32), axis=3
    ).transpose(0, 2, 1)
    norm_blocks = (
        log_norm.astype(jnp.float32).reshape(heads_dev, per_device, block_rows).transpose(1, 0, 2)
    )
    key_blocks = jnp.broadcast_to(key_win, (per_device,) + key_win.shape)
    value_blocks = jnp.broadcast_to(value_win, (per_device,) + value_win.shape)
    block_index = seq_index * per_device + jnp.arange(per_device, dtype=jnp.int32)
    window_start = jnp.broadcast_to(seq_index * tokens_dev, (per_device,))
    query_pos = block_index[:, None] * block_rows + offsets[None, :]
    key_pos = window_start[:, None] + window_offsets[None, :]
    query_grads, key_grads, value_grads = block_grads(
        query_blocks,
        outgrad_blocks,
        norm_blocks,
        delta_blocks,
        key_blocks,
        value_blocks,
        query_pos,
        key_pos,
        doc_ends,
        scaling,
    )
    query_half = query_grads.reshape(tokens_dev, feature).astype(jnp.bfloat16)
    partner_half = swapped(query_half, "seq", top_bit)
    stacked_grads = jnp.stack([query_half, partner_half]).reshape(
        2, per_device, block_rows, feature
    )
    query_grad = stacked_grads[from_partner, local_block].reshape(tokens_dev, feature)
    key_acc = jnp.sum(key_grads, axis=0)
    value_acc = jnp.sum(value_grads, axis=0)
    key_own = key_acc[back_shards * tokens_dev :]
    value_own = value_acc[back_shards * tokens_dev :]
    for distance in range(1, back_shards + 1):
        lower_row = (back_shards - distance) * tokens_dev
        arriving = from_behind(
            (
                key_acc[lower_row : lower_row + tokens_dev],
                value_acc[lower_row : lower_row + tokens_dev],
            ),
            "seq",
            -distance,
        )
        key_own = key_own + arriving[0]
        value_own = value_own + arriving[1]
    half_cols = HEAD_DIM // 2
    column_side = head_index % 2
    keep_key = lax.dynamic_slice_in_dim(key_own, column_side * half_cols, half_cols, 1)
    keep_value = lax.dynamic_slice_in_dim(value_own, column_side * half_cols, half_cols, 1)
    send_key = lax.dynamic_slice_in_dim(key_own, (1 - column_side) * half_cols, half_cols, 1)
    send_value = lax.dynamic_slice_in_dim(value_own, (1 - column_side) * half_cols, half_cols, 1)
    arriving = swapped((send_key, send_value), "head", 0)
    key_grad = keep_key + arriving[0]
    value_grad = keep_value + arriving[1]
    return (query_grad, key_grad.astype(jnp.bfloat16), value_grad.astype(jnp.bfloat16))


def solution(mesh):
    placed = (
        P("seq", "head"),
        P("seq", None),
        P("seq", None),
        P("seq", "head"),
        P("seq", "head"),
        P("head", "seq"),
        P(),
        P(),
    )
    return jax.shard_map(
        on_device,
        mesh=mesh,
        in_specs=placed,
        out_specs=(P("seq", "head"), P("seq", "head"), P("seq", "head")),
        check_vma=False,
    )
```

profile of v0, /device:TPU:45, one launch (start us, length us, event | category | flops | bytes accessed | tf_op | source)
XLA Modules:
  0.0 159.3 jit_solution(15701479236225423738)
XLA Ops:
  0.7 1.1 copy-done
  1.8 5.5 %collective-permute-start = (bf16[384,128]{1,0:T(8,128)(2,1)S(1)}, bf16[384,128]{1,0:T(8,128)(2,1)}, u32[]{:S(2)}, u32[]{:S(2)}) collective-permute-start(bf16[384,128]{1,0:T(8,128)(2,1)S(1)} %constant_dynamic-slice_fusion.3), channel_id=1, source_target_pairs={{0,48},{16,64},{32,80},{48,96},{64,112},{80,128},{96,144},{112,160... | collective-permute-start | bytes 294920 | tf_op jit(solution)/shard_map/ppermute | solution.py:16
  7.3 4.8 %collective-permute-start.1 = (bf16[384,128]{1,0:T(8,128)(2,1)S(1)}, bf16[384,128]{1,0:T(8,128)(2,1)}, u32[]{:S(2)}, u32[]{:S(2)}) collective-permute-start(bf16[384,128]{1,0:T(8,128)(2,1)S(1)} %constant_dynamic-slice_fusion.3), channel_id=1, source_target_pairs={{0,32},{16,48},{32,64},{48,80},{64,96},{80,112},{96,128},{112,144}... | collective-permute-start | bytes 294920 | tf_op jit(solution)/shard_map/ppermute | solution.py:16
  12.0 2.2 %collective-permute-start.2 = (bf16[384,128]{1,0:T(8,128)(2,1)S(1)}, bf16[384,128]{1,0:T(8,128)(2,1)}, u32[]{:S(2)}, u32[]{:S(2)}) collective-permute-start(bf16[384,128]{1,0:T(8,128)(2,1)S(1)} %constant_dynamic-slice_fusion.3), channel_id=1, source_target_pairs={{0,16},{16,32},{32,48},{48,64},{64,80},{80,96},{96,112},{112,128},... | collective-permute-start | bytes 294920 | tf_op jit(solution)/shard_map/ppermute | solution.py:16
  15.1 5.0 %collective-permute-start.3 = (bf16[384,128]{1,0:T(8,128)(2,1)S(1)}, bf16[384,128]{1,0:T(8,128)(2,1)}, u32[]{:S(2)}, u32[]{:S(2)}) collective-permute-start(bf16[384,128]{1,0:T(8,128)(2,1)S(1)} %constant_dynamic-slice_fusion.2), channel_id=1, source_target_pairs={{0,48},{16,64},{32,80},{48,96},{64,112},{80,128},{96,144},{112,160... | collective-permute-start | bytes 294920 | tf_op jit(solution)/shard_map/ppermute | solution.py:16
  20.1 3.5 %collective-permute-start.4 = (bf16[384,128]{1,0:T(8,128)(2,1)S(1)}, bf16[384,128]{1,0:T(8,128)(2,1)}, u32[]{:S(2)}, u32[]{:S(2)}) collective-permute-start(bf16[384,128]{1,0:T(8,128)(2,1)S(1)} %constant_dynamic-slice_fusion.2), channel_id=1, source_target_pairs={{0,32},{16,48},{32,64},{48,80},{64,96},{80,112},{96,128},{112,144}... | collective-permute-start | bytes 294920 | tf_op jit(solution)/shard_map/ppermute | solution.py:16
  26.2 2.4 %reshape.104 = bf16[3,128,6,128]{3,2,1,0:T(8,128)(2,1)} reshape(bf16[384,768]{1,0:T(8,128)(2,1)} %param.8) | data formatting | bytes 1179648 | tf_op jit(solution)/shard_map/reshape | solution.py:124
  28.6 1.3 convert_bitcast_fusion
  29.9 1.8 %reshape.106 = bf16[3,128,6,128]{3,2,1,0:T(8,128)(2,1)S(1)} reshape(bf16[384,768]{1,0:T(8,128)(2,1)} %param.12) | data formatting | bytes 1179648 | tf_op jit(solution)/shard_map/reshape | solution.py:125
  31.7 1.7 %reshape.108 = f32[3,128,6,128]{3,2,1,0:T(8,128)S(1)} reshape(bf16[384,768]{1,0:T(8,128)(2,1)} %param.11) | data formatting | bytes 1769472 | tf_op jit(solution)/shard_map/convert_element_type | solution.py:128
  33.9 3.2 %and_and_fusion = pred[3,128,1536]{1,2,0:T(8,128)(4,1)S(1)} fusion(s32[3,128]{1,0:T(4,128)S(1)} %iota_add_fusion, s32[3,1536]{1,0:T(4,128)} %convert_reduce_fusion, s32[3,128]{1,0:T(4,128)} %convert_reduce_fusion.1, s32[1536]{0:T(1024)S(1)} %add_add_fusion, pred[1536]{0:T(1024)(128)(4,1)S(1)} %broadcast_compare_fusion), kind=kLoop, calls=%fused_computation.13 | loop fusion | flops 2359296 | bytes 619008 | tf_op jit(solution)/shard_map/vmap()/and | solution.py:44
  37.9 2.8 %collective-permute-start.5 = (bf16[384,128]{1,0:T(8,128)(2,1)S(1)}, bf16[384,128]{1,0:T(8,128)(2,1)S(1)}, u32[]{:S(2)}, u32[]{:S(2)}) collective-permute-start(bf16[384,128]{1,0:T(8,128)(2,1)S(1)} %constant_dynamic-slice_fusion.2), channel_id=1, source_target_pairs={{0,16},{16,32},{32,48},{48,64},{64,80},{80,96},{96,112},{112,128},... | collective-permute-start | bytes 294920 | tf_op jit(solution)/shard_map/ppermute | solution.py:16
  42.0 7.1 %fusion.4 = (bf16[3,6,128,1536]{2,3,1,0:T(8,128)(2,1)}, f32[3,1536,128,6]{2,1,3,0:T(8,128)S(1)}) fusion(f32[3,6,128]{2,1,0:T(8,128)} %convert_bitcast_fusion, pred[3,128,1536]{1,2,0:T(8,128)(4,1)S(1)} %and_and_fusion, bf16[3,128,6,128]{3,2,1,0:T(8,128)(2,1)} %reshape.104, bf16[1536,128]{0,1:T(8,128)(2,1)S(1)} %copy.48), kind=kOutput, calls=%fused_computation.7 | convolution fusion | flops 920125440 | bytes 22815744 | tf_op jit(solution)/shard_map/vmap(qhd,kd->hqk)/dot_general | solution.py:40
  50.1 6.7 %fusion.1 = bf16[3,6,128,1536]{2,3,1,0:T(8,128)(2,1)} fusion(f32[3,1536,128,6]{2,1,3,0:T(8,128)S(1)} %get-tuple-element.16, f32[3,6,128]{2,1,0:T(8,128)S(1)} %copy.54, f32[3,6,128]{2,1,0:T(8,128)S(1)} %copy-done.5, pred[3,128,1536]{1,2,0:T(8,128)(4,1)S(1)} %and_and_fusion, bf16[1536,128]{1,0:T(8,128)(2,1)S(1)} %pad_maximum_fusion.2, ...), kind=kOutput, calls=%fused_computation.3 | convolution fusion | flops 927203328 | bytes 22824960 | tf_op jit(solution)/shard_map/vmap(qhd,kd->hqk)/dot_general | solution.py:50
  56.7 5.2 %fusion.11 = f32[1536,128]{1,0:T(8,128)S(1)} fusion(bf16[3,6,128,1536]{2,3,1,0:T(8,128)(2,1)} %fusion.1, bf16[3,128,6,128]{3,2,1,0:T(8,128)(2,1)S(1)} %copy-done.2), kind=kOutput, calls=%fused_computation.15 | convolution fusion | flops 906952704 | bytes 8454144 | tf_op jit(solution)/shard_map/vmap(hqk,qhd->kd)/dot_general | solution.py:59
  62.0 4.4 %fusion.12 = bf16[3,128,6,128]{3,1,2,0:T(8,128)(2,1)S(1)} fusion(bf16[3,6,128,1536]{2,3,1,0:T(8,128)(2,1)} %fusion.1, bf16[1536,128]{0,1:T(8,128)(2,1)S(1)} %copy.48), kind=kOutput, calls=%fused_computation.17 | convolution fusion | flops 906559488 | bytes 8060928 | tf_op jit(solution)/shard_map/vmap(hqk,kd->qhd)/dot_general | solution.py:55
  66.4 2.4 %fusion.8 = f32[1536,128]{0,1:T(8,128)S(1)} fusion(bf16[3,6,128,1536]{2,3,1,0:T(8,128)(2,1)S(1)} %copy-done.1, bf16[3,128,6,128]{3,2,1,0:T(8,128)(2,1)S(1)} %reshape.106), kind=kOutput, calls=%fused_computation.12 | convolution fusion | flops 905969664 | bytes 8454144 | tf_op jit(solution)/shard_map/vmap(hqk,qhd->kd)/dot_general | solution.py:62
  69.7 1.9 %collective-permute-start.7 = (f32[384,128]{1,0:T(8,128)}, f32[384,128]{1,0:T(8,128)}, u32[]{:S(2)}, u32[]{:S(2)}) collective-permute-start(f32[384,128]{1,0:T(8,128)} %get-tuple-element.12), channel_id=1, source_target_pairs={{16,0},{32,16},{48,32},{64,48},{80,64},{96,80},{112,96},{128,112},... | collective-permute-start | bytes 589832 | tf_op jit(solution)/shard_map/ppermute | solution.py:16
  71.6 2.1 %collective-permute-start.8 = (f32[384,128]{1,0:T(8,128)}, f32[384,128]{1,0:T(8,128)}, u32[]{:S(2)}, u32[]{:S(2)}) collective-permute-start(f32[384,128]{1,0:T(8,128)} %get-tuple-element.14), channel_id=1, source_target_pairs={{32,0},{48,16},{64,32},{80,48},{96,64},{112,80},{128,96},{144,112}... | collective-permute-start | bytes 589832 | tf_op jit(solution)/shard_map/ppermute | solution.py:16
  73.8 1.9 %collective-permute-start.9 = (f32[384,128]{1,0:T(8,128)}, f32[384,128]{1,0:T(8,128)}, u32[]{:S(2)}, u32[]{:S(2)}) collective-permute-start(f32[384,128]{1,0:T(8,128)} %get-tuple-element.13), channel_id=1, source_target_pairs={{48,0},{64,16},{80,32},{96,48},{112,64},{128,80},{144,96},{160,112... | collective-permute-start | bytes 589832 | tf_op jit(solution)/shard_map/ppermute | solution.py:16
  76.5 1.9 %collective-permute-start.11 = (f32[384,128]{0,1:T(8,128)}, f32[384,128]{0,1:T(8,128)}, u32[]{:S(2)}, u32[]{:S(2)}) collective-permute-start(f32[384,128]{0,1:T(8,128)} %get-tuple-element.9), channel_id=1, source_target_pairs={{16,0},{32,16},{48,32},{64,48},{80,64},{96,80},{112,96},{128,112},... | collective-permute-start | bytes 589832 | tf_op jit(solution)/shard_map/ppermute | solution.py:16
  78.5 1.9 %collective-permute-start.12 = (f32[384,128]{0,1:T(8,128)}, f32[384,128]{0,1:T(8,128)}, u32[]{:S(2)}, u32[]{:S(2)}) collective-permute-start(f32[384,128]{0,1:T(8,128)} %get-tuple-element.11), channel_id=1, source_target_pairs={{32,0},{48,16},{64,32},{80,48},{96,64},{112,80},{128,96},{144,112}... | collective-permute-start | bytes 589832 | tf_op jit(solution)/shard_map/ppermute | solution.py:16
  82.0 1.9 %collective-permute-start.13 = (f32[384,128]{0,1:T(8,128)}, f32[384,128]{0,1:T(8,128)S(1)}, u32[]{:S(2)}, u32[]{:S(2)}) collective-permute-start(f32[384,128]{0,1:T(8,128)} %get-tuple-element.10), channel_id=1, source_target_pairs={{48,0},{64,16},{80,32},{96,48},{112,64},{128,80},{144,96},{160,112... | collective-permute-start | bytes 589832 | tf_op jit(solution)/shard_map/ppermute | solution.py:16
  83.9 15.6 %collective-permute-start.6 = (bf16[384,768]{1,0:T(8,128)(2,1)}, bf16[384,768]{1,0:T(8,128)(2,1)S(1)}, u32[]{:S(2)}, u32[]{:S(2)}) collective-permute-start(bf16[384,768]{1,0:T(8,128)(2,1)} %bitcast.64), channel_id=1, source_target_pairs={{0,256},{16,272},{32,288},{48,304},{64,320},{80,336},{96,352},{112... | collective-permute-start | bytes 1769480 | tf_op jit(solution)/shard_map/ppermute | solution.py:20
  99.5 1.3 fusion.27
  100.9 2.1 %collective-permute-start.10 = (f32[384,64]{1,0:T(8,128)S(1)}, f32[384,64]{1,0:T(8,128)S(1)}, u32[]{:S(2)}, u32[]{:S(2)}) collective-permute-start(f32[384,64]{1,0:T(8,128)S(1)} %constant_dynamic-slice_fusion.1), channel_id=1, source_target_pairs={{0,1},{1,0},{2,3},{3,2},{4,5},{5,4},{6,7},{7,6},{8,9},{9,8},{10,11... | collective-permute-start | bytes 294920 | tf_op jit(solution)/shard_map/ppermute | solution.py:20
  104.1 3.2 %collective-permute-start.14 = (f32[384,64]{0,1:T(8,128)S(1)}, f32[384,64]{0,1:T(8,128)S(1)}, u32[]{:S(2)}, u32[]{:S(2)}) collective-permute-start(f32[384,64]{0,1:T(8,128)S(1)} %constant_dynamic-slice_fusion), channel_id=1, source_target_pairs={{0,1},{1,0},{2,3},{3,2},{4,5},{5,4},{6,7},{7,6},{8,9},{9,8},{10,11... | collective-permute-start | bytes 294920 | tf_op jit(solution)/shard_map/ppermute | solution.py:20
  107.3 2.1 %collective-permute-done.10 = f32[384,64]{1,0:T(8,128)S(1)} collective-permute-done((f32[384,64]{1,0:T(8,128)S(1)}, f32[384,64]{1,0:T(8,128)S(1)}, u32[]{:S(2)}, u32[]{:S(2)}) %collective-permute-start.10) | collective-permute-done | bytes 98336 | tf_op jit(solution)/shard_map/ppermute | solution.py:20
  110.2 1.3 collective-permute-done.14
  112.1 43.8 %collective-permute-done.6 = bf16[384,768]{1,0:T(8,128)(2,1)S(1)} collective-permute-done((bf16[384,768]{1,0:T(8,128)(2,1)}, bf16[384,768]{1,0:T(8,128)(2,1)S(1)}, u32[]{:S(2)}, u32[]{:S(2)}) %collective-permute-start.6) | collective-permute-done | bytes 589856 | tf_op jit(solution)/shard_map/ppermute | solution.py:20
  156.8 1.2 pad_maximum_fusion
  157.9 1.4 gather_fusion
  (51 shorter events, 13.6 us)
Async XLA Ops:
  0.6 1.1 copy-start
  1.8 36.1 %collective-permute-start = (bf16[384,128]{1,0:T(8,128)(2,1)S(1)}, bf16[384,128]{1,0:T(8,128)(2,1)}, u32[]{:S(2)}, u32[]{:S(2)}) collective-permute-start(bf16[384,128]{1,0:T(8,128)(2,1)S(1)} %constant_dynamic-slice_fusion.3), channel_id=1, source_target_pairs={{0,48},{16,64},{32,80},{48,96},{64,112},{80,128},{96,144},{112,160... | collective-permute-start | bytes 294920 | tf_op jit(solution)/shard_map/ppermute | solution.py:16
  7.3 33.5 %collective-permute-start.1 = (bf16[384,128]{1,0:T(8,128)(2,1)S(1)}, bf16[384,128]{1,0:T(8,128)(2,1)}, u32[]{:S(2)}, u32[]{:S(2)}) collective-permute-start(bf16[384,128]{1,0:T(8,128)(2,1)S(1)} %constant_dynamic-slice_fusion.3), channel_id=1, source_target_pairs={{0,32},{16,48},{32,64},{48,80},{64,96},{80,112},{96,128},{112,144}... | collective-permute-start | bytes 294920 | tf_op jit(solution)/shard_map/ppermute | solution.py:16
  12.0 28.7 %collective-permute-start.2 = (bf16[384,128]{1,0:T(8,128)(2,1)S(1)}, bf16[384,128]{1,0:T(8,128)(2,1)}, u32[]{:S(2)}, u32[]{:S(2)}) collective-permute-start(bf16[384,128]{1,0:T(8,128)(2,1)S(1)} %constant_dynamic-slice_fusion.3), channel_id=1, source_target_pairs={{0,16},{16,32},{32,48},{48,64},{64,80},{80,96},{96,112},{112,128},... | collective-permute-start | bytes 294920 | tf_op jit(solution)/shard_map/ppermute | solution.py:16
  15.1 33.9 %collective-permute-start.3 = (bf16[384,128]{1,0:T(8,128)(2,1)S(1)}, bf16[384,128]{1,0:T(8,128)(2,1)}, u32[]{:S(2)}, u32[]{:S(2)}) collective-permute-start(bf16[384,128]{1,0:T(8,128)(2,1)S(1)} %constant_dynamic-slice_fusion.2), channel_id=1, source_target_pairs={{0,48},{16,64},{32,80},{48,96},{64,112},{80,128},{96,144},{112,160... | collective-permute-start | bytes 294920 | tf_op jit(solution)/shard_map/ppermute | solution.py:16
  20.1 28.9 %collective-permute-start.4 = (bf16[384,128]{1,0:T(8,128)(2,1)S(1)}, bf16[384,128]{1,0:T(8,128)(2,1)}, u32[]{:S(2)}, u32[]{:S(2)}) collective-permute-start(bf16[384,128]{1,0:T(8,128)(2,1)S(1)} %constant_dynamic-slice_fusion.2), channel_id=1, source_target_pairs={{0,32},{16,48},{32,64},{48,80},{64,96},{80,112},{96,128},{112,144}... | collective-permute-start | bytes 294920 | tf_op jit(solution)/shard_map/ppermute | solution.py:16
  37.9 11.2 %collective-permute-start.5 = (bf16[384,128]{1,0:T(8,128)(2,1)S(1)}, bf16[384,128]{1,0:T(8,128)(2,1)S(1)}, u32[]{:S(2)}, u32[]{:S(2)}) collective-permute-start(bf16[384,128]{1,0:T(8,128)(2,1)S(1)} %constant_dynamic-slice_fusion.2), channel_id=1, source_target_pairs={{0,16},{16,32},{32,48},{48,64},{64,80},{80,96},{96,112},{112,128},... | collective-permute-start | bytes 294920 | tf_op jit(solution)/shard_map/ppermute | solution.py:16
  41.9 8.1 %copy-start.5 = (f32[3,6,128]{2,1,0:T(8,128)S(1)}, f32[3,6,128]{2,1,0:T(8,128)}, u32[]{:S(2)}) copy-start(f32[3,6,128]{2,1,0:T(8,128)} %convert_bitcast_fusion) | copy-start | bytes 27652
  50.0 6.7 %copy-start.2 = (bf16[3,128,6,128]{3,2,1,0:T(8,128)(2,1)S(1)}, bf16[3,128,6,128]{3,2,1,0:T(8,128)(2,1)}, u32[]{:S(2)}) copy-start(bf16[3,128,6,128]{3,2,1,0:T(8,128)(2,1)} %reshape.104) | copy-start | bytes 1769476
  56.7 9.7 %copy-start.1 = (bf16[3,6,128,1536]{2,3,1,0:T(8,128)(2,1)S(1)}, bf16[3,6,128,1536]{2,3,1,0:T(8,128)(2,1)}, u32[]{:S(2)}) copy-start(bf16[3,6,128,1536]{2,3,1,0:T(8,128)(2,1)} %get-tuple-element.15) | copy-start | bytes 21233668
  62.0 18.4 %copy-start.3 = (f32[1536,128]{1,0:T(8,128)}, f32[1536,128]{1,0:T(8,128)S(1)}, u32[]{:S(2)}) copy-start(f32[1536,128]{1,0:T(8,128)S(1)} %fusion.11) | copy-start | bytes 2359300
  69.7 12.3 %collective-permute-start.7 = (f32[384,128]{1,0:T(8,128)}, f32[384,128]{1,0:T(8,128)}, u32[]{:S(2)}, u32[]{:S(2)}) collective-permute-start(f32[384,128]{1,0:T(8,128)} %get-tuple-element.12), channel_id=1, source_target_pairs={{16,0},{32,16},{48,32},{64,48},{80,64},{96,80},{112,96},{128,112},... | collective-permute-start | bytes 589832 | tf_op jit(solution)/shard_map/ppermute | solution.py:16
  71.6 12.3 %collective-permute-start.8 = (f32[384,128]{1,0:T(8,128)}, f32[384,128]{1,0:T(8,128)}, u32[]{:S(2)}, u32[]{:S(2)}) collective-permute-start(f32[384,128]{1,0:T(8,128)} %get-tuple-element.14), channel_id=1, source_target_pairs={{32,0},{48,16},{64,32},{80,48},{96,64},{112,80},{128,96},{144,112}... | collective-permute-start | bytes 589832 | tf_op jit(solution)/shard_map/ppermute | solution.py:16
  73.8 25.7 %collective-permute-start.9 = (f32[384,128]{1,0:T(8,128)}, f32[384,128]{1,0:T(8,128)}, u32[]{:S(2)}, u32[]{:S(2)}) collective-permute-start(f32[384,128]{1,0:T(8,128)} %get-tuple-element.13), channel_id=1, source_target_pairs={{48,0},{64,16},{80,32},{96,48},{112,64},{128,80},{144,96},{160,112... | collective-permute-start | bytes 589832 | tf_op jit(solution)/shard_map/ppermute | solution.py:16
  76.5 26.4 %collective-permute-start.11 = (f32[384,128]{0,1:T(8,128)}, f32[384,128]{0,1:T(8,128)}, u32[]{:S(2)}, u32[]{:S(2)}) collective-permute-start(f32[384,128]{0,1:T(8,128)} %get-tuple-element.9), channel_id=1, source_target_pairs={{16,0},{32,16},{48,32},{64,48},{80,64},{96,80},{112,96},{128,112},... | collective-permute-start | bytes 589832 | tf_op jit(solution)/shard_map/ppermute | solution.py:16
  78.5 24.5 %collective-permute-start.12 = (f32[384,128]{0,1:T(8,128)}, f32[384,128]{0,1:T(8,128)}, u32[]{:S(2)}, u32[]{:S(2)}) collective-permute-start(f32[384,128]{0,1:T(8,128)} %get-tuple-element.11), channel_id=1, source_target_pairs={{32,0},{48,16},{64,32},{80,48},{96,64},{112,80},{128,96},{144,112}... | collective-permute-start | bytes 589832 | tf_op jit(solution)/shard_map/ppermute | solution.py:16
  82.0 21.0 %collective-permute-start.13 = (f32[384,128]{0,1:T(8,128)}, f32[384,128]{0,1:T(8,128)S(1)}, u32[]{:S(2)}, u32[]{:S(2)}) collective-permute-start(f32[384,128]{0,1:T(8,128)} %get-tuple-element.10), channel_id=1, source_target_pairs={{48,0},{64,16},{80,32},{96,48},{112,64},{128,80},{144,96},{160,112... | collective-permute-start | bytes 589832 | tf_op jit(solution)/shard_map/ppermute | solution.py:16
  83.9 72.0 %collective-permute-start.6 = (bf16[384,768]{1,0:T(8,128)(2,1)}, bf16[384,768]{1,0:T(8,128)(2,1)S(1)}, u32[]{:S(2)}, u32[]{:S(2)}) collective-permute-start(bf16[384,768]{1,0:T(8,128)(2,1)} %bitcast.64), channel_id=1, source_target_pairs={{0,256},{16,272},{32,288},{48,304},{64,320},{80,336},{96,352},{112... | collective-permute-start | bytes 1769480 | tf_op jit(solution)/shard_map/ppermute | solution.py:20
  100.9 8.5 %collective-permute-start.10 = (f32[384,64]{1,0:T(8,128)S(1)}, f32[384,64]{1,0:T(8,128)S(1)}, u32[]{:S(2)}, u32[]{:S(2)}) collective-permute-start(f32[384,64]{1,0:T(8,128)S(1)} %constant_dynamic-slice_fusion.1), channel_id=1, source_target_pairs={{0,1},{1,0},{2,3},{3,2},{4,5},{5,4},{6,7},{7,6},{8,9},{9,8},{10,11... | collective-permute-start | bytes 294920 | tf_op jit(solution)/shard_map/ppermute | solution.py:20
  104.1 7.4 %collective-permute-start.14 = (f32[384,64]{0,1:T(8,128)S(1)}, f32[384,64]{0,1:T(8,128)S(1)}, u32[]{:S(2)}, u32[]{:S(2)}) collective-permute-start(f32[384,64]{0,1:T(8,128)S(1)} %constant_dynamic-slice_fusion), channel_id=1, source_target_pairs={{0,1},{1,0},{2,3},{3,2},{4,5},{5,4},{6,7},{7,6},{8,9},{9,8},{10,11... | collective-permute-start | bytes 294920 | tf_op jit(solution)/shard_map/ppermute | solution.py:20
  155.9 0.8 copy-start.4
where the time goes:
time: 160 us; the launch traced here: 159 us
  starting transfers between devices  56.3 us (35%)
  waiting for transfers between devices  47.2 us (30%)
  matrix products  25.8 us (16%)
  local copies, waits for them, and re-layouts  15.3 us (10%)
  other arithmetic  13.6 us (8%)
    ppermute x3, waiting for transfers between devices, swapped(): lax.ppermute(array, axis, [(i, i ^ 1 << apart) for i in range(lax.axis_si...  47.1 us
    ppermute x12, starting transfers between devices, from_behind(): lax.ppermute(value, axis, [(source, source + steps) for source in range(f...  35.5 us
    ppermute x3, starting transfers between devices, swapped(): lax.ppermute(array, axis, [(i, i ^ 1 << apart) for i in range(lax.axis_si...  20.8 us
    dot_general x1, matrix products, tile_grads(): jnp.einsum('qhd,kd->hqk', query_rows, key_rows, preferred_element_type=jn...  7.09 us
    dot_general x1, matrix products, tile_grads(): jnp.einsum('qhd,kd->hqk', outgrad_rows, value_rows, preferred_element_typ...  6.67 us
    dot_general x1, matrix products, tile_grads(): jnp.einsum('hqk,qhd->kd', score_grad, query_rows, preferred_element_type=...  5.24 us
    dot_general x1, matrix products, tile_grads(): jnp.einsum('hqk,kd->qhd', score_grad, key_rows, preferred_element_type=jn...  4.39 us
    unnamed x14, local copies, waits for them, and re-layouts  3.56 us
  transfers between devices with their start and end apart: 15, of which 3 were waited for; matrix products, arithmetic and copies ran while one was open for 19% of the time, Pallas kernels for 0%

commit v1 on v0

v1 whole, which is shorter than its diff:
```python
import functools

import jax
import jax.numpy as jnp
from jax import lax
from jax.experimental import pallas as pl
from jax.experimental.pallas import tpu as pltpu
from jax.sharding import PartitionSpec as P

HEAD_DIM = 128
BLOCK = 128
BACK = 3
LOG2E = 1.4426950408889634
SCALE = HEAD_DIM ** -0.5


def shifted(value, axis, steps):
    count = lax.axis_size(axis)
    first, last = (max(0, -steps), min(count, count - steps))
    return lax.ppermute(value, axis, [(i, i + steps) for i in range(first, last)])


def swapped(array, axis, apart):
    return lax.ppermute(array, axis, [(i, i ^ apart) for i in range(lax.axis_size(axis))])


def dot(a, b):
    return jnp.dot(a, b, preferred_element_type=jnp.float32)


def dot_nt(a, b):
    return lax.dot_general(a, b, (((1,), (1,)), ((), ())), preferred_element_type=jnp.float32)


def stack_heads(wide_ref, stacked_ref, heads):
    for h in range(heads):
        stacked_ref[pl.ds(h * HEAD_DIM, HEAD_DIM), :] = wide_ref[:, pl.ds(h * HEAD_DIM, HEAD_DIM)]


def tile_grads(kt, vt, qs_ref, dos_ref, lse_ref, delta_ref, allowed, heads):
    scores = dot_nt(kt, qs_ref[...])
    prob_grad = dot_nt(vt, dos_ref[...])
    weights, score_grads = [], []
    for h in range(heads):
        cols = slice(h * BLOCK, (h + 1) * BLOCK)
        lse = lse_ref[h : h + 1, :].astype(jnp.float32) * LOG2E
        w = jnp.where(allowed, jnp.exp2(scores[:, cols] * (SCALE * LOG2E) - lse), 0.0)
        weights.append(w.astype(jnp.bfloat16))
        score_grads.append((w * (prob_grad[:, cols] - delta_ref[h : h + 1, :])).astype(jnp.bfloat16))
    w_half = jnp.concatenate(weights, axis=1)
    s_grad = jnp.concatenate(score_grads, axis=1)
    dv = dot(w_half, dos_ref[...])
    dk = dot(s_grad, qs_ref[...])
    dq_t = dot(kt.T, s_grad)
    return dq_t, dk, dv


def own_kernel(heads, starts_ref, pos_ref, kv_ref, q_ref, o_ref, do_ref, lse_ref,
               dq_ref, dkv_ref, delta_ref, qs_ref, dos_ref):
    j = pl.program_id(0)

    @pl.when(j == 0)
    def _():
        dkv_ref[...] = jnp.zeros_like(dkv_ref)

    stack_heads(q_ref, qs_ref, heads)
    stack_heads(do_ref, dos_ref, heads)
    ones = jnp.ones((8, 2 * HEAD_DIM), jnp.bfloat16)
    for h in range(heads):
        cols = pl.ds(h * HEAD_DIM, HEAD_DIM)
        prod = do_ref[:, cols].astype(jnp.float32) * o_ref[:, cols].astype(jnp.float32)
        high = prod.astype(jnp.bfloat16)
        low = (prod - high.astype(jnp.float32)).astype(jnp.bfloat16)
        row = dot_nt(ones, jnp.concatenate([high, low], axis=1))
        delta_ref[h : h + 1, :] = row[0:1, :]
    dq_ref[...] = jnp.zeros_like(dq_ref)
    start_row = starts_ref[...]
    pos_row = pos_ref[...]
    base = pos_ref[0, 0] - j * BLOCK

    def step(t, carry):
        rows = pl.ds(pl.multiple_of(t * BLOCK, BLOCK), BLOCK)
        kt = kv_ref[rows, 0:HEAD_DIM]
        vt = kv_ref[rows, HEAD_DIM : 2 * HEAD_DIM]
        key_pos = base + t * BLOCK + lax.broadcasted_iota(jnp.int32, (BLOCK, BLOCK), 0)
        allowed = (key_pos >= start_row) & (key_pos <= pos_row)
        dq_t, dk, dv = tile_grads(kt, vt, qs_ref, dos_ref, lse_ref, delta_ref, allowed, heads)
        dq_ref[...] += dq_t
        dkv_ref[rows, 0:HEAD_DIM] += dk
        dkv_ref[rows, HEAD_DIM : 2 * HEAD_DIM] += dv
        return carry

    lax.fori_loop(0, j + 1, step, 0)


def rest_kernel(heads, tokens, info, starts_ref, kv3_ref, kv2_ref, kv1_ref, q_ref, do_ref, lse_ref, delta_ref,
                dqa_ref, dkva_ref, first_ref, last_ref, send_ref, keep_ref,
                qs_ref, dos_ref, dq_ref, kv_ref, dkv_ref):
    i = pl.program_id(0)
    window = BACK * tokens
    tiles = window // BLOCK

    @pl.when(i == 0)
    def _():
        for n, ref in enumerate((kv3_ref, kv2_ref, kv1_ref)):
            kv_ref[pl.ds(n * tokens, tokens), :] = ref[...]
        dkv_ref[...] = jnp.zeros_like(dkv_ref)

    base = info[0] * tokens - window
    first = jnp.clip(lax.div(info[5 + i] - base, BLOCK), 0, tiles)
    dq_ref[...] = dqa_ref[...]

    @pl.when(first < tiles)
    def _():
        stack_heads(q_ref, qs_ref, heads)
        stack_heads(do_ref, dos_ref, heads)
        start_row = starts_ref[...]

        def step(t, carry):
            rows = pl.ds(pl.multiple_of(t * BLOCK, BLOCK), BLOCK)
            kt = kv_ref[rows, 0:HEAD_DIM]
            vt = kv_ref[rows, HEAD_DIM : 2 * HEAD_DIM]
            key_pos = base + t * BLOCK + lax.broadcasted_iota(jnp.int32, (BLOCK, BLOCK), 0)
            allowed = key_pos >= start_row
            dq_t, dk, dv = tile_grads(kt, vt, qs_ref, dos_ref, lse_ref, delta_ref, allowed, heads)
            dq_ref[...] += dq_t
            dkv_ref[rows, 0:HEAD_DIM] += dk
            dkv_ref[rows, HEAD_DIM : 2 * HEAD_DIM] += dv
            return carry

        lax.fori_loop(first, tiles, step, 0)

    def put(ref, row):
        for h in range(heads):
            cols = pl.ds(h * HEAD_DIM, HEAD_DIM)
            ref[pl.ds(row, BLOCK), cols] = (dq_ref[:, cols].T * SCALE).astype(jnp.bfloat16)

    @pl.when(i < 2)
    def _():
        put(first_ref, pl.multiple_of(i * BLOCK, BLOCK))

    @pl.when(i == 2)
    def _():
        put(last_ref, 0)
        side = info[1]
        half = HEAD_DIM // 2
        left = lax.broadcasted_iota(jnp.int32, (tokens, HEAD_DIM), 1) < half
        for n in range(BACK + 1):
            rows = pl.ds(n * tokens, tokens)
            if n < BACK:
                dk, dv = dkv_ref[rows, 0:HEAD_DIM], dkv_ref[rows, HEAD_DIM : 2 * HEAD_DIM]
            else:
                dk, dv = dkva_ref[:, 0:HEAD_DIM], dkva_ref[:, HEAD_DIM : 2 * HEAD_DIM]
            dk = dk * SCALE
            low = jnp.where(left, dk, pltpu.roll(dv, half, 1))
            high = jnp.where(left, pltpu.roll(dk, half, 1), dv)
            keep_ref[rows, :] = jnp.where(side == 0, low, high)
            send_ref[rows, :] = jnp.where(side == 0, high, low).astype(jnp.bfloat16)


def place_kernel(info, mine12, mine3, theirs12, theirs3, out, sems):
    for s in range(3):
        source = info[8 + s]
        dst = out.at[pl.ds(s * BLOCK, BLOCK), :]

        def copy(src, s=s, dst=dst):
            return pltpu.make_async_copy(src, dst, sems.at[s])

        for number, array in enumerate((mine12, theirs12)):
            @pl.when((source == 3 * number) | (source == 3 * number + 1))
            def _(array=array, number=number, source=source, copy=copy):
                row = pl.multiple_of(jnp.clip(source - 3 * number, 0, 1) * BLOCK, BLOCK)
                copy(array.at[pl.ds(row, BLOCK), :]).start()
        for number, array in enumerate((mine3, theirs3)):
            @pl.when(source == 3 * number + 2)
            def _(array=array, copy=copy):
                copy(array).start()
    for s in range(3):
        pltpu.make_async_copy(mine3, out.at[pl.ds(s * BLOCK, BLOCK), :], sems.at[s]).wait()


def plan_info(block_plan, starts, seq_index, head_index, per_device, half_axis):
    partner = seq_index ^ half_axis
    mine = lax.dynamic_slice_in_dim(block_plan, seq_index * per_device, per_device)
    theirs = lax.dynamic_slice_in_dim(block_plan, partner * per_device, per_device)
    wanted = theirs // per_device == seq_index
    local = jnp.arange(per_device, dtype=jnp.int32)
    is_it = (theirs[None, :] == (seq_index * per_device + local)[:, None]) & wanted[None, :]
    sent = jnp.any(is_it, axis=1)
    slot = jnp.sum(jnp.where(is_it, local[None, :], 0), axis=1)
    rank_key = jnp.where(sent, slot, per_device + local)
    position = jnp.sum((rank_key[None, :] < rank_key[:, None]).astype(jnp.int32), axis=1)
    order = jnp.sum(jnp.where(position[None, :] == local[:, None], local[None, :], 0), axis=1)
    block_starts = starts.reshape(per_device, BLOCK)[:, 0]
    order_starts = jnp.sum(jnp.where(order[:, None] == local[None, :], block_starts[None, :], 0), axis=1)
    far = mine // per_device != seq_index
    far_rank = jnp.cumsum(far.astype(jnp.int32)) - 1
    near_pos = jnp.sum(jnp.where((mine % per_device)[:, None] == local[None, :], position[None, :], 0), axis=1)
    source = jnp.where(far, per_device + far_rank, near_pos)
    head = jnp.stack([seq_index, head_index % 2])
    return jnp.concatenate([head, order, order_starts, source]).astype(jnp.int32)


def on_device(queries, key_states, value_states, attn_out, grad_out, log_norm, lengths, block_plan):
    tokens = queries.shape[0]
    feature = queries.shape[1]
    heads = feature // HEAD_DIM
    per_device = tokens // BLOCK
    seq_index = lax.axis_index("seq")
    head_index = lax.axis_index("head")
    half_axis = lax.axis_size("seq") // 2
    kv_group = head_index // 2
    own_kv = jnp.concatenate([
        lax.dynamic_slice_in_dim(key_states, kv_group * HEAD_DIM, HEAD_DIM, 1),
        lax.dynamic_slice_in_dim(value_states, kv_group * HEAD_DIM, HEAD_DIM, 1)], axis=1)
    kv3, kv2, kv1 = (shifted(own_kv, "seq", n) for n in (3, 2, 1))

    doc_ends = jnp.cumsum(lengths)
    doc_begins = doc_ends - lengths
    pos = seq_index * tokens + jnp.arange(tokens, dtype=jnp.int32)
    starts = jnp.max(jnp.where(doc_begins[:, None] <= pos[None, :], doc_begins[:, None], 0), axis=0)
    info = plan_info(block_plan, starts, seq_index, head_index, per_device, half_axis)
    starts = starts.reshape(1, tokens)
    pos = pos.reshape(1, tokens)

    f32, bf16 = jnp.float32, jnp.bfloat16
    row_block = pl.BlockSpec((BLOCK, feature), lambda j: (j, 0))
    lane_row = pl.BlockSpec((1, BLOCK), lambda j: (0, j))
    own_dq, own_dkv, delta = pl.pallas_call(
        functools.partial(own_kernel, heads),
        grid=(per_device,),
        in_specs=[lane_row, lane_row,
                  pl.BlockSpec((tokens, 2 * HEAD_DIM), lambda j: (0, 0)),
                  row_block, row_block, row_block,
                  pl.BlockSpec((heads, BLOCK), lambda j: (0, j))],
        out_specs=[row_block,
                   pl.BlockSpec((tokens, 2 * HEAD_DIM), lambda j: (0, 0)),
                   pl.BlockSpec((heads, BLOCK), lambda j: (0, j))],
        out_shape=[jax.ShapeDtypeStruct((tokens, feature), f32),
                   jax.ShapeDtypeStruct((tokens, 2 * HEAD_DIM), f32),
                   jax.ShapeDtypeStruct((heads, tokens), f32)],
        scratch_shapes=[pltpu.VMEM((feature, HEAD_DIM), bf16), pltpu.VMEM((feature, HEAD_DIM), bf16)],
        compiler_params=pltpu.CompilerParams(vmem_limit_bytes=32 * 2**20),
        cost_estimate=pl.CostEstimate(flops=2_000_000_000, bytes_accessed=4_000_000, transcendentals=600_000),
        name="own_keys",
    )(starts, pos, own_kv, queries, attn_out, grad_out, log_norm)

    picked = lambda i, info: (info[2 + i], 0)
    picked_lane = lambda i, info: (0, info[2 + i])
    fixed = lambda i, info: (0, 0)
    picked_rows = pl.BlockSpec((BLOCK, feature), picked)
    kv_spec = pl.BlockSpec((tokens, 2 * HEAD_DIM), fixed)
    window = BACK * tokens
    dq12, dq3, send, keep = pl.pallas_call(
        functools.partial(rest_kernel, heads, tokens),
        grid_spec=pltpu.PrefetchScalarGridSpec(
            num_scalar_prefetch=1,
            grid=(per_device,),
            in_specs=[pl.BlockSpec((1, BLOCK), picked_lane), kv_spec, kv_spec, kv_spec,
                      picked_rows, picked_rows,
                      pl.BlockSpec((heads, BLOCK), picked_lane), pl.BlockSpec((heads, BLOCK), picked_lane),
                      picked_rows, kv_spec],
            out_specs=[pl.BlockSpec((2 * BLOCK, feature), fixed), pl.BlockSpec((BLOCK, feature), fixed),
                       pl.BlockSpec((window + tokens, HEAD_DIM), fixed),
                       pl.BlockSpec((window + tokens, HEAD_DIM), fixed)],
            scratch_shapes=[pltpu.VMEM((feature, HEAD_DIM), bf16), pltpu.VMEM((feature, HEAD_DIM), bf16),
                            pltpu.VMEM((BLOCK, feature), f32),
                            pltpu.VMEM((window, 2 * HEAD_DIM), bf16), pltpu.VMEM((window, 2 * HEAD_DIM), f32)]),
        out_shape=[jax.ShapeDtypeStruct((2 * BLOCK, feature), bf16),
                   jax.ShapeDtypeStruct((BLOCK, feature), bf16),
                   jax.ShapeDtypeStruct((window + tokens, HEAD_DIM), bf16),
                   jax.ShapeDtypeStruct((window + tokens, HEAD_DIM), f32)],
        compiler_params=pltpu.CompilerParams(vmem_limit_bytes=32 * 2**20),
        cost_estimate=pl.CostEstimate(flops=2_000_000_000, bytes_accessed=4_000_000, transcendentals=600_000),
        name="rest_keys",
    )(info, starts, kv3, kv2, kv1, queries, grad_out, log_norm, delta, own_dq, own_dkv)

    far12 = swapped(dq12, "seq", half_axis)
    far3 = swapped(dq3, "seq", half_axis)

    arrived = swapped(send, "head", 1)
    both = keep + arrived.astype(f32)
    total = both[window:]
    for n in (3, 2, 1):
        piece = both[(BACK - n) * tokens : (BACK - n + 1) * tokens].astype(bf16)
        total = total + shifted(piece, "seq", -n).astype(f32)
    total = total.astype(bf16)
    half = HEAD_DIM // 2

    anywhere = pl.BlockSpec(memory_space=pl.ANY)
    query_grad = pl.pallas_call(
        place_kernel,
        in_specs=[pl.BlockSpec(memory_space=pltpu.SMEM)] + [anywhere] * 4,
        out_specs=anywhere,
        out_shape=jax.ShapeDtypeStruct((tokens, feature), bf16),
        scratch_shapes=[pltpu.SemaphoreType.DMA((3,))],
        name="place_blocks",
    )(info, dq12, dq3, far12, far3)
    return query_grad, total[:, :half], total[:, half:]


def solution(mesh):
    placed = (
        P("seq", "head"),
        P("seq", None),
        P("seq", None),
        P("seq", "head"),
        P("seq", "head"),
        P("head", "seq"),
        P(),
        P(),
    )
    return jax.shard_map(
        on_device,
        mesh=mesh,
        in_specs=placed,
        out_specs=(P("seq", "head"), P("seq", "head"), P("seq", "head")),
        check_vma=False,
    )
```

time: 160 us -> 121 us (0.76)
  the two profiles are of different devices: /device:TPU:45 before, /device:TPU:160 now
where the time goes in v1:
time: 121 us; the launch traced here: 120 us
  waiting for transfers between devices  43.1 us (36%)
  starting transfers between devices  36 us (30%)
  Pallas kernels  28.2 us (23%)
  local copies, waits for them, and re-layouts  8.12 us (7%)
  other arithmetic  3.78 us (3%)
    ppermute x3, waiting for transfers between devices, swapped(): lax.ppermute(array, axis, [(i, i ^ apart) for i in range(lax.axis_size(ax...  43.1 us
    pallas_call x1, Pallas kernels, on_device(): pl.pallas_call(place_kernel, in_specs=[pl.BlockSpec(memory_space=pltpu.SM...  19.7 us
    ppermute x3, starting transfers between devices, swapped(): lax.ppermute(array, axis, [(i, i ^ apart) for i in range(lax.axis_size(ax...  18.1 us
    ppermute x6, starting transfers between devices, shifted(): lax.ppermute(value, axis, [(i, i + steps) for i in range(first, last)])  18 us
    unnamed x24, local copies, waits for them, and re-layouts  6.09 us
    pallas_call x1, Pallas kernels, on_device(): pl.pallas_call(functools.partial(rest_kernel, heads, tokens), grid_spec=p...  4.77 us
    pallas_call x1, Pallas kernels, on_device(): pl.pallas_call(functools.partial(own_kernel, heads), grid=(per_device,),...  3.78 us
  transfers between devices with their start and end apart: 9, of which 2 were waited for; matrix products, arithmetic and copies ran while one was open for 4% of the time, Pallas kernels for 19%

profile of v1, /device:TPU:160, one launch (start us, length us, event | category | flops | bytes accessed | tf_op | source)
XLA Modules:
  0.0 120.3 jit_solution(13924842644180734402)
XLA Ops:
  0.6 1.0 constant_dynamic-slice_fusion
  1.6 1.9 %collective-permute-start.2 = (bf16[384,256]{1,0:T(8,128)(2,1)S(1)}, bf16[384,256]{1,0:T(8,128)(2,1)S(1)}, u32[]{:S(2)}, u32[]{:S(2)}) collective-permute-start(bf16[384,256]{1,0:T(8,128)(2,1)S(1)} %pad_maximum_fusion.kv_ref), channel_id=1, source_target_pairs={{0,16},{16,32},{32,48},{48,64},{64,80},{80,96},{96,112},{112,128},... | collective-permute-start | bytes 589832 | tf_op jit(solution)/shard_map/ppermute | solution.py:20
  3.6 3.8 %collective-permute-start.1 = (bf16[384,256]{1,0:T(8,128)(2,1)S(1)}, bf16[384,256]{1,0:T(8,128)(2,1)S(1)}, u32[]{:S(2)}, u32[]{:S(2)}) collective-permute-start(bf16[384,256]{1,0:T(8,128)(2,1)S(1)} %pad_maximum_fusion.kv_ref), channel_id=1, source_target_pairs={{0,32},{16,48},{32,64},{48,80},{64,96},{80,112},{96,128},{112,144}... | collective-permute-start | bytes 589832 | tf_op jit(solution)/shard_map/ppermute | solution.py:20
  7.4 6.4 %collective-permute-start = (bf16[384,256]{1,0:T(8,128)(2,1)S(1)}, bf16[384,256]{1,0:T(8,128)(2,1)S(1)}, u32[]{:S(2)}, u32[]{:S(2)}) collective-permute-start(bf16[384,256]{1,0:T(8,128)(2,1)S(1)} %pad_maximum_fusion.kv_ref), channel_id=1, source_target_pairs={{0,48},{16,64},{32,80},{48,96},{64,112},{80,128},{96,144},{112,160... | collective-permute-start | bytes 589832 | tf_op jit(solution)/shard_map/ppermute | solution.py:20
  13.8 0.7 and_select_fusion
  14.6 0.8 fusion.4
  15.4 0.2 select_reduce_fusion.4
  15.6 0.2 fusion.3
  15.8 0.2 reduce-window.19
  15.9 0.2 convert_reduce_fusion
  16.1 0.8 copy.20
  17.1 0.7 sub.16
  17.9 0.2 select_reduce_fusion.1
  18.1 0.2 select_reduce_fusion.2
  18.4 1.1 copy-done.3
  19.5 1.1 copy-done.4
  20.6 1.1 copy-done.5
  21.6 0.7 copy-done.7
  22.3 3.8 %own_keys.1 = (f32[384,768]{1,0:T(8,128)S(1)}, f32[384,256]{1,0:T(8,128)S(1)}, f32[6,384]{1,0:T(8,128)S(1)}) custom-call(s32[1,384]{1,0:T(1,128)S(1)} %reshape.107.starts_ref, s32[1,384]{1,0:T(1,128)S(1)} %iota_add_fusion.1.pos_ref, bf16[384,256]{1,0:T(8,128)(2,1)S(1)} %pad_maximum_fusion.kv_ref, bf16[384,768]{1,0:T(8,128)(2,1)S(1)} %copy-done.4, ...), custom_call_target="tpu_custom_call" | custom-call | flops 2000000000 | bytes 4000000 | tf_op jit(solution)/shard_map/own_keys/pallas_call | solution.py:229
  26.2 4.8 %rest_keys.1 = (bf16[256,768]{1,0:T(8,128)(2,1)S(1)}, bf16[128,768]{1,0:T(8,128)(2,1)S(1)}, bf16[1536,128]{1,0:T(8,128)(2,1)S(1)}, f32[1536,128]{1,0:T(8,128)S(1)}) custom-call(s32[11]{0:T(128)S(1)} %concatenate.6.info, s32[1,384]{1,0:T(1,128)S(1)} %reshape.107.starts_ref, bf16[384,256]{1,0:T(8,128)(2,1)S(1)} %collective-permute-done.kv3_ref, ...), custom_call_target="tpu_custom_call" | custom-call | flops 2000000000 | bytes 4000000 | tf_op jit(solution)/shard_map/rest_keys/pallas_call | solution.py:254
  31.0 3.5 %collective-permute-start.5 = (bf16[1536,128]{1,0:T(8,128)(2,1)S(1)}, bf16[1536,128]{1,0:T(8,128)(2,1)S(1)}, u32[]{:S(2)}, u32[]{:S(2)}) collective-permute-start(bf16[1536,128]{1,0:T(8,128)(2,1)S(1)} %get-tuple-element.16), channel_id=1, source_target_pairs={{0,1},{1,0},{2,3},{3,2},{4,5},{5,4},{6,7},{7,6},{8,9},{9,8},{10,11... | collective-permute-start | bytes 1179656 | tf_op jit(solution)/shard_map/ppermute | solution.py:24
  34.5 4.0 %collective-permute-start.4 = (bf16[128,768]{1,0:T(8,128)(2,1)S(1)}, bf16[128,768]{1,0:T(8,128)(2,1)S(1)}, u32[]{:S(2)}, u32[]{:S(2)}) collective-permute-start(bf16[128,768]{1,0:T(8,128)(2,1)S(1)} %get-tuple-element.14.mine3), channel_id=1, source_target_pairs={{0,256},{16,272},{32,288},{48,304},{64,320},{80,336},{96,352},{112... | collective-permute-start | bytes 589832 | tf_op jit(solution)/shard_map/ppermute | solution.py:24
  38.5 10.6 %collective-permute-start.3 = (bf16[256,768]{1,0:T(8,128)(2,1)S(1)}, bf16[256,768]{1,0:T(8,128)(2,1)S(1)}, u32[]{:S(2)}, u32[]{:S(2)}) collective-permute-start(bf16[256,768]{1,0:T(8,128)(2,1)S(1)} %get-tuple-element.13.mine12), channel_id=1, source_target_pairs={{0,256},{16,272},{32,288},{48,304},{64,320},{80,336},{96,352},{112... | collective-permute-start | bytes 1179656 | tf_op jit(solution)/shard_map/ppermute | solution.py:24
  49.2 1.9 %collective-permute-start.6 = (bf16[384,128]{1,0:T(8,128)(2,1)S(1)}, bf16[384,128]{1,0:T(8,128)(2,1)S(1)}, u32[]{:S(2)}, u32[]{:S(2)}) collective-permute-start(bf16[384,128]{1,0:T(8,128)(2,1)S(1)} %get-tuple-element.37), channel_id=1, source_target_pairs={{48,0},{64,16},{80,32},{96,48},{112,64},{128,80},{144,96},{160,112... | collective-permute-start | bytes 294920 | tf_op jit(solution)/shard_map/ppermute | solution.py:20
  51.2 1.9 %collective-permute-start.8 = (bf16[384,128]{1,0:T(8,128)(2,1)S(1)}, bf16[384,128]{1,0:T(8,128)(2,1)S(1)}, u32[]{:S(2)}, u32[]{:S(2)}) collective-permute-start(bf16[384,128]{1,0:T(8,128)(2,1)S(1)} %get-tuple-element.38), channel_id=1, source_target_pairs={{16,0},{32,16},{48,32},{64,48},{80,64},{96,80},{112,96},{128,112},... | collective-permute-start | bytes 294920 | tf_op jit(solution)/shard_map/ppermute | solution.py:20
  53.1 2.0 %collective-permute-start.7 = (bf16[384,128]{1,0:T(8,128)(2,1)S(1)}, bf16[384,128]{1,0:T(8,128)(2,1)S(1)}, u32[]{:S(2)}, u32[]{:S(2)}) collective-permute-start(bf16[384,128]{1,0:T(8,128)(2,1)S(1)} %get-tuple-element.39), channel_id=1, source_target_pairs={{32,0},{48,16},{64,32},{80,48},{96,64},{112,80},{128,96},{144,112}... | collective-permute-start | bytes 294920 | tf_op jit(solution)/shard_map/ppermute | solution.py:20
  55.1 29.0 %collective-permute-done.4.theirs3 = bf16[128,768]{1,0:T(8,128)(2,1)S(1)} collective-permute-done((bf16[128,768]{1,0:T(8,128)(2,1)S(1)}, bf16[128,768]{1,0:T(8,128)(2,1)S(1)}, u32[]{:S(2)}, u32[]{:S(2)}) %collective-permute-start.4) | collective-permute-done | bytes 196640 | tf_op jit(solution)/shard_map/ppermute | solution.py:24
  84.1 14.1 %collective-permute-done.3.theirs12 = bf16[256,768]{1,0:T(8,128)(2,1)S(1)} collective-permute-done((bf16[256,768]{1,0:T(8,128)(2,1)S(1)}, bf16[256,768]{1,0:T(8,128)(2,1)S(1)}, u32[]{:S(2)}, u32[]{:S(2)}) %collective-permute-start.3) | collective-permute-done | bytes 393248 | tf_op jit(solution)/shard_map/ppermute | solution.py:24
  98.2 0.7 copy-done.9
  99.0 19.7 %place_blocks.1 = bf16[384,768]{1,0:T(8,128)(2,1)} custom-call(s32[11]{0:T(128)} %copy-done.2, bf16[256,768]{1,0:T(8,128)(2,1)} %copy-done, bf16[128,768]{1,0:T(8,128)(2,1)} %copy-done.1, bf16[256,768]{1,0:T(8,128)(2,1)} %copy-done.9, bf16[128,768]{1,0:T(8,128)(2,1)} %copy-done.10), custom_call_target="tpu_custom_call" | custom-call | tf_op jit(solution)/shard_map/place_blocks/pallas_call | solution.py:291
  118.8 0.7 copy.22
  119.6 0.7 copy.21
  (40 shorter events, 0.8 us)
Async XLA Ops:
  1.6 24.5 %collective-permute-start.2 = (bf16[384,256]{1,0:T(8,128)(2,1)S(1)}, bf16[384,256]{1,0:T(8,128)(2,1)S(1)}, u32[]{:S(2)}, u32[]{:S(2)}) collective-permute-start(bf16[384,256]{1,0:T(8,128)(2,1)S(1)} %pad_maximum_fusion.kv_ref), channel_id=1, source_target_pairs={{0,16},{16,32},{32,48},{48,64},{64,80},{80,96},{96,112},{112,128},... | collective-permute-start | bytes 589832 | tf_op jit(solution)/shard_map/ppermute | solution.py:20
  3.6 22.6 %collective-permute-start.1 = (bf16[384,256]{1,0:T(8,128)(2,1)S(1)}, bf16[384,256]{1,0:T(8,128)(2,1)S(1)}, u32[]{:S(2)}, u32[]{:S(2)}) collective-permute-start(bf16[384,256]{1,0:T(8,128)(2,1)S(1)} %pad_maximum_fusion.kv_ref), channel_id=1, source_target_pairs={{0,32},{16,48},{32,64},{48,80},{64,96},{80,112},{96,128},{112,144}... | collective-permute-start | bytes 589832 | tf_op jit(solution)/shard_map/ppermute | solution.py:20
  7.4 18.7 %collective-permute-start = (bf16[384,256]{1,0:T(8,128)(2,1)S(1)}, bf16[384,256]{1,0:T(8,128)(2,1)S(1)}, u32[]{:S(2)}, u32[]{:S(2)}) collective-permute-start(bf16[384,256]{1,0:T(8,128)(2,1)S(1)} %pad_maximum_fusion.kv_ref), channel_id=1, source_target_pairs={{0,48},{16,64},{32,80},{48,96},{64,112},{80,128},{96,144},{112,160... | collective-permute-start | bytes 589832 | tf_op jit(solution)/shard_map/ppermute | solution.py:20
  18.4 1.1 copy-start.3
  19.5 1.1 copy-start.4
  20.6 1.1 copy-start.5
  21.6 0.7 copy-start.7
  22.3 3.8 %copy-start.2 = (s32[11]{0:T(128)}, s32[11]{0:T(128)S(1)}, u32[]{:S(2)}) copy-start(s32[11]{0:T(128)S(1)} %concatenate.6.info) | copy-start | bytes 136
  22.3 3.8 %copy-start.6 = (bf16[384,768]{1,0:T(8,128)(2,1)S(1)}, bf16[384,768]{1,0:T(8,128)(2,1)}, u32[]{:S(2)}) copy-start(bf16[384,768]{1,0:T(8,128)(2,1)} %do_ref.3) | copy-start | bytes 1769476
  22.3 3.8 %copy-start.8 = (bf16[6,384]{1,0:T(8,128)(2,1)S(1)}, bf16[6,384]{1,0:T(8,128)(2,1)}, u32[]{:S(2)}) copy-start(bf16[6,384]{1,0:T(8,128)(2,1)} %lse_ref.3) | copy-start | bytes 13828
  31.0 18.2 %copy-start = (bf16[256,768]{1,0:T(8,128)(2,1)}, bf16[256,768]{1,0:T(8,128)(2,1)S(1)}, u32[]{:S(2)}) copy-start(bf16[256,768]{1,0:T(8,128)(2,1)S(1)} %get-tuple-element.13.mine12) | copy-start | bytes 1179652
  31.0 18.2 %copy-start.1 = (bf16[128,768]{1,0:T(8,128)(2,1)}, bf16[128,768]{1,0:T(8,128)(2,1)S(1)}, u32[]{:S(2)}) copy-start(bf16[128,768]{1,0:T(8,128)(2,1)S(1)} %get-tuple-element.14.mine3) | copy-start | bytes 589828
  31.0 18.1 %collective-permute-start.5 = (bf16[1536,128]{1,0:T(8,128)(2,1)S(1)}, bf16[1536,128]{1,0:T(8,128)(2,1)S(1)}, u32[]{:S(2)}, u32[]{:S(2)}) collective-permute-start(bf16[1536,128]{1,0:T(8,128)(2,1)S(1)} %get-tuple-element.16), channel_id=1, source_target_pairs={{0,1},{1,0},{2,3},{3,2},{4,5},{5,4},{6,7},{7,6},{8,9},{9,8},{10,11... | collective-permute-start | bytes 1179656 | tf_op jit(solution)/shard_map/ppermute | solution.py:24
  34.5 49.6 %collective-permute-start.4 = (bf16[128,768]{1,0:T(8,128)(2,1)S(1)}, bf16[128,768]{1,0:T(8,128)(2,1)S(1)}, u32[]{:S(2)}, u32[]{:S(2)}) collective-permute-start(bf16[128,768]{1,0:T(8,128)(2,1)S(1)} %get-tuple-element.14.mine3), channel_id=1, source_target_pairs={{0,256},{16,272},{32,288},{48,304},{64,320},{80,336},{96,352},{112... | collective-permute-start | bytes 589832 | tf_op jit(solution)/shard_map/ppermute | solution.py:24
  38.5 59.7 %collective-permute-start.3 = (bf16[256,768]{1,0:T(8,128)(2,1)S(1)}, bf16[256,768]{1,0:T(8,128)(2,1)S(1)}, u32[]{:S(2)}, u32[]{:S(2)}) collective-permute-start(bf16[256,768]{1,0:T(8,128)(2,1)S(1)} %get-tuple-element.13.mine12), channel_id=1, source_target_pairs={{0,256},{16,272},{32,288},{48,304},{64,320},{80,336},{96,352},{112... | collective-permute-start | bytes 1179656 | tf_op jit(solution)/shard_map/ppermute | solution.py:24
  49.2 69.4 %collective-permute-start.6 = (bf16[384,128]{1,0:T(8,128)(2,1)S(1)}, bf16[384,128]{1,0:T(8,128)(2,1)S(1)}, u32[]{:S(2)}, u32[]{:S(2)}) collective-permute-start(bf16[384,128]{1,0:T(8,128)(2,1)S(1)} %get-tuple-element.37), channel_id=1, source_target_pairs={{48,0},{64,16},{80,32},{96,48},{112,64},{128,80},{144,96},{160,112... | collective-permute-start | bytes 294920 | tf_op jit(solution)/shard_map/ppermute | solution.py:20
  51.2 67.5 %collective-permute-start.8 = (bf16[384,128]{1,0:T(8,128)(2,1)S(1)}, bf16[384,128]{1,0:T(8,128)(2,1)S(1)}, u32[]{:S(2)}, u32[]{:S(2)}) collective-permute-start(bf16[384,128]{1,0:T(8,128)(2,1)S(1)} %get-tuple-element.38), channel_id=1, source_target_pairs={{16,0},{32,16},{48,32},{64,48},{80,64},{96,80},{112,96},{128,112},... | collective-permute-start | bytes 294920 | tf_op jit(solution)/shard_map/ppermute | solution.py:20
  53.1 65.6 %collective-permute-start.7 = (bf16[384,128]{1,0:T(8,128)(2,1)S(1)}, bf16[384,128]{1,0:T(8,128)(2,1)S(1)}, u32[]{:S(2)}, u32[]{:S(2)}) collective-permute-start(bf16[384,128]{1,0:T(8,128)(2,1)S(1)} %get-tuple-element.39), channel_id=1, source_target_pairs={{32,0},{48,16},{64,32},{80,48},{96,64},{112,80},{128,96},{144,112}... | collective-permute-start | bytes 294920 | tf_op jit(solution)/shard_map/ppermute | solution.py:20
  84.1 14.1 %copy-start.10 = (bf16[128,768]{1,0:T(8,128)(2,1)}, bf16[128,768]{1,0:T(8,128)(2,1)S(1)}, u32[]{:S(2)}) copy-start(bf16[128,768]{1,0:T(8,128)(2,1)S(1)} %collective-permute-done.4.theirs3) | copy-start | bytes 589828
  98.2 0.7 copy-start.9

commit v2 on v1

--- a/solution.py
+++ b/solution.py
@@ -10,6 +10,7 @@
 HEAD_DIM = 128
 BLOCK = 128
 BACK = 3
+VMEM_LIMIT = 56 * 2**20
 LOG2E = 1.4426950408889634
 SCALE = HEAD_DIM ** -0.5
 
@@ -55,13 +56,49 @@
     return dq_t, dk, dv
 
 
-def own_kernel(heads, starts_ref, pos_ref, kv_ref, q_ref, o_ref, do_ref, lse_ref,
-               dq_ref, dkv_ref, delta_ref, qs_ref, dos_ref):
+def plan_info(info_ref, lengths_ref, plan_ref, device, partner, side, per_device):
+    first = device * per_device
+    locals_ = range(per_device)
+    theirs = [plan_ref[partner * per_device + s] for s in locals_]
+    mine = [plan_ref[first + s] for s in locals_]
+    ranks = []
+    for l in locals_:
+        rank = per_device + l
+        for s in locals_:
+            rank = jnp.where(theirs[s] == first + l, s, rank)
+        ranks.append(rank)
+    position = [sum((ranks[m] < ranks[l]).astype(jnp.int32) for m in locals_ if m != l) for l in locals_]
+    starts = [jnp.int32(0)] * per_device
+    begin = jnp.int32(0)
+    for n in range(lengths_ref.shape[0]):
+        starts = [jnp.where(begin <= (first + l) * BLOCK, begin, starts[l]) for l in locals_]
+        begin = begin + lengths_ref[n]
+    info_ref[0] = device
+    info_ref[1] = side
+    for i in locals_:
+        info_ref[2 + i] = sum(jnp.where(position[l] == i, l, 0) for l in locals_)
+        info_ref[5 + i] = sum(jnp.where(position[l] == i, starts[l], 0) for l in locals_)
+    far_rank = jnp.int32(0)
+    for s in locals_:
+        local = mine[s] - first
+        near = (local >= 0) & (local < per_device)
+        near_position = sum(jnp.where(local == l, position[l], 0) for l in locals_)
+        info_ref[8 + s] = jnp.where(near, near_position, per_device + far_rank)
+        far_rank = far_rank + jnp.where(near, 0, 1)
+
+
+def own_kernel(heads, half_axis, lengths_ref, plan_ref, kv_ref, q_ref, o_ref, do_ref, lse_ref,
+               dq_ref, dkv_ref, delta_ref, starts_ref, info_ref, qs_ref, dos_ref):
     j = pl.program_id(0)
+    per_device = pl.num_programs(0)
+    device = lax.axis_index("seq")
+    base = device * kv_ref.shape[0]
 
     @pl.when(j == 0)
     def _():
         dkv_ref[...] = jnp.zeros_like(dkv_ref)
+        plan_info(info_ref, lengths_ref, plan_ref, device, device ^ half_axis,
+                  lax.axis_index("head") & 1, kv_ref.shape[0] // BLOCK)
 
     stack_heads(q_ref, qs_ref, heads)
     stack_heads(do_ref, dos_ref, heads)
@@ -74,9 +111,13 @@
         row = dot_nt(ones, jnp.concatenate([high, low], axis=1))
         delta_ref[h : h + 1, :] = row[0:1, :]
     dq_ref[...] = jnp.zeros_like(dq_ref)
-    start_row = starts_ref[...]
-    pos_row = pos_ref[...]
-    base = pos_ref[0, 0] - j * BLOCK
+    pos_row = base + j * BLOCK + lax.broadcasted_iota(jnp.int32, (1, BLOCK), 1)
+    start_row = jnp.zeros((1, BLOCK), jnp.int32)
+    begin = jnp.int32(0)
+    for n in range(lengths_ref.shape[0]):
+        start_row = jnp.where(pos_row >= begin, begin, start_row)
+        begin = begin + lengths_ref[n]
+    starts_ref[...] = start_row
 
     def step(t, carry):
         rows = pl.ds(pl.multiple_of(t * BLOCK, BLOCK), BLOCK)
@@ -158,10 +199,11 @@
             send_ref[rows, :] = jnp.where(side == 0, high, low).astype(jnp.bfloat16)
 
 
-def place_kernel(info, mine12, mine3, theirs12, theirs3, out, sems):
+def finish_kernel(info, mine12, mine3, theirs12, theirs3, own_ref, r1_ref, r2_ref, r3_ref,
+                  out_ref, key_ref, value_ref, sems):
     for s in range(3):
         source = info[8 + s]
-        dst = out.at[pl.ds(s * BLOCK, BLOCK), :]
+        dst = out_ref.at[pl.ds(s * BLOCK, BLOCK), :]
 
         def copy(src, s=s, dst=dst):
             return pltpu.make_async_copy(src, dst, sems.at[s])
@@ -175,30 +217,24 @@
             @pl.when(source == 3 * number + 2)
             def _(array=array, copy=copy):
                 copy(array).start()
+    total = own_ref[...]
+    for ref in (r1_ref, r2_ref, r3_ref):
+        total = total + ref[...].astype(jnp.float32)
+    half = HEAD_DIM // 2
+    key_ref[...] = total[:, :half].astype(jnp.bfloat16)
+    value_ref[...] = total[:, half:].astype(jnp.bfloat16)
     for s in range(3):
-        pltpu.make_async_copy(mine3, out.at[pl.ds(s * BLOCK, BLOCK), :], sems.at[s]).wait()
-
-
-def plan_info(block_plan, starts, seq_index, head_index, per_device, half_axis):
-    partner = seq_index ^ half_axis
-    mine = lax.dynamic_slice_in_dim(block_plan, seq_index * per_device, per_device)
-    theirs = lax.dynamic_slice_in_dim(block_plan, partner * per_device, per_device)
-    wanted = theirs // per_device == seq_index
-    local = jnp.arange(per_device, dtype=jnp.int32)
-    is_it = (theirs[None, :] == (seq_index * per_device + local)[:, None]) & wanted[None, :]
-    sent = jnp.any(is_it, axis=1)
-    slot = jnp.sum(jnp.where(is_it, local[None, :], 0), axis=1)
-    rank_key = jnp.where(sent, slot, per_device + local)
-    position = jnp.sum((rank_key[None, :] < rank_key[:, None]).astype(jnp.int32), axis=1)
-    order = jnp.sum(jnp.where(position[None, :] == local[:, None], local[None, :], 0), axis=1)
-    block_starts = starts.reshape(per_device, BLOCK)[:, 0]
-    order_starts = jnp.sum(jnp.where(order[:, None] == local[None, :], block_starts[None, :], 0), axis=1)
-    far = mine // per_device != seq_index
-    far_rank = jnp.cumsum(far.astype(jnp.int32)) - 1
-    near_pos = jnp.sum(jnp.where((mine % per_device)[:, None] == local[None, :], position[None, :], 0), axis=1)
-    source = jnp.where(far, per_device + far_rank, near_pos)
-    head = jnp.stack([seq_index, head_index % 2])
-    return jnp.concatenate([head, order, order_starts, source]).astype(jnp.int32)
+        pltpu.make_async_copy(mine3, out_ref.at[pl.ds(s * BLOCK, BLOCK), :], sems.at[s]).wait()
+
+
+GROUPS = 4
+
+
+def third_needed(block_plan, per_device, half_axis):
+    holder = block_plan.reshape(-1, per_device)[:half_axis] // per_device
+    here = jnp.arange(half_axis, dtype=jnp.int32)
+    full = jnp.all(holder != here[:, None], axis=1)
+    return sum(jnp.max(jnp.where(full & (here % GROUPS == g), 1 << g, 0)) for g in range(GROUPS))
 
 
 def on_device(queries, key_states, value_states, attn_out, grad_out, log_norm, lengths, block_plan):
@@ -206,51 +242,46 @@
     feature = queries.shape[1]
     heads = feature // HEAD_DIM
     per_device = tokens // BLOCK
-    seq_index = lax.axis_index("seq")
-    head_index = lax.axis_index("head")
     half_axis = lax.axis_size("seq") // 2
-    kv_group = head_index // 2
+    window = BACK * tokens
+    kv_group = lax.axis_index("head") // 2
     own_kv = jnp.concatenate([
         lax.dynamic_slice_in_dim(key_states, kv_group * HEAD_DIM, HEAD_DIM, 1),
         lax.dynamic_slice_in_dim(value_states, kv_group * HEAD_DIM, HEAD_DIM, 1)], axis=1)
     kv3, kv2, kv1 = (shifted(own_kv, "seq", n) for n in (3, 2, 1))
-
-    doc_ends = jnp.cumsum(lengths)
-    doc_begins = doc_ends - lengths
-    pos = seq_index * tokens + jnp.arange(tokens, dtype=jnp.int32)
-    starts = jnp.max(jnp.where(doc_begins[:, None] <= pos[None, :], doc_begins[:, None], 0), axis=0)
-    info = plan_info(block_plan, starts, seq_index, head_index, per_device, half_axis)
-    starts = starts.reshape(1, tokens)
-    pos = pos.reshape(1, tokens)
+    branch = third_needed(block_plan, per_device, half_axis)
 
     f32, bf16 = jnp.float32, jnp.bfloat16
+    smem = pl.BlockSpec(memory_space=pltpu.SMEM)
     row_block = pl.BlockSpec((BLOCK, feature), lambda j: (j, 0))
-    lane_row = pl.BlockSpec((1, BLOCK), lambda j: (0, j))
-    own_dq, own_dkv, delta = pl.pallas_call(
-        functools.partial(own_kernel, heads),
+    own_dq, own_dkv, delta, starts, info = pl.pallas_call(
+        functools.partial(own_kernel, heads, half_axis),
         grid=(per_device,),
-        in_specs=[lane_row, lane_row,
+        in_specs=[smem, smem,
                   pl.BlockSpec((tokens, 2 * HEAD_DIM), lambda j: (0, 0)),
                   row_block, row_block, row_block,
                   pl.BlockSpec((heads, BLOCK), lambda j: (0, j))],
         out_specs=[row_block,
                    pl.BlockSpec((tokens, 2 * HEAD_DIM), lambda j: (0, 0)),
-                   pl.BlockSpec((heads, BLOCK), lambda j: (0, j))],
+                   pl.BlockSpec((heads, BLOCK), lambda j: (0, j)),
+                   pl.BlockSpec((1, BLOCK), lambda j: (0, j)),
+                   smem],
         out_shape=[jax.ShapeDtypeStruct((tokens, feature), f32),
                    jax.ShapeDtypeStruct((tokens, 2 * HEAD_DIM), f32),
-                   jax.ShapeDtypeStruct((heads, tokens), f32)],
+                   jax.ShapeDtypeStruct((heads, tokens), f32),
+                   jax.ShapeDtypeStruct((1, tokens), jnp.int32),
+                   jax.ShapeDtypeStruct((16,), jnp.int32)],
         scratch_shapes=[pltpu.VMEM((feature, HEAD_DIM), bf16), pltpu.VMEM((feature, HEAD_DIM), bf16)],
-        compiler_params=pltpu.CompilerParams(vmem_limit_bytes=32 * 2**20),
+        compiler_params=pltpu.CompilerParams(vmem_limit_bytes=VMEM_LIMIT),
         cost_estimate=pl.CostEstimate(flops=2_000_000_000, bytes_accessed=4_000_000, transcendentals=600_000),
         name="own_keys",
-    )(starts, pos, own_kv, queries, attn_out, grad_out, log_norm)
+    )(lengths, block_plan, own_kv, queries, attn_out, grad_out, log_norm)
 
     picked = lambda i, info: (info[2 + i], 0)
     picked_lane = lambda i, info: (0, info[2 + i])
     fixed = lambda i, info: (0, 0)
     picked_rows = pl.BlockSpec((BLOCK, feature), picked)
     kv_spec = pl.BlockSpec((tokens, 2 * HEAD_DIM), fixed)
-    window = BACK * tokens
     dq12, dq3, send, keep = pl.pallas_call(
         functools.partial(rest_kernel, heads, tokens),
         grid_spec=pltpu.PrefetchScalarGridSpec(
@@ -270,33 +301,35 @@
                    jax.ShapeDtypeStruct((BLOCK, feature), bf16),
                    jax.ShapeDtypeStruct((window + tokens, HEAD_DIM), bf16),
                    jax.ShapeDtypeStruct((window + tokens, HEAD_DIM), f32)],
-        compiler_params=pltpu.CompilerParams(vmem_limit_bytes=32 * 2**20),
+        compiler_params=pltpu.CompilerParams(vmem_limit_bytes=VMEM_LIMIT),
         cost_estimate=pl.CostEstimate(flops=2_000_000_000, bytes_accessed=4_000_000, transcendentals=600_000),
         name="rest_keys",
     )(info, starts, kv3, kv2, kv1, queries, grad_out, log_norm, delta, own_dq, own_dkv)
 
     far12 = swapped(dq12, "seq", half_axis)
-    far3 = swapped(dq3, "seq", half_axis)
-
-    arrived = swapped(send, "head", 1)
-    both = keep + arrived.astype(f32)
-    total = both[window:]
-    for n in (3, 2, 1):
-        piece = both[(BACK - n) * tokens : (BACK - n + 1) * tokens].astype(bf16)
-        total = total + shifted(piece, "seq", -n).astype(f32)
-    total = total.astype(bf16)
-    half = HEAD_DIM // 2
+
+    def returns(mask, dq3, send, keep):
+        pairs = [(i, i ^ half_axis) for i in range(2 * half_axis) if mask >> (i % half_axis % GROUPS) & 1]
+        far3 = lax.ppermute(dq3, "seq", pairs) if pairs else dq3
+        both = keep + swapped(send, "head", 1).astype(f32)
+        pieces = [both[(BACK - n) * tokens : (BACK - n + 1) * tokens].astype(bf16) for n in (3, 2, 1)]
+        back = [shifted(piece, "seq", -n) for piece, n in zip(pieces, (3, 2, 1))]
+        return (far3, both[window:], *back)
+
+    branches = [functools.partial(returns, mask) for mask in range(1 << GROUPS)]
+    far3, own, back3, back2, back1 = lax.switch(branch, branches, dq3, send, keep)
 
     anywhere = pl.BlockSpec(memory_space=pl.ANY)
-    query_grad = pl.pallas_call(
-        place_kernel,
-        in_specs=[pl.BlockSpec(memory_space=pltpu.SMEM)] + [anywhere] * 4,
-        out_specs=anywhere,
-        out_shape=jax.ShapeDtypeStruct((tokens, feature), bf16),
+    vmem = pl.BlockSpec(memory_space=pltpu.VMEM)
+    grad_half = jax.ShapeDtypeStruct((tokens, HEAD_DIM // 2), bf16)
+    return pl.pallas_call(
+        finish_kernel,
+        in_specs=[smem] + [anywhere] * 4 + [vmem] * 4,
+        out_specs=[vmem] * 3,
+        out_shape=[jax.ShapeDtypeStruct((tokens, feature), bf16), grad_half, grad_half],
         scratch_shapes=[pltpu.SemaphoreType.DMA((3,))],
         name="place_blocks",
-    )(info, dq12, dq3, far12, far3)
-    return query_grad, total[:, :half], total[:, half:]
+    )(info, dq12, dq3, far12, far3, own, back1, back2, back3)
 
 
 def solution(mesh):

time: 121 us -> 90.7 us (0.75)
  the two profiles are of different devices: /device:TPU:160 before, /device:TPU:1 now
where the time goes in v2:
time: 90.7 us; the launch traced here: 90.2 us
  starting transfers between devices  38.6 us (43%)
  waiting for transfers between devices  22.7 us (25%)
  Pallas kernels  17.1 us (19%)
  local copies, waits for them, and re-layouts  6.59 us (7%)
  between operations  3.38 us (4%)
  other arithmetic  1.68 us (2%)
    ppermute x6, starting transfers between devices, shifted(): lax.ppermute(value, axis, [(i, i + steps) for i in range(first, last)])  22.8 us
    ppermute x6, waiting for transfers between devices, shifted(): lax.ppermute(value, axis, [(i, i + steps) for i in range(first, last)])  17.1 us
    ppermute x2, starting transfers between devices, swapped(): lax.ppermute(array, axis, [(i, i ^ apart) for i in range(lax.axis_size(ax...  15.8 us
    pallas_call x1, Pallas kernels, on_device(): pl.pallas_call(functools.partial(rest_kernel, heads, tokens), grid_spec=p...  7.56 us
    pallas_call x1, Pallas kernels, on_device(): pl.pallas_call(functools.partial(own_kernel, heads, half_axis), grid=(per...  6.37 us
    ppermute x2, waiting for transfers between devices, swapped(): lax.ppermute(array, axis, [(i, i ^ apart) for i in range(lax.axis_size(ax...  5.6 us
    pallas_call x2, local copies, waits for them, and re-layouts, on_device(): pl.pallas_call(finish_kernel, in_specs=[smem] + [anywhere] * 4 + [vmem] *...  3.2 us
    pallas_call x1, Pallas kernels, on_device(): pl.pallas_call(finish_kernel, in_specs=[smem] + [anywhere] * 4 + [vmem] *...  3.18 us
  transfers between devices with their start and end apart: 8, of which 4 were waited for; matrix products, arithmetic and copies ran while one was open for 3% of the time, Pallas kernels for 7%

profile of v2, /device:TPU:1, one launch (start us, length us, event | category | flops | bytes accessed | tf_op | source)
XLA Modules:
  0.0 90.2 jit_solution(15770112704809392722)
XLA Ops:
  0.6 1.0 %constant_dynamic-slice_fusion = (bf16[384,128]{1,0:T(8,128)(2,1)S(1)}, bf16[384,128]{1,0:T(8,128)(2,1)S(1)}) fusion(bf16[384,1024]{1,0:T(8,128)(2,1)} %param.26, s32[]{:T(128)S(6)} %select_n.46, bf16[384,1024]{1,0:T(8,128)(2,1)} %param.25), kind=kLoop, calls=%fused_computation.26 | loop fusion | bytes 393220 | tf_op jit(solution)/shard_map/dynamic_slice | solution.py:250
  1.7 6.3 %collective-permute-start.79 = (bf16[384,256]{1,0:T(8,128)(2,1)S(1)}, bf16[384,256]{1,0:T(8,128)(2,1)S(1)}, u32[]{:S(2)}, u32[]{:S(2)}) collective-permute-start(bf16[384,256]{1,0:T(8,128)(2,1)S(1)} %pad_maximum_fusion.kv_ref), channel_id=1, source_target_pairs={{0,48},{16,64},{32,80},{48,96},{64,112},{80,128},{96,144},{112,160... | collective-permute-start | bytes 589832 | tf_op jit(solution)/shard_map/ppermute | solution.py:21
  8.0 3.5 %collective-permute-start.80 = (bf16[384,256]{1,0:T(8,128)(2,1)S(1)}, bf16[384,256]{1,0:T(8,128)(2,1)S(1)}, u32[]{:S(2)}, u32[]{:S(2)}) collective-permute-start(bf16[384,256]{1,0:T(8,128)(2,1)S(1)} %pad_maximum_fusion.kv_ref), channel_id=1, source_target_pairs={{0,32},{16,48},{32,64},{48,80},{64,96},{80,112},{96,128},{112,144}... | collective-permute-start | bytes 589832 | tf_op jit(solution)/shard_map/ppermute | solution.py:21
  11.5 2.2 %collective-permute-start.81 = (bf16[384,256]{1,0:T(8,128)(2,1)S(1)}, bf16[384,256]{1,0:T(8,128)(2,1)S(1)}, u32[]{:S(2)}, u32[]{:S(2)}) collective-permute-start(bf16[384,256]{1,0:T(8,128)(2,1)S(1)} %pad_maximum_fusion.kv_ref), channel_id=1, source_target_pairs={{0,16},{16,32},{32,48},{48,64},{64,80},{80,96},{96,112},{112,128},... | collective-permute-start | bytes 589832 | tf_op jit(solution)/shard_map/ppermute | solution.py:21
  13.7 0.7 slice_divide_fusion
  14.4 0.1 div.21
  14.5 6.4 %own_keys.1 = (f32[384,768]{1,0:T(8,128)}, f32[384,256]{1,0:T(8,128)}, f32[6,384]{1,0:T(8,128)}, s32[1,384]{1,0:T(1,128)}, s32[16]{0:T(128)}) custom-call(s32[30]{0:T(128)} %lengths_ref.1, s32[96]{0:T(128)} %plan_ref.1, bf16[384,256]{1,0:T(8,128)(2,1)} %copy-done.1, bf16[384,768]{1,0:T(8,128)(2,1)} %q_ref.3, bf16[384,768]{1,0:T(8,128)(2,1)} %o_ref.1, ...), custom_call_target="tpu_custom_call" | custom-call | flops 2000000000 | bytes 4000000 | tf_op jit(solution)/shard_map/own_keys/pallas_call | solution.py:257
  20.8 0.0 collective-permute-done.79.kv3_ref
  20.9 0.0 collective-permute-done.80.kv2_ref
  20.9 0.6 copy-done.2
  21.5 0.1 copy-done.3
  21.6 0.0 copy-done.4
  21.7 7.6 %rest_keys.1 = (bf16[256,768]{1,0:T(8,128)(2,1)}, bf16[128,768]{1,0:T(8,128)(2,1)S(1)}, bf16[1536,128]{1,0:T(8,128)(2,1)S(1)}, f32[1536,128]{1,0:T(8,128)S(1)}) custom-call(s32[16]{0:T(128)} %get-tuple-element.161.info, s32[1,384]{1,0:T(1,128)} %get-tuple-element.162.starts_ref, bf16[384,256]{1,0:T(8,128)(2,1)} %copy-done.2, bf16[384,256]{1,0:T(8,128)(2,1)} %copy-done.3, ...), custom_call_target="tpu_custom_call" | custom-call | flops 2000000000 | bytes 4000000 | tf_op jit(solution)/shard_map/rest_keys/pallas_call | solution.py:285
  29.2 12.6 %collective-permute-start.82 = (bf16[256,768]{1,0:T(8,128)(2,1)}, bf16[256,768]{1,0:T(8,128)(2,1)S(1)}, u32[]{:S(2)}, u32[]{:S(2)}) collective-permute-start(bf16[256,768]{1,0:T(8,128)(2,1)} %get-tuple-element.166.mine12), channel_id=1, source_target_pairs={{0,256},{16,272},{32,288},{48,304},{64,320},{80,336},{96,352},{112... | collective-permute-start | bytes 1179656 | tf_op jit(solution)/shard_map/ppermute | solution.py:25
  41.8 0.1 and.41
  41.9 0.1 fusion.1
  42.0 0.8 fusion.5
  45.4 37.6 %conditional.1 = (bf16[128,768]{1,0:T(8,128)(2,1)}, f32[384,128]{1,0:T(8,128)S(1)}, bf16[384,128]{1,0:T(8,128)(2,1)}, bf16[384,128]{1,0:T(8,128)(2,1)}, bf16[384,128]{1,0:T(8,128)(2,1)}) conditional(s32[]{:T(128)} %clamp.3, (bf16[1536,128]{1,0:T(8,128)(2,1)S(1)}, f32[1536,128]{1,0:T(8,128)S(1)}, ...), branch_computations={%region_5.6_spmd, %region_6.7_spmd, %region_7.8_spmd, %region_8.9_... | conditional | flops 589824 | bytes 6881520 | solution.py:320
  45.4 3.2 %collective-permute-start = (bf16[1536,128]{1,0:T(8,128)(2,1)S(1)}, bf16[1536,128]{1,0:T(8,128)(2,1)S(1)}, u32[]{:S(2)}, u32[]{:S(2)}) collective-permute-start(bf16[1536,128]{1,0:T(8,128)(2,1)S(1)} %get-tuple-element.98), channel_id=1, source_target_pairs={{0,1},{1,0},{2,3},{3,2},{4,5},{5,4},{6,7},{7,6},{8,9},{9,8},{10,11... | collective-permute-start | bytes 1179656 | tf_op jit(solution)/shard_map/cond/branch_0_fun/ppermute | solution.py:25
  48.6 5.6 %collective-permute-done = bf16[1536,128]{1,0:T(8,128)(2,1)S(1)} collective-permute-done((bf16[1536,128]{1,0:T(8,128)(2,1)S(1)}, bf16[1536,128]{1,0:T(8,128)(2,1)S(1)}, u32[]{:S(2)}, u32[]{:S(2)}) %collective-permute-start) | collective-permute-done | bytes 393248 | tf_op jit(solution)/shard_map/cond/branch_0_fun/ppermute | solution.py:25
  54.2 0.1 fusion.6
  54.4 1.3 %collective-permute-start.1 = (bf16[384,128]{1,0:T(8,128)(2,1)S(1)}, bf16[384,128]{1,0:T(8,128)(2,1)}, u32[]{:S(2)}, u32[]{:S(2)}) collective-permute-start(bf16[384,128]{1,0:T(8,128)(2,1)S(1)} %get-tuple-element.219), channel_id=1, source_target_pairs={{48,0},{64,16},{80,32},{96,48},{112,64},{128,80},{144,96},{160,112... | collective-permute-start | bytes 294920 | tf_op jit(solution)/shard_map/cond/branch_0_fun/ppermute | solution.py:21
  55.7 1.3 %collective-permute-start.2 = (bf16[384,128]{1,0:T(8,128)(2,1)S(1)}, bf16[384,128]{1,0:T(8,128)(2,1)}, u32[]{:S(2)}, u32[]{:S(2)}) collective-permute-start(bf16[384,128]{1,0:T(8,128)(2,1)S(1)} %get-tuple-element.218), channel_id=1, source_target_pairs={{32,0},{48,16},{64,32},{80,48},{96,64},{112,80},{128,96},{144,112}... | collective-permute-start | bytes 294920 | tf_op jit(solution)/shard_map/cond/branch_0_fun/ppermute | solution.py:21
  57.0 8.2 %collective-permute-start.3 = (bf16[384,128]{1,0:T(8,128)(2,1)S(1)}, bf16[384,128]{1,0:T(8,128)(2,1)}, u32[]{:S(2)}, u32[]{:S(2)}) collective-permute-start(bf16[384,128]{1,0:T(8,128)(2,1)S(1)} %get-tuple-element.217), channel_id=1, source_target_pairs={{16,0},{32,16},{48,32},{64,48},{80,64},{96,80},{112,96},{128,112},... | collective-permute-start | bytes 294920 | tf_op jit(solution)/shard_map/cond/branch_0_fun/ppermute | solution.py:21
  65.2 0.7 copy.15
  65.9 14.7 %collective-permute-done.1 = bf16[384,128]{1,0:T(8,128)(2,1)} collective-permute-done((bf16[384,128]{1,0:T(8,128)(2,1)S(1)}, bf16[384,128]{1,0:T(8,128)(2,1)}, u32[]{:S(2)}, u32[]{:S(2)}) %collective-permute-start.1) | collective-permute-done | bytes 98336 | tf_op jit(solution)/shard_map/cond/branch_0_fun/ppermute | solution.py:21
  80.5 1.9 %collective-permute-done.2 = bf16[384,128]{1,0:T(8,128)(2,1)} collective-permute-done((bf16[384,128]{1,0:T(8,128)(2,1)S(1)}, bf16[384,128]{1,0:T(8,128)(2,1)}, u32[]{:S(2)}, u32[]{:S(2)}) %collective-permute-start.2) | collective-permute-done | bytes 98336 | tf_op jit(solution)/shard_map/cond/branch_0_fun/ppermute | solution.py:21
  82.4 0.6 collective-permute-done.3
  83.0 0.8 copy-done
  83.8 3.2 %place_blocks.1 = (bf16[384,768]{1,0:T(8,128)(2,1)}, bf16[384,64]{1,0:T(8,128)(2,1)}, bf16[384,64]{1,0:T(8,128)(2,1)}) custom-call(s32[16]{0:T(128)} %get-tuple-element.161.info, bf16[256,768]{1,0:T(8,128)(2,1)} %get-tuple-element.166.mine12, bf16[128,768]{1,0:T(8,128)(2,1)S(1)} %get-tuple-element.167.mine3, bf16[256,768]{1,0:T(8,128)(2,1)} %copy-done, ...), custom_call_target="tpu_custom_call" | custom-call | tf_op jit(solution)/shard_map/place_blocks/pallas_call | solution.py:325
  87.0 1.6 %copy.13 = bf16[384,64]{0,1:T(8,128)(2,1)} copy(bf16[384,64]{1,0:T(8,128)(2,1)} %get-tuple-element.179) | data formatting | bytes 98304 | tf_op jit(solution)/shard_map/place_blocks/pallas_call | solution.py:325
  88.6 1.6 %copy.14 = bf16[384,64]{0,1:T(8,128)(2,1)} copy(bf16[384,64]{1,0:T(8,128)(2,1)} %get-tuple-element.180) | data formatting | bytes 98304 | tf_op jit(solution)/shard_map/place_blocks/pallas_call | solution.py:325
  (14 shorter events, 0.1 us)
Async XLA Ops:
  1.6 12.8 %copy-start.1 = (bf16[384,256]{1,0:T(8,128)(2,1)}, bf16[384,256]{1,0:T(8,128)(2,1)S(1)}, u32[]{:S(2)}) copy-start(bf16[384,256]{1,0:T(8,128)(2,1)S(1)} %pad_maximum_fusion.kv_ref) | copy-start | bytes 589828
  1.7 19.2 %collective-permute-start.79 = (bf16[384,256]{1,0:T(8,128)(2,1)S(1)}, bf16[384,256]{1,0:T(8,128)(2,1)S(1)}, u32[]{:S(2)}, u32[]{:S(2)}) collective-permute-start(bf16[384,256]{1,0:T(8,128)(2,1)S(1)} %pad_maximum_fusion.kv_ref), channel_id=1, source_target_pairs={{0,48},{16,64},{32,80},{48,96},{64,112},{80,128},{96,144},{112,160... | collective-permute-start | bytes 589832 | tf_op jit(solution)/shard_map/ppermute | solution.py:21
  8.0 12.9 %collective-permute-start.80 = (bf16[384,256]{1,0:T(8,128)(2,1)S(1)}, bf16[384,256]{1,0:T(8,128)(2,1)S(1)}, u32[]{:S(2)}, u32[]{:S(2)}) collective-permute-start(bf16[384,256]{1,0:T(8,128)(2,1)S(1)} %pad_maximum_fusion.kv_ref), channel_id=1, source_target_pairs={{0,32},{16,48},{32,64},{48,80},{64,96},{80,112},{96,128},{112,144}... | collective-permute-start | bytes 589832 | tf_op jit(solution)/shard_map/ppermute | solution.py:21
  11.5 9.4 %collective-permute-start.81 = (bf16[384,256]{1,0:T(8,128)(2,1)S(1)}, bf16[384,256]{1,0:T(8,128)(2,1)S(1)}, u32[]{:S(2)}, u32[]{:S(2)}) collective-permute-start(bf16[384,256]{1,0:T(8,128)(2,1)S(1)} %pad_maximum_fusion.kv_ref), channel_id=1, source_target_pairs={{0,16},{16,32},{32,48},{48,64},{64,80},{80,96},{96,112},{112,128},... | collective-permute-start | bytes 589832 | tf_op jit(solution)/shard_map/ppermute | solution.py:21
  20.8 0.7 copy-start.2
  20.9 0.8 copy-start.3
  20.9 0.8 copy-start.4
  21.7 20.1 %copy-start.5 = (s32[96]{0:T(128)S(1)}, s32[96]{0:T(128)}, u32[]{:S(2)}) copy-start(s32[96]{0:T(128)} %plan_ref.1) | copy-start | bytes 1156
  29.2 53.8 %collective-permute-start.82 = (bf16[256,768]{1,0:T(8,128)(2,1)}, bf16[256,768]{1,0:T(8,128)(2,1)S(1)}, u32[]{:S(2)}, u32[]{:S(2)}) collective-permute-start(bf16[256,768]{1,0:T(8,128)(2,1)} %get-tuple-element.166.mine12), channel_id=1, source_target_pairs={{0,256},{16,272},{32,288},{48,304},{64,320},{80,336},{96,352},{112... | collective-permute-start | bytes 1179656 | tf_op jit(solution)/shard_map/ppermute | solution.py:25
  45.4 8.8 %collective-permute-start = (bf16[1536,128]{1,0:T(8,128)(2,1)S(1)}, bf16[1536,128]{1,0:T(8,128)(2,1)S(1)}, u32[]{:S(2)}, u32[]{:S(2)}) collective-permute-start(bf16[1536,128]{1,0:T(8,128)(2,1)S(1)} %get-tuple-element.98), channel_id=1, source_target_pairs={{0,1},{1,0},{2,3},{3,2},{4,5},{5,4},{6,7},{7,6},{8,9},{9,8},{10,11... | collective-permute-start | bytes 1179656 | tf_op jit(solution)/shard_map/cond/branch_0_fun/ppermute | solution.py:25
  54.4 26.2 %collective-permute-start.1 = (bf16[384,128]{1,0:T(8,128)(2,1)S(1)}, bf16[384,128]{1,0:T(8,128)(2,1)}, u32[]{:S(2)}, u32[]{:S(2)}) collective-permute-start(bf16[384,128]{1,0:T(8,128)(2,1)S(1)} %get-tuple-element.219), channel_id=1, source_target_pairs={{48,0},{64,16},{80,32},{96,48},{112,64},{128,80},{144,96},{160,112... | collective-permute-start | bytes 294920 | tf_op jit(solution)/shard_map/cond/branch_0_fun/ppermute | solution.py:21
  55.7 26.7 %collective-permute-start.2 = (bf16[384,128]{1,0:T(8,128)(2,1)S(1)}, bf16[384,128]{1,0:T(8,128)(2,1)}, u32[]{:S(2)}, u32[]{:S(2)}) collective-permute-start(bf16[384,128]{1,0:T(8,128)(2,1)S(1)} %get-tuple-element.218), channel_id=1, source_target_pairs={{32,0},{48,16},{64,32},{80,48},{96,64},{112,80},{128,96},{144,112}... | collective-permute-start | bytes 294920 | tf_op jit(solution)/shard_map/cond/branch_0_fun/ppermute | solution.py:21
  57.0 26.0 %collective-permute-start.3 = (bf16[384,128]{1,0:T(8,128)(2,1)S(1)}, bf16[384,128]{1,0:T(8,128)(2,1)}, u32[]{:S(2)}, u32[]{:S(2)}) collective-permute-start(bf16[384,128]{1,0:T(8,128)(2,1)S(1)} %get-tuple-element.217), channel_id=1, source_target_pairs={{16,0},{32,16},{48,32},{64,48},{80,64},{96,80},{112,96},{128,112},... | collective-permute-start | bytes 294920 | tf_op jit(solution)/shard_map/cond/branch_0_fun/ppermute | solution.py:21
  83.0 0.8 copy-start

commit v3 on v2

v3 whole, which is shorter than its diff:
```python
import functools

import jax
import jax.numpy as jnp
from jax import lax
from jax.experimental import pallas as pl
from jax.experimental.pallas import tpu as pltpu
from jax.sharding import PartitionSpec as P

HEAD_DIM = 128
BLOCK = 128
BACK = 3
VMEM_LIMIT = 20 * 2**20
GROUPS = 4
LOG2E = 1.4426950408889634
SCALE = HEAD_DIM ** -0.5


def shifted(value, axis, steps):
    count = lax.axis_size(axis)
    first, last = (max(0, -steps), min(count, count - steps))
    return lax.ppermute(value, axis, [(i, i + steps) for i in range(first, last)])


def swapped(array, axis, apart):
    return lax.ppermute(array, axis, [(i, i ^ apart) for i in range(lax.axis_size(axis))])


def dot(a, b):
    return jnp.dot(a, b, preferred_element_type=jnp.float32)


def dot_nt(a, b):
    return lax.dot_general(a, b, (((1,), (1,)), ((), ())), preferred_element_type=jnp.float32)


def tile_grads(kt, vt, qs, dos, rows, allowed, heads):
    scores = dot_nt(kt, qs)
    prob_grad = dot_nt(vt, dos)
    weights, score_grads = [], []
    for h in range(heads):
        cols = slice(h * BLOCK, (h + 1) * BLOCK)
        lse = rows[h : h + 1, :]
        delta = rows[heads + h : heads + h + 1, :]
        w = jnp.where(allowed, jnp.exp2(scores[:, cols] * (SCALE * LOG2E) - lse), 0.0)
        weights.append(w.astype(jnp.bfloat16))
        score_grads.append((w * (prob_grad[:, cols] - delta)).astype(jnp.bfloat16))
    w_half = jnp.concatenate(weights, axis=1)
    s_grad = jnp.concatenate(score_grads, axis=1)
    dv = dot(w_half, dos)
    dk = dot(s_grad, qs)
    dq_t = dot(kt.T, s_grad)
    return dq_t, dk, dv


def plan_info(info_ref, branch_ref, lengths_ref, plan_ref, device, half_axis, side, per_device):
    first = device * per_device
    partner = device ^ half_axis
    locals_ = range(per_device)
    theirs = [plan_ref[partner * per_device + s] for s in locals_]
    mine = [plan_ref[first + s] for s in locals_]
    ranks = []
    for l in locals_:
        rank = per_device + l
        for s in locals_:
            rank = jnp.where(theirs[s] == first + l, s, rank)
        ranks.append(rank)
    position = [sum((ranks[m] < ranks[l]).astype(jnp.int32) for m in locals_ if m != l) for l in locals_]
    starts = [jnp.int32(0)] * per_device
    begin = jnp.int32(0)
    for n in range(lengths_ref.shape[0]):
        starts = [jnp.where(begin <= (first + l) * BLOCK, begin, starts[l]) for l in locals_]
        begin = begin + lengths_ref[n]
    info_ref[0] = device
    info_ref[1] = side
    for i in locals_:
        info_ref[2 + i] = sum(jnp.where(position[l] == i, l, 0) for l in locals_)
        info_ref[5 + i] = sum(jnp.where(position[l] == i, starts[l], 0) for l in locals_)
    far_rank = jnp.int32(0)
    for s in locals_:
        local = mine[s] - first
        near = (local >= 0) & (local < per_device)
        near_position = sum(jnp.where(local == l, position[l], 0) for l in locals_)
        info_ref[8 + s] = jnp.where(near, near_position, per_device + far_rank)
        far_rank = far_rank + jnp.where(near, 0, 1)
    mask = jnp.int32(0)
    for pair in range(half_axis):
        full = jnp.bool_(True)
        for s in locals_:
            local = plan_ref[pair * per_device + s] - pair * per_device
            full = full & ((local < 0) | (local >= per_device))
        mask = mask | jnp.where(full, 1 << (pair % GROUPS), 0)
    branch_ref[0] = mask


def own_kernel(heads, half_axis, lengths_ref, plan_ref, kv_ref, q_hbm, o_hbm, do_hbm, lse_ref,
               dq_ref, dkv_ref, rows_ref, starts_ref, qs_ref, dos_ref, info_ref, branch_ref,
               q_buf, o_buf, do_buf, sems):
    tokens = kv_ref.shape[0]
    blocks = tokens // BLOCK
    feature = heads * HEAD_DIM

    def copies(j):
        rows = pl.ds(j * BLOCK, BLOCK)
        pairs = ((do_hbm, do_buf), (o_hbm, o_buf), (q_hbm, q_buf))
        return [pltpu.make_async_copy(a.at[rows, :], b.at[rows, :], sems.at[j, n]) for n, (a, b) in enumerate(pairs)]

    for j in range(blocks):
        for c in copies(j):
            c.start()
    device = lax.axis_index("seq")
    base = device * tokens
    dkv_ref[...] = jnp.zeros_like(dkv_ref)
    plan_info(info_ref, branch_ref, lengths_ref, plan_ref, device, half_axis, lax.axis_index("head") & 1, blocks)

    pos = base + lax.broadcasted_iota(jnp.int32, (1, tokens), 1)
    start = jnp.zeros((1, tokens), jnp.int32)
    begin = jnp.int32(0)
    for n in range(lengths_ref.shape[0]):
        start = jnp.where(pos >= begin, begin, start)
        begin = begin + lengths_ref[n]

    ones = jnp.ones((8, 2 * HEAD_DIM), jnp.bfloat16)
    for j in range(blocks):
        rows = pl.ds(j * BLOCK, BLOCK)
        lanes = slice(j * BLOCK, (j + 1) * BLOCK)
        for c in copies(j):
            c.wait()
        for h in range(heads):
            cols = pl.ds(h * HEAD_DIM, HEAD_DIM)
            stacked = pl.ds(j * feature + h * HEAD_DIM, HEAD_DIM)
            qs_ref[stacked, :] = q_buf[rows, cols]
            dos_ref[stacked, :] = do_buf[rows, cols]
            prod = do_buf[rows, cols].astype(jnp.float32) * o_buf[rows, cols].astype(jnp.float32)
            high = prod.astype(jnp.bfloat16)
            low = (prod - high.astype(jnp.float32)).astype(jnp.bfloat16)
            row = dot_nt(ones, jnp.concatenate([high, low], axis=1))
            rows_ref[j, heads + h : heads + h + 1, :] = row[0:1, :]
        rows_ref[j, 0:heads, :] = lse_ref[:, lanes].astype(jnp.float32) * LOG2E
        start_row, pos_row = start[:, lanes], pos[:, lanes]
        starts_ref[j] = jnp.broadcast_to(start_row, (8, BLOCK))
        dq_ref[rows, :] = jnp.zeros((BLOCK, feature), jnp.float32)

        def step(t, carry, j=j, rows=rows, start_row=start_row, pos_row=pos_row):
            keys = pl.ds(pl.multiple_of(t * BLOCK, BLOCK), BLOCK)
            queries = pl.ds(j * feature, feature)
            key_pos = base + t * BLOCK + lax.broadcasted_iota(jnp.int32, (BLOCK, BLOCK), 0)
            allowed = (key_pos >= start_row) & (key_pos <= pos_row)
            dq_t, dk, dv = tile_grads(kv_ref[keys, 0:HEAD_DIM], kv_ref[keys, HEAD_DIM : 2 * HEAD_DIM],
                                      qs_ref[queries, :], dos_ref[queries, :], rows_ref.at[j], allowed, heads)
            dq_ref[rows, :] += dq_t
            dkv_ref[keys, 0:HEAD_DIM] += dk
            dkv_ref[keys, HEAD_DIM : 2 * HEAD_DIM] += dv
            return carry

        lax.fori_loop(0, j + 1, step, 0)


def rest_kernel(heads, info, starts_ref, kv3_ref, kv2_ref, kv1_ref, qs_ref, dos_ref, rows_ref, dqa_ref, dkva_ref,
                first_ref, last_ref, send_ref, far_ref, own_ref, dq_ref, kv_ref, dkv_ref):
    tokens = dkva_ref.shape[0]
    blocks = tokens // BLOCK
    feature = heads * HEAD_DIM
    window = BACK * tokens
    tiles = window // BLOCK
    for n, ref in enumerate((kv3_ref, kv2_ref, kv1_ref)):
        kv_ref[pl.ds(n * tokens, tokens), :] = ref[...]
    dkv_ref[...] = jnp.zeros_like(dkv_ref)
    base = info[0] * tokens - window
    for i in range(blocks):
        block = jnp.clip(info[2 + i], 0, blocks - 1)
        first = jnp.clip(lax.div(info[5 + i] - base, BLOCK), 0, tiles)
        queries = pl.ds(pl.multiple_of(block * feature, feature), feature)
        dq_ref[...] = dqa_ref[pl.ds(pl.multiple_of(block * BLOCK, BLOCK), BLOCK), :]
        start_row = starts_ref[block, 0:1, :]

        def step(t, carry, block=block, queries=queries, start_row=start_row):
            keys = pl.ds(pl.multiple_of(t * BLOCK, BLOCK), BLOCK)
            key_pos = base + t * BLOCK + lax.broadcasted_iota(jnp.int32, (BLOCK, BLOCK), 0)
            dq_t, dk, dv = tile_grads(kv_ref[keys, 0:HEAD_DIM], kv_ref[keys, HEAD_DIM : 2 * HEAD_DIM],
                                      qs_ref[queries, :], dos_ref[queries, :], rows_ref.at[block],
                                      key_pos >= start_row, heads)
            dq_ref[...] += dq_t
            dkv_ref[keys, 0:HEAD_DIM] += dk
            dkv_ref[keys, HEAD_DIM : 2 * HEAD_DIM] += dv
            return carry

        lax.fori_loop(first, tiles, step, 0)
        out, row = (first_ref, i * BLOCK) if i < 2 else (last_ref, 0)
        for h in range(heads):
            cols = pl.ds(h * HEAD_DIM, HEAD_DIM)
            out[pl.ds(row, BLOCK), cols] = (dq_ref[:, cols].T * SCALE).astype(jnp.bfloat16)

    side = info[1]
    half = HEAD_DIM // 2
    left = lax.broadcasted_iota(jnp.int32, (tokens, HEAD_DIM), 1) < half
    for n in range(BACK + 1):
        rows = pl.ds(n * tokens, tokens)
        if n < BACK:
            dk, dv = dkv_ref[rows, 0:HEAD_DIM], dkv_ref[rows, HEAD_DIM : 2 * HEAD_DIM]
        else:
            dk, dv = dkva_ref[:, 0:HEAD_DIM], dkva_ref[:, HEAD_DIM : 2 * HEAD_DIM]
        dk = dk * SCALE
        low = jnp.where(left, dk, pltpu.roll(dv, half, 1))
        high = jnp.where(left, pltpu.roll(dk, half, 1), dv)
        send_ref[rows, :] = jnp.where(side == 0, high, low).astype(jnp.bfloat16)
        kept = jnp.where(side == 0, low, high)
        if n < BACK:
            far_ref[rows, :] = kept.astype(jnp.bfloat16)
        else:
            own_ref[...] = kept


def finish_kernel(info, mine12, mine3, theirs12, theirs3, own_ref, r1_ref, r2_ref, r3_ref,
                  out_ref, key_ref, value_ref, sems):
    for s in range(3):
        source = info[8 + s]
        dst = out_ref.at[pl.ds(s * BLOCK, BLOCK), :]

        def copy(src, s=s, dst=dst):
            return pltpu.make_async_copy(src, dst, sems.at[s])

        for number, array in enumerate((mine12, theirs12)):
            @pl.when((source == 3 * number) | (source == 3 * number + 1))
            def _(array=array, number=number, source=source, copy=copy):
                row = pl.multiple_of(jnp.clip(source - 3 * number, 0, 1) * BLOCK, BLOCK)
                copy(array.at[pl.ds(row, BLOCK), :]).start()
        for number, array in enumerate((mine3, theirs3)):
            @pl.when(source == 3 * number + 2)
            def _(array=array, copy=copy):
                copy(array).start()
    total = own_ref[...]
    for ref in (r1_ref, r2_ref, r3_ref):
        total = total + ref[...].astype(jnp.float32)
    half = HEAD_DIM // 2
    for n in range(total.shape[0] // BLOCK):
        lanes = slice(n * BLOCK, (n + 1) * BLOCK)
        turned = total[lanes, :].T.astype(jnp.bfloat16)
        key_ref[:, lanes] = turned[:half]
        value_ref[:, lanes] = turned[half:]
    for s in range(3):
        pltpu.make_async_copy(mine3, out_ref.at[pl.ds(s * BLOCK, BLOCK), :], sems.at[s]).wait()


def on_device(queries, key_states, value_states, attn_out, grad_out, log_norm, lengths, block_plan):
    tokens, feature = queries.shape
    heads = feature // HEAD_DIM
    blocks = tokens // BLOCK
    half_axis = lax.axis_size("seq") // 2
    window = BACK * tokens
    kv_group = lax.axis_index("head") // 2
    own_kv = jnp.concatenate([
        lax.dynamic_slice_in_dim(key_states, kv_group * HEAD_DIM, HEAD_DIM, 1),
        lax.dynamic_slice_in_dim(value_states, kv_group * HEAD_DIM, HEAD_DIM, 1)], axis=1)
    kv3, kv2, kv1 = (shifted(own_kv, "seq", n) for n in (3, 2, 1))

    f32, bf16, i32 = jnp.float32, jnp.bfloat16, jnp.int32
    queries, attn_out, grad_out, log_norm, lengths, block_plan = (
        pltpu.with_memory_space_constraint(a, pltpu.HBM)
        for a in (queries, attn_out, grad_out, log_norm, lengths, block_plan))
    smem = pl.BlockSpec(memory_space=pltpu.SMEM)
    vmem = pl.BlockSpec(memory_space=pltpu.VMEM)
    hbm = pl.BlockSpec(memory_space=pltpu.HBM)
    params = pltpu.CompilerParams(vmem_limit_bytes=VMEM_LIMIT)
    own_dq, own_dkv, rows, starts, qs, dos, info, branch = pl.pallas_call(
        functools.partial(own_kernel, heads, half_axis),
        in_specs=[smem, smem, vmem, hbm, hbm, hbm, vmem],
        out_specs=[vmem] * 6 + [smem] * 2,
        out_shape=[pltpu.VMEM((tokens, feature), f32),
                   pltpu.VMEM((tokens, 2 * HEAD_DIM), f32),
                   pltpu.VMEM((blocks, 16, BLOCK), f32),
                   pltpu.VMEM((blocks, 8, BLOCK), i32),
                   pltpu.VMEM((blocks * feature, HEAD_DIM), bf16),
                   pltpu.VMEM((blocks * feature, HEAD_DIM), bf16),
                   jax.ShapeDtypeStruct((16,), i32),
                   jax.ShapeDtypeStruct((1,), i32)],
        scratch_shapes=[pltpu.VMEM((tokens, feature), bf16)] * 3 + [pltpu.SemaphoreType.DMA((blocks, 3))],
        compiler_params=params,
        cost_estimate=pl.CostEstimate(flops=2_000_000_000, bytes_accessed=4_000_000, transcendentals=600_000),
        name="own_keys",
    )(lengths, block_plan, own_kv, queries, attn_out, grad_out, log_norm)

    dq12, dq3, send, far, own = pl.pallas_call(
        functools.partial(rest_kernel, heads),
        in_specs=[smem] + [vmem] * 9,
        out_specs=[vmem] * 5,
        out_shape=[pltpu.VMEM((2 * BLOCK, feature), bf16),
                   pltpu.VMEM((BLOCK, feature), bf16),
                   pltpu.VMEM((window + tokens, HEAD_DIM), bf16),
                   pltpu.VMEM((window, HEAD_DIM), bf16),
                   pltpu.VMEM((tokens, HEAD_DIM), f32)],
        scratch_shapes=[pltpu.VMEM((BLOCK, feature), f32),
                        pltpu.VMEM((window, 2 * HEAD_DIM), bf16), pltpu.VMEM((window, 2 * HEAD_DIM), f32)],
        compiler_params=params,
        cost_estimate=pl.CostEstimate(flops=2_000_000_000, bytes_accessed=4_000_000, transcendentals=600_000),
        name="rest_keys",
    )(info, starts, kv3, kv2, kv1, qs, dos, rows, own_dq, own_dkv)

    theirs12 = swapped(dq12, "seq", half_axis)

    def returns(mask, dq3, send, far, own):
        pairs = [(i, i ^ half_axis) for i in range(2 * half_axis) if mask >> (i % half_axis % GROUPS) & 1]
        theirs3 = lax.ppermute(dq3, "seq", pairs) if pairs else dq3
        arrived = swapped(send, "head", 1).astype(f32)
        both = (far.astype(f32) + arrived[:window]).astype(bf16)
        back = [shifted(both[(BACK - n) * tokens : (BACK - n + 1) * tokens], "seq", -n) for n in (3, 2, 1)]
        return (theirs3, own + arrived[window:], *back)

    branches = [functools.partial(returns, mask) for mask in range(1 << GROUPS)]
    theirs3, own, back3, back2, back1 = lax.switch(branch.reshape(()), branches, dq3, send, far, own)

    grad_half = jax.ShapeDtypeStruct((HEAD_DIM // 2, tokens), bf16)
    query_grad, key_grad, value_grad = pl.pallas_call(
        finish_kernel,
        in_specs=[smem] + [vmem] * 8,
        out_specs=[hbm, vmem, vmem],
        out_shape=[jax.ShapeDtypeStruct((tokens, feature), bf16), grad_half, grad_half],
        scratch_shapes=[pltpu.SemaphoreType.DMA((3,))],
        compiler_params=params,
        name="place_blocks",
    )(info, dq12, dq3, theirs12, theirs3, own, back1, back2, back3)
    return query_grad, key_grad.T, value_grad.T


def solution(mesh):
    placed = (
        P("seq", "head"),
        P("seq", None),
        P("seq", None),
        P("seq", "head"),
        P("seq", "head"),
        P("head", "seq"),
        P(),
        P(),
    )
    return jax.shard_map(
        on_device,
        mesh=mesh,
        in_specs=placed,
        out_specs=(P("seq", "head"), P("seq", "head"), P("seq", "head")),
        check_vma=False,
    )
```

time: 90.7 us -> 81.7 us (0.901)
  waiting for transfers between devices: 22.7 us -> 29.1 us
  local copies, waits for them, and re-layouts: 6.59 us -> 1.66 us
  Pallas kernels: 17.1 us -> 12.9 us
  starting transfers between devices: 38.6 us -> 36 us
  between operations: 3.38 us -> 1.38 us
  other arithmetic: 1.68 us -> 0.18 us
    ppermute x6, starting transfers between devices: 22.8 us -> 17.5 us  [shifted(): lax.ppermute(value, axis, [(i, i + steps) for i in range(first, last)])]
    pallas_call x3, Pallas kernels: 17.1 us -> 12.9 us  [the longest x1 5.91 us: on_device(): pl.pallas_call(functools.partial(own_kernel, heads, half_axis), in_specs=...]
    ppermute x6, waiting for transfers between devices: 17.1 us -> 20.6 us  [shifted(): lax.ppermute(value, axis, [(i, i + steps) for i in range(first, last)])]
    pallas_call x2 -> x0, local copies, waits for them, and re-layouts: 3.2 us -> none  [on_device(): pl.pallas_call(finish_kernel, in_specs=[smem] + [anywhere] * 4 + [vmem] *...]
    ppermute x2, waiting for transfers between devices: 5.6 us -> 8.55 us  [swapped(): lax.ppermute(array, axis, [(i, i ^ apart) for i in range(lax.axis_size(ax...]
    ppermute x2, starting transfers between devices: 15.8 us -> 18.5 us  [swapped(): lax.ppermute(array, axis, [(i, i ^ apart) for i in range(lax.axis_size(ax...]
    unnamed x12 -> x0, local copies, waits for them, and re-layouts: 1.54 us -> none
  transfers between devices with their start and end apart: 8 -> 8, of which waited for: 4 -> 3; matrix products, arithmetic and copies ran while one was open for 3% -> 1% of each run, Pallas kernels for 7% -> 7%
where the time goes in v3:
time: 81.7 us; the launch traced here: 81.3 us
  starting transfers between devices  36 us (44%)
  waiting for transfers between devices  29.1 us (36%)
  Pallas kernels  12.9 us (16%)
  local copies, waits for them, and re-layouts  1.66 us (2%)
  between operations  1.38 us (2%)
    ppermute x6, waiting for transfers between devices, shifted(): lax.ppermute(value, axis, [(i, i + steps) for i in range(first, last)])  20.6 us
    ppermute x2, starting transfers between devices, swapped(): lax.ppermute(array, axis, [(i, i ^ apart) for i in range(lax.axis_size(ax...  18.5 us
    ppermute x6, starting transfers between devices, shifted(): lax.ppermute(value, axis, [(i, i + steps) for i in range(first, last)])  17.5 us
    ppermute x2, waiting for transfers between devices, swapped(): lax.ppermute(array, axis, [(i, i ^ apart) for i in range(lax.axis_size(ax...  8.55 us
    pallas_call x1, Pallas kernels, on_device(): pl.pallas_call(functools.partial(own_kernel, heads, half_axis), in_specs=...  5.91 us
    pallas_call x1, Pallas kernels, on_device(): pl.pallas_call(functools.partial(rest_kernel, heads), in_specs=[smem] + [...  4.37 us
    pallas_call x1, Pallas kernels, on_device(): pl.pallas_call(finish_kernel, in_specs=[smem] + [vmem] * 8, out_specs=[hb...  2.6 us
  transfers between devices with their start and end apart: 8, of which 3 were waited for; matrix products, arithmetic and copies ran while one was open for 1% of the time, Pallas kernels for 7%

profile of v3, /device:TPU:1, one launch (start us, length us, event | category | flops | bytes accessed | tf_op | source)
XLA Modules:
  0.0 81.3 jit_solution(16032607174636618063)
XLA Ops:
  0.6 1.0 %constant_dynamic-slice_fusion = (bf16[384,128]{1,0:T(8,128)(2,1)S(1)}, bf16[384,128]{1,0:T(8,128)(2,1)S(1)}) fusion(bf16[384,1024]{1,0:T(8,128)(2,1)} %param.26, s32[]{:T(128)S(6)} %select_n.10, bf16[384,1024]{1,0:T(8,128)(2,1)} %param.25), kind=kLoop, calls=%fused_computation.49 | loop fusion | bytes 393220 | tf_op jit(solution)/shard_map/dynamic_slice | solution.py:254
  1.6 4.9 %collective-permute-start.81 = (bf16[384,256]{1,0:T(8,128)(2,1)S(1)}, bf16[384,256]{1,0:T(8,128)(2,1)S(1)}, u32[]{:S(2)}, u32[]{:S(2)}) collective-permute-start(bf16[384,256]{1,0:T(8,128)(2,1)S(1)} %pad_maximum_fusion.kv_ref), channel_id=1, source_target_pairs={{0,16},{16,32},{32,48},{48,64},{64,80},{80,96},{96,112},{112,128},... | collective-permute-start | bytes 589832 | tf_op jit(solution)/shard_map/ppermute | solution.py:22
  6.6 3.6 %collective-permute-start.80 = (bf16[384,256]{1,0:T(8,128)(2,1)S(1)}, bf16[384,256]{1,0:T(8,128)(2,1)S(1)}, u32[]{:S(2)}, u32[]{:S(2)}) collective-permute-start(bf16[384,256]{1,0:T(8,128)(2,1)S(1)} %pad_maximum_fusion.kv_ref), channel_id=1, source_target_pairs={{0,32},{16,48},{32,64},{48,80},{64,96},{80,112},{96,128},{112,144}... | collective-permute-start | bytes 589832 | tf_op jit(solution)/shard_map/ppermute | solution.py:22
  10.2 3.6 %collective-permute-start.79 = (bf16[384,256]{1,0:T(8,128)(2,1)S(1)}, bf16[384,256]{1,0:T(8,128)(2,1)S(1)}, u32[]{:S(2)}, u32[]{:S(2)}) collective-permute-start(bf16[384,256]{1,0:T(8,128)(2,1)S(1)} %pad_maximum_fusion.kv_ref), channel_id=1, source_target_pairs={{0,48},{16,64},{32,80},{48,96},{64,112},{80,128},{96,144},{112,160... | collective-permute-start | bytes 589832 | tf_op jit(solution)/shard_map/ppermute | solution.py:22
  13.7 5.9 %own_keys.1 = (f32[384,768]{1,0:T(8,128)S(1)}, f32[384,256]{1,0:T(8,128)S(1)}, f32[3,16,128]{2,1,0:T(8,128)S(1)}, s32[3,8,128]{2,1,0:T(8,128)S(1)}, bf16[2304,12...) custom-call(s32[30]{0:T(128)} %lengths_ref.1, s32[96]{0:T(128)} %plan_ref.1, ...), custom_call_target="tpu_custom_call" | custom-call | flops 2000000000 | bytes 4000000 | tf_op jit(solution)/shard_map/own_keys/pallas_call | solution.py:265
  19.6 0.0 collective-permute-done.81.kv1_ref
  19.6 0.0 collective-permute-done.80.kv2_ref
  19.7 0.0 collective-permute-done.79.kv3_ref
  19.7 4.4 %rest_keys.1 = (bf16[256,768]{1,0:T(8,128)(2,1)S(1)}, bf16[128,768]{1,0:T(8,128)(2,1)S(1)}, bf16[1536,128]{1,0:T(8,128)(2,1)S(1)}, bf16[1152,128]{1,0:T(8,128)(2,1)S(1)}, f32[384,128]{1,0:T(8,128)S(1)}) custom-call(s32[16]{0:T(128)S(1)} %get-tuple-element.216.info, s32[3,8,128]{2,1,0:T(8,128)S(1)} %get-tuple-element.217.starts_ref, ...), custom_call_target="tpu_custom_call" | custom-call | flops 2000000000 | bytes 4000000 | tf_op jit(solution)/shard_map/rest_keys/pallas_call | solution.py:283
  24.0 15.3 %collective-permute-start.82 = (bf16[256,768]{1,0:T(8,128)(2,1)S(1)}, bf16[256,768]{1,0:T(8,128)(2,1)S(1)}, u32[]{:S(2)}, u32[]{:S(2)}) collective-permute-start(bf16[256,768]{1,0:T(8,128)(2,1)S(1)} %get-tuple-element.223.mine12), channel_id=1, source_target_pairs={{0,256},{16,272},{32,288},{48,304},{64,320},{80,336},{96,352},{112... | collective-permute-start | bytes 1179656 | tf_op jit(solution)/shard_map/ppermute | solution.py:26
  40.0 38.7 %conditional.1 = (bf16[128,768]{1,0:T(8,128)(2,1)}, f32[384,128]{1,0:T(8,128)S(1)}, bf16[384,128]{1,0:T(8,128)(2,1)}, bf16[384,128]{1,0:T(8,128)(2,1)}, bf16[384,128]{1,0:T(8,128)(2,1)}) conditional(s32[]{:T(128)} %bitcast, (bf16[1536,128]{1,0:T(8,128)(2,1)S(1)}, f32[384,128]{1,0:T(8,128)S(1)}, ...), branch_computations={%region_0.1_spmd, %region_1.2_spmd, %region_2.3_spmd, %region_3.4_... | conditional | flops 688128 | bytes 7078128 | solution.py:310
  40.0 3.2 %collective-permute-start = (bf16[1536,128]{1,0:T(8,128)(2,1)S(1)}, bf16[1536,128]{1,0:T(8,128)(2,1)S(1)}, u32[]{:S(2)}, u32[]{:S(2)}) collective-permute-start(bf16[1536,128]{1,0:T(8,128)(2,1)S(1)} %get-tuple-element.130), channel_id=1, source_target_pairs={{0,1},{1,0},{2,3},{3,2},{4,5},{5,4},{6,7},{7,6},{8,9},{9,8},{10,11... | collective-permute-start | bytes 1179656 | tf_op jit(solution)/shard_map/cond/branch_0_fun/ppermute | solution.py:26
  43.2 0.7 copy.11
  43.9 8.5 %collective-permute-done = bf16[1536,128]{1,0:T(8,128)(2,1)S(1)} collective-permute-done((bf16[1536,128]{1,0:T(8,128)(2,1)S(1)}, bf16[1536,128]{1,0:T(8,128)(2,1)S(1)}, u32[]{:S(2)}, u32[]{:S(2)}) %collective-permute-start) | collective-permute-done | bytes 393248 | tf_op jit(solution)/shard_map/cond/branch_0_fun/ppermute | solution.py:26
  52.5 0.1 convert_element_type.96
  52.5 0.1 fusion
  52.6 2.9 %collective-permute-start.3 = (bf16[384,128]{1,0:T(8,128)(2,1)S(1)}, bf16[384,128]{1,0:T(8,128)(2,1)}, u32[]{:S(2)}, u32[]{:S(2)}) collective-permute-start(bf16[384,128]{1,0:T(8,128)(2,1)S(1)} %get-tuple-element.237), channel_id=1, source_target_pairs={{16,0},{32,16},{48,32},{64,48},{80,64},{96,80},{112,96},{128,112},... | collective-permute-start | bytes 294920 | tf_op jit(solution)/shard_map/cond/branch_0_fun/ppermute | solution.py:22
  55.5 1.3 %collective-permute-start.2 = (bf16[384,128]{1,0:T(8,128)(2,1)S(1)}, bf16[384,128]{1,0:T(8,128)(2,1)}, u32[]{:S(2)}, u32[]{:S(2)}) collective-permute-start(bf16[384,128]{1,0:T(8,128)(2,1)S(1)} %get-tuple-element.238), channel_id=1, source_target_pairs={{32,0},{48,16},{64,32},{80,48},{96,64},{112,80},{128,96},{144,112}... | collective-permute-start | bytes 294920 | tf_op jit(solution)/shard_map/cond/branch_0_fun/ppermute | solution.py:22
  56.8 1.3 %collective-permute-start.1 = (bf16[384,128]{1,0:T(8,128)(2,1)S(1)}, bf16[384,128]{1,0:T(8,128)(2,1)}, u32[]{:S(2)}, u32[]{:S(2)}) collective-permute-start(bf16[384,128]{1,0:T(8,128)(2,1)S(1)} %get-tuple-element.239), channel_id=1, source_target_pairs={{48,0},{64,16},{80,32},{96,48},{112,64},{128,80},{144,96},{160,112... | collective-permute-start | bytes 294920 | tf_op jit(solution)/shard_map/cond/branch_0_fun/ppermute | solution.py:22
  58.2 16.9 %collective-permute-done.3 = bf16[384,128]{1,0:T(8,128)(2,1)} collective-permute-done((bf16[384,128]{1,0:T(8,128)(2,1)S(1)}, bf16[384,128]{1,0:T(8,128)(2,1)}, u32[]{:S(2)}, u32[]{:S(2)}) %collective-permute-start.3) | collective-permute-done | bytes 98336 | tf_op jit(solution)/shard_map/cond/branch_0_fun/ppermute | solution.py:22
  75.1 0.0 collective-permute-done.2
  75.1 3.6 %collective-permute-done.1 = bf16[384,128]{1,0:T(8,128)(2,1)} collective-permute-done((bf16[384,128]{1,0:T(8,128)(2,1)S(1)}, bf16[384,128]{1,0:T(8,128)(2,1)}, u32[]{:S(2)}, u32[]{:S(2)}) %collective-permute-start.1) | collective-permute-done | bytes 98336 | tf_op jit(solution)/shard_map/cond/branch_0_fun/ppermute | solution.py:22
  78.7 0.0 collective-permute-done.82.theirs12
  78.7 2.6 %place_blocks.1 = (bf16[384,768]{1,0:T(8,128)(2,1)}, bf16[64,384]{1,0:T(8,128)(2,1)}, bf16[64,384]{1,0:T(8,128)(2,1)}) custom-call(s32[16]{0:T(128)S(1)} %get-tuple-element.216.info, bf16[256,768]{1,0:T(8,128)(2,1)S(1)} %get-tuple-element.223.mine12, bf16[128,768]{1,0:T(8,128)(2,1)S(1)} %get-tuple-element.224.mine3, ...), custom_call_target="tpu_custom_call" | custom-call | tf_op jit(solution)/shard_map/place_blocks/pallas_call | solution.py:313
  (3 shorter events, 0.1 us)
Async XLA Ops:
  1.6 18.0 %collective-permute-start.81 = (bf16[384,256]{1,0:T(8,128)(2,1)S(1)}, bf16[384,256]{1,0:T(8,128)(2,1)S(1)}, u32[]{:S(2)}, u32[]{:S(2)}) collective-permute-start(bf16[384,256]{1,0:T(8,128)(2,1)S(1)} %pad_maximum_fusion.kv_ref), channel_id=1, source_target_pairs={{0,16},{16,32},{32,48},{48,64},{64,80},{80,96},{96,112},{112,128},... | collective-permute-start | bytes 589832 | tf_op jit(solution)/shard_map/ppermute | solution.py:22
  6.6 13.1 %collective-permute-start.80 = (bf16[384,256]{1,0:T(8,128)(2,1)S(1)}, bf16[384,256]{1,0:T(8,128)(2,1)S(1)}, u32[]{:S(2)}, u32[]{:S(2)}) collective-permute-start(bf16[384,256]{1,0:T(8,128)(2,1)S(1)} %pad_maximum_fusion.kv_ref), channel_id=1, source_target_pairs={{0,32},{16,48},{32,64},{48,80},{64,96},{80,112},{96,128},{112,144}... | collective-permute-start | bytes 589832 | tf_op jit(solution)/shard_map/ppermute | solution.py:22
  10.2 9.5 %collective-permute-start.79 = (bf16[384,256]{1,0:T(8,128)(2,1)S(1)}, bf16[384,256]{1,0:T(8,128)(2,1)S(1)}, u32[]{:S(2)}, u32[]{:S(2)}) collective-permute-start(bf16[384,256]{1,0:T(8,128)(2,1)S(1)} %pad_maximum_fusion.kv_ref), channel_id=1, source_target_pairs={{0,48},{16,64},{32,80},{48,96},{64,112},{80,128},{96,144},{112,160... | collective-permute-start | bytes 589832 | tf_op jit(solution)/shard_map/ppermute | solution.py:22
  24.0 54.7 %collective-permute-start.82 = (bf16[256,768]{1,0:T(8,128)(2,1)S(1)}, bf16[256,768]{1,0:T(8,128)(2,1)S(1)}, u32[]{:S(2)}, u32[]{:S(2)}) collective-permute-start(bf16[256,768]{1,0:T(8,128)(2,1)S(1)} %get-tuple-element.223.mine12), channel_id=1, source_target_pairs={{0,256},{16,272},{32,288},{48,304},{64,320},{80,336},{96,352},{112... | collective-permute-start | bytes 1179656 | tf_op jit(solution)/shard_map/ppermute | solution.py:26
  40.0 12.4 %collective-permute-start = (bf16[1536,128]{1,0:T(8,128)(2,1)S(1)}, bf16[1536,128]{1,0:T(8,128)(2,1)S(1)}, u32[]{:S(2)}, u32[]{:S(2)}) collective-permute-start(bf16[1536,128]{1,0:T(8,128)(2,1)S(1)} %get-tuple-element.130), channel_id=1, source_target_pairs={{0,1},{1,0},{2,3},{3,2},{4,5},{5,4},{6,7},{7,6},{8,9},{9,8},{10,11... | collective-permute-start | bytes 1179656 | tf_op jit(solution)/shard_map/cond/branch_0_fun/ppermute | solution.py:26
  52.6 22.4 %collective-permute-start.3 = (bf16[384,128]{1,0:T(8,128)(2,1)S(1)}, bf16[384,128]{1,0:T(8,128)(2,1)}, u32[]{:S(2)}, u32[]{:S(2)}) collective-permute-start(bf16[384,128]{1,0:T(8,128)(2,1)S(1)} %get-tuple-element.237), channel_id=1, source_target_pairs={{16,0},{32,16},{48,32},{64,48},{80,64},{96,80},{112,96},{128,112},... | collective-permute-start | bytes 294920 | tf_op jit(solution)/shard_map/cond/branch_0_fun/ppermute | solution.py:22
  55.5 19.6 %collective-permute-start.2 = (bf16[384,128]{1,0:T(8,128)(2,1)S(1)}, bf16[384,128]{1,0:T(8,128)(2,1)}, u32[]{:S(2)}, u32[]{:S(2)}) collective-permute-start(bf16[384,128]{1,0:T(8,128)(2,1)S(1)} %get-tuple-element.238), channel_id=1, source_target_pairs={{32,0},{48,16},{64,32},{80,48},{96,64},{112,80},{128,96},{144,112}... | collective-permute-start | bytes 294920 | tf_op jit(solution)/shard_map/cond/branch_0_fun/ppermute | solution.py:22
  56.8 21.9 %collective-permute-start.1 = (bf16[384,128]{1,0:T(8,128)(2,1)S(1)}, bf16[384,128]{1,0:T(8,128)(2,1)}, u32[]{:S(2)}, u32[]{:S(2)}) collective-permute-start(bf16[384,128]{1,0:T(8,128)(2,1)S(1)} %get-tuple-element.239), channel_id=1, source_target_pairs={{48,0},{64,16},{80,32},{96,48},{112,64},{128,80},{144,96},{160,112... | collective-permute-start | bytes 294920 | tf_op jit(solution)/shard_map/cond/branch_0_fun/ppermute | solution.py:22

commit v4 on v3

v4 whole, which is shorter than its diff:
```python
import functools

import jax
import jax.numpy as jnp
from jax import lax
from jax.experimental import pallas as pl
from jax.experimental.pallas import tpu as pltpu
from jax.sharding import PartitionSpec as P

HEAD_DIM = 128
BLOCK = 128
BACK = 3
VMEM_LIMIT = 20 * 2**20
GROUPS = 4
LOG2E = 1.4426950408889634
SCALE = HEAD_DIM ** -0.5


def shifted(value, axis, steps):
    count = lax.axis_size(axis)
    first, last = (max(0, -steps), min(count, count - steps))
    return lax.ppermute(value, axis, [(i, i + steps) for i in range(first, last)])


def swapped(array, axis, apart):
    return lax.ppermute(array, axis, [(i, i ^ apart) for i in range(lax.axis_size(axis))])


def dot(a, b):
    return jnp.dot(a, b, preferred_element_type=jnp.float32)


def dot_nt(a, b):
    return lax.dot_general(a, b, (((1,), (1,)), ((), ())), preferred_element_type=jnp.float32)


def tile_grads(kt, vt, qs, dos, rows, allowed, heads):
    scores = dot_nt(kt, qs)
    prob_grad = dot_nt(vt, dos)
    weights, score_grads = [], []
    for h in range(heads):
        cols = slice(h * BLOCK, (h + 1) * BLOCK)
        lse = rows[h : h + 1, :]
        delta = rows[heads + h : heads + h + 1, :]
        w = jnp.where(allowed, jnp.exp2(scores[:, cols] * (SCALE * LOG2E) - lse), 0.0)
        weights.append(w.astype(jnp.bfloat16))
        score_grads.append((w * (prob_grad[:, cols] - delta)).astype(jnp.bfloat16))
    w_half = jnp.concatenate(weights, axis=1)
    s_grad = jnp.concatenate(score_grads, axis=1)
    dv = dot(w_half, dos)
    dk = dot(s_grad, qs)
    dq_t = dot(kt.T, s_grad)
    return dq_t, dk, dv


def plan_info(info_ref, branch_ref, lengths_ref, plan_ref, device, half_axis, side, per_device):
    first = device * per_device
    partner = device ^ half_axis
    locals_ = range(per_device)
    theirs = [plan_ref[partner * per_device + s] for s in locals_]
    mine = [plan_ref[first + s] for s in locals_]
    ranks = []
    for l in locals_:
        rank = per_device + l
        for s in locals_:
            rank = jnp.where(theirs[s] == first + l, s, rank)
        ranks.append(rank)
    position = [sum((ranks[m] < ranks[l]).astype(jnp.int32) for m in locals_ if m != l) for l in locals_]
    starts = [jnp.int32(0)] * per_device
    begin = jnp.int32(0)
    for n in range(lengths_ref.shape[0]):
        starts = [jnp.where(begin <= (first + l) * BLOCK, begin, starts[l]) for l in locals_]
        begin = begin + lengths_ref[n]
    info_ref[0] = device
    info_ref[1] = side
    for i in locals_:
        info_ref[2 + i] = sum(jnp.where(position[l] == i, l, 0) for l in locals_)
        info_ref[5 + i] = sum(jnp.where(position[l] == i, starts[l], 0) for l in locals_)
    far_rank = jnp.int32(0)
    for s in locals_:
        local = mine[s] - first
        near = (local >= 0) & (local < per_device)
        near_position = sum(jnp.where(local == l, position[l], 0) for l in locals_)
        info_ref[8 + s] = jnp.where(near, near_position, per_device + far_rank)
        far_rank = far_rank + jnp.where(near, 0, 1)
    mask = jnp.int32(0)
    for pair in range(half_axis):
        full = jnp.bool_(True)
        for s in locals_:
            local = plan_ref[pair * per_device + s] - pair * per_device
            full = full & ((local < 0) | (local >= per_device))
        mask = mask | jnp.where(full, 1 << (pair * GROUPS // half_axis), 0)
    branch_ref[0] = mask
    return starts


def own_kernel(heads, half_axis, lengths_ref, plan_ref, kv_ref, kv1_ref, q_hbm, o_hbm, do_hbm, lse_ref,
               dq_ref, dkv_ref, rows_ref, starts_ref, qs_ref, dos_ref, info_ref, branch_ref,
               q_buf, o_buf, do_buf, sems):
    tokens = kv_ref.shape[0]
    blocks = tokens // BLOCK
    feature = heads * HEAD_DIM

    def copies(j):
        rows = pl.ds(j * BLOCK, BLOCK)
        pairs = ((do_hbm, do_buf), (o_hbm, o_buf), (q_hbm, q_buf))
        return [pltpu.make_async_copy(a.at[rows, :], b.at[rows, :], sems.at[j, n]) for n, (a, b) in enumerate(pairs)]

    for j in range(blocks):
        for c in copies(j):
            c.start()
    device = lax.axis_index("seq")
    base = device * tokens
    dkv_ref[...] = jnp.zeros_like(dkv_ref)
    first_starts = plan_info(info_ref, branch_ref, lengths_ref, plan_ref, device, half_axis, lax.axis_index("head") & 1, blocks)

    pos = base + lax.broadcasted_iota(jnp.int32, (1, tokens), 1)
    start = jnp.zeros((1, tokens), jnp.int32)
    begin = jnp.int32(0)
    for n in range(lengths_ref.shape[0]):
        start = jnp.where(pos >= begin, begin, start)
        begin = begin + lengths_ref[n]

    ones = jnp.ones((8, 2 * HEAD_DIM), jnp.bfloat16)
    for j in range(blocks):
        rows = pl.ds(j * BLOCK, BLOCK)
        lanes = slice(j * BLOCK, (j + 1) * BLOCK)
        for c in copies(j):
            c.wait()
        for h in range(heads):
            cols = pl.ds(h * HEAD_DIM, HEAD_DIM)
            stacked = pl.ds(j * feature + h * HEAD_DIM, HEAD_DIM)
            qs_ref[stacked, :] = q_buf[rows, cols]
            dos_ref[stacked, :] = do_buf[rows, cols]
            prod = do_buf[rows, cols].astype(jnp.float32) * o_buf[rows, cols].astype(jnp.float32)
            high = prod.astype(jnp.bfloat16)
            low = (prod - high.astype(jnp.float32)).astype(jnp.bfloat16)
            row = dot_nt(ones, jnp.concatenate([high, low], axis=1))
            rows_ref[j, heads + h : heads + h + 1, :] = row[0:1, :]
        rows_ref[j, 0:heads, :] = lse_ref[:, lanes].astype(jnp.float32) * LOG2E
        start_row, pos_row = start[:, lanes], pos[:, lanes]
        starts_ref[j] = jnp.broadcast_to(start_row, (8, BLOCK))
        keys = slice(0, (j + 1) * BLOCK)
        queries = pl.ds(j * feature, feature)
        key_pos = base + lax.broadcasted_iota(jnp.int32, ((j + 1) * BLOCK, BLOCK), 0)
        allowed = (key_pos >= start_row) & (key_pos <= pos_row)
        dq_t, dk, dv = tile_grads(kv_ref[keys, 0:HEAD_DIM], kv_ref[keys, HEAD_DIM : 2 * HEAD_DIM],
                                  qs_ref[queries, :], dos_ref[queries, :], rows_ref.at[j], allowed, heads)
        dq_ref[rows, :] = dq_t
        mine = pl.ds(tokens, (j + 1) * BLOCK)
        dkv_ref[mine, 0:HEAD_DIM] += dk
        dkv_ref[mine, HEAD_DIM : 2 * HEAD_DIM] += dv

        @pl.when(first_starts[j] < base)
        def _(j=j, rows=rows, queries=queries, start_row=start_row):
            key_pos = base - tokens + lax.broadcasted_iota(jnp.int32, (tokens, BLOCK), 0)
            dq_t, dk, dv = tile_grads(kv1_ref[:, 0:HEAD_DIM], kv1_ref[:, HEAD_DIM : 2 * HEAD_DIM],
                                      qs_ref[queries, :], dos_ref[queries, :], rows_ref.at[j],
                                      key_pos >= start_row, heads)
            dq_ref[rows, :] += dq_t
            dkv_ref[pl.ds(0, tokens), 0:HEAD_DIM] += dk
            dkv_ref[pl.ds(0, tokens), HEAD_DIM : 2 * HEAD_DIM] += dv


def block_rest(i, heads, info, starts_ref, kv_ref, qs_ref, dos_ref, rows_ref, dqa_ref, dkv_ref, dq_ref, out_ref, row=0):
    tokens = dqa_ref.shape[0]
    feature = heads * HEAD_DIM
    blocks = tokens // BLOCK
    base = (info[0] - BACK) * tokens
    block = jnp.clip(info[2 + i], 0, blocks - 1)
    first = jnp.clip(lax.div(info[5 + i] - base, tokens), 0, BACK - 1)
    queries = pl.ds(pl.multiple_of(block * feature, feature), feature)
    dq_ref[...] = dqa_ref[pl.ds(pl.multiple_of(block * BLOCK, BLOCK), BLOCK), :]
    start_row = starts_ref[block, 0:1, :]

    def step(t, carry):
        keys = pl.ds(pl.multiple_of(t * tokens, tokens), tokens)
        key_pos = base + t * tokens + lax.broadcasted_iota(jnp.int32, (tokens, BLOCK), 0)
        dq_t, dk, dv = tile_grads(kv_ref[keys, 0:HEAD_DIM], kv_ref[keys, HEAD_DIM : 2 * HEAD_DIM],
                                  qs_ref[queries, :], dos_ref[queries, :], rows_ref.at[block],
                                  key_pos >= start_row, heads)
        dq_ref[...] += dq_t
        dkv_ref[keys, 0:HEAD_DIM] += dk
        dkv_ref[keys, HEAD_DIM : 2 * HEAD_DIM] += dv
        return carry

    lax.fori_loop(first, BACK - 1, step, 0)
    for h in range(heads):
        cols = pl.ds(h * HEAD_DIM, HEAD_DIM)
        out_ref[pl.ds(row, BLOCK), cols] = (dq_ref[:, cols].T * SCALE).astype(jnp.bfloat16)


def first_kernel(heads, info, starts_ref, kv2_ref, kv3_ref, qs_ref, dos_ref, rows_ref, dqa_ref,
                 out_ref, kv_ref, dkv_ref, dq_ref):
    tokens = kv3_ref.shape[0]
    dkv_ref[...] = jnp.zeros_like(dkv_ref)
    for n, ref in enumerate((kv3_ref, kv2_ref)):
        kv_ref[pl.ds(n * tokens, tokens), :] = ref[...]
    for i in range(2):
        block_rest(i, heads, info, starts_ref, kv_ref, qs_ref, dos_ref, rows_ref, dqa_ref, dkv_ref, dq_ref, out_ref,
                   i * BLOCK)


def rest_kernel(heads, info, starts_ref, kv_ref, qs_ref, dos_ref, rows_ref, dqa_ref, dkva_ref, dkvb_ref,
                third_ref, send_ref, far_ref, own_ref, dq_ref, dkv_ref):
    tokens = dkva_ref.shape[0] // 2
    dkv_ref[...] = dkvb_ref[...]
    block_rest(2, heads, info, starts_ref, kv_ref, qs_ref, dos_ref, rows_ref, dqa_ref, dkv_ref, dq_ref, third_ref)

    side = info[1]
    half = HEAD_DIM // 2
    left = lax.broadcasted_iota(jnp.int32, (tokens, HEAD_DIM), 1) < half
    for n in range(BACK + 1):
        rows = pl.ds(n * tokens, tokens)
        ref, first = (dkv_ref, n * tokens) if n < BACK - 1 else (dkva_ref, (n - BACK + 1) * tokens)
        dk = ref[pl.ds(first, tokens), 0:HEAD_DIM] * SCALE
        dv = ref[pl.ds(first, tokens), HEAD_DIM : 2 * HEAD_DIM]
        low = jnp.where(left, dk, pltpu.roll(dv, half, 1))
        high = jnp.where(left, pltpu.roll(dk, half, 1), dv)
        send_ref[rows, :] = jnp.where(side == 0, high, low).astype(jnp.bfloat16)
        kept = jnp.where(side == 0, low, high)
        if n < BACK:
            far_ref[rows, :] = kept.astype(jnp.bfloat16)
        else:
            own_ref[...] = kept


def place(info, first, pair, single, out_ref, sems, act):
    arrays = (pair.at[pl.ds(0, BLOCK), :], pair.at[pl.ds(BLOCK, BLOCK), :], single)
    for s in range(3):
        for number, array in enumerate(arrays):
            @pl.when(info[8 + s] == first + number)
            def _(array=array, s=s):
                getattr(pltpu.make_async_copy(array, out_ref.at[pl.ds(s * BLOCK, BLOCK), :], sems.at[s]), act)()


def keep_kernel(info, mine12, mine3, out_ref, sems):
    place(info, 0, mine12, mine3, out_ref, sems, "start")
    place(info, 0, mine12, mine3, out_ref, sems, "wait")


def finish_kernel(info, theirs12, theirs3, own_ref, mate_ref, r2_ref, r3_ref, placed_ref,
                  out_ref, key_ref, value_ref, sems):
    place(info, 3, theirs12, theirs3, out_ref, sems, "start")
    total = own_ref[...] + r2_ref[...].astype(jnp.float32) + r3_ref[...].astype(jnp.float32)
    tokens = total.shape[0]
    total = total + jnp.where(lax.rem(info[0], 2) == 0, mate_ref[tokens:, :].astype(jnp.float32), 0.0)
    half = HEAD_DIM // 2
    for n in range(total.shape[0] // BLOCK):
        lanes = slice(n * BLOCK, (n + 1) * BLOCK)
        turned = total[lanes, :].T.astype(jnp.bfloat16)
        key_ref[:, lanes] = turned[:half]
        value_ref[:, lanes] = turned[half:]
    place(info, 3, theirs12, theirs3, out_ref, sems, "wait")


def on_device(queries, key_states, value_states, attn_out, grad_out, log_norm, lengths, block_plan):
    tokens, feature = queries.shape
    heads = feature // HEAD_DIM
    blocks = tokens // BLOCK
    half_axis = lax.axis_size("seq") // 2
    window = BACK * tokens
    kv_group = lax.axis_index("head") // 2
    own_kv = jnp.concatenate([
        lax.dynamic_slice_in_dim(key_states, kv_group * HEAD_DIM, HEAD_DIM, 1),
        lax.dynamic_slice_in_dim(value_states, kv_group * HEAD_DIM, HEAD_DIM, 1)], axis=1)
    devices = 2 * half_axis
    kv1, kv2, kv3 = (shifted(own_kv, "seq", n) for n in (1, 2, 3))
    later = (BACK - 1) * tokens
    f32, bf16, i32 = jnp.float32, jnp.bfloat16, jnp.int32
    queries, attn_out, grad_out, log_norm, lengths, block_plan = (
        pltpu.with_memory_space_constraint(a, pltpu.HBM)
        for a in (queries, attn_out, grad_out, log_norm, lengths, block_plan))
    smem = pl.BlockSpec(memory_space=pltpu.SMEM)
    vmem = pl.BlockSpec(memory_space=pltpu.VMEM)
    hbm = pl.BlockSpec(memory_space=pltpu.HBM)
    params = pltpu.CompilerParams(vmem_limit_bytes=VMEM_LIMIT)
    own_dq, own_dkv, rows, starts, qs, dos, info, branch = pl.pallas_call(
        functools.partial(own_kernel, heads, half_axis),
        in_specs=[smem, smem, vmem, vmem, hbm, hbm, hbm, vmem],
        out_specs=[vmem] * 6 + [smem] * 2,
        out_shape=[pltpu.VMEM((tokens, feature), f32),
                   pltpu.VMEM((2 * tokens, 2 * HEAD_DIM), f32),
                   pltpu.VMEM((blocks, 16, BLOCK), f32),
                   pltpu.VMEM((blocks, 8, BLOCK), i32),
                   pltpu.VMEM((blocks * feature, HEAD_DIM), bf16),
                   pltpu.VMEM((blocks * feature, HEAD_DIM), bf16),
                   jax.ShapeDtypeStruct((16,), i32),
                   jax.ShapeDtypeStruct((1,), i32)],
        scratch_shapes=[pltpu.VMEM((tokens, feature), bf16)] * 3 + [pltpu.SemaphoreType.DMA((blocks, 3))],
        compiler_params=params,
        cost_estimate=pl.CostEstimate(flops=2_000_000_000, bytes_accessed=4_000_000, transcendentals=600_000),
        name="own_keys",
    )(lengths, block_plan, own_kv, kv1, queries, attn_out, grad_out, log_norm)

    cost = pl.CostEstimate(flops=1_000, bytes_accessed=1_000, transcendentals=0)
    dq12, kv, dkv = pl.pallas_call(
        functools.partial(first_kernel, heads),
        in_specs=[smem] + [vmem] * 7,
        out_specs=[vmem] * 3,
        out_shape=[pltpu.VMEM((2 * BLOCK, feature), bf16),
                   pltpu.VMEM((later, 2 * HEAD_DIM), bf16),
                   pltpu.VMEM((later, 2 * HEAD_DIM), f32)],
        scratch_shapes=[pltpu.VMEM((BLOCK, feature), f32)],
        compiler_params=params,
        cost_estimate=cost,
        name="first_blocks",
    )(info, starts, kv2, kv3, qs, dos, rows, own_dq)
    theirs12 = swapped(dq12, "seq", half_axis)

    dq3, send, far, own = pl.pallas_call(
        functools.partial(rest_kernel, heads),
        in_specs=[smem] + [vmem] * 8,
        out_specs=[vmem] * 4,
        out_shape=[pltpu.VMEM((BLOCK, feature), bf16),
                   pltpu.VMEM((window + tokens, HEAD_DIM), bf16),
                   pltpu.VMEM((window, HEAD_DIM), bf16),
                   pltpu.VMEM((tokens, HEAD_DIM), f32)],
        scratch_shapes=[pltpu.VMEM((BLOCK, feature), f32), pltpu.VMEM((later, 2 * HEAD_DIM), f32)],
        compiler_params=params,
        cost_estimate=cost,
        name="last_block",
    )(info, starts, kv, qs, dos, rows, own_dq, own_dkv, dkv)

    def returns(mask, dq3, send, far, own):
        pairs = [(i, i ^ half_axis) for i in range(2 * half_axis) if mask >> (i % half_axis * GROUPS // half_axis) & 1]
        theirs3 = lax.ppermute(dq3, "seq", pairs) if pairs else dq3
        arrived = swapped(send, "head", 1).astype(f32)
        third, second, first = ((far[n * tokens : (n + 1) * tokens].astype(f32)
                                 + arrived[n * tokens : (n + 1) * tokens]).astype(bf16) for n in range(BACK))
        odd = lax.axis_index("seq") % 2 == 1
        mate = swapped(jnp.concatenate([jnp.where(odd, third, first), first], axis=0), "seq", 1)
        back3 = lax.ppermute(third, "seq", [(i, i - 3) for i in range(4, devices, 2)])
        back2 = shifted((second.astype(f32) + mate[:tokens].astype(f32)).astype(bf16), "seq", -2)
        return (theirs3, own + arrived[window:], mate, back2, back3)

    branches = [functools.partial(returns, mask) for mask in range(1 << GROUPS)]
    theirs3, own, mate, back2, back3 = lax.switch(branch.reshape(()), branches, dq3, send, far, own)

    grad_half = jax.ShapeDtypeStruct((HEAD_DIM // 2, tokens), bf16)
    whole = jax.ShapeDtypeStruct((tokens, feature), bf16)
    copy_sems = [pltpu.SemaphoreType.DMA((3,))]
    placed = pl.pallas_call(
        keep_kernel,
        in_specs=[smem, vmem, vmem],
        out_specs=hbm,
        out_shape=whole,
        scratch_shapes=copy_sems,
        compiler_params=params,
        name="keep_blocks",
    )(info, dq12, dq3)
    query_grad, key_grad, value_grad = pl.pallas_call(
        finish_kernel,
        in_specs=[smem] + [vmem] * 6 + [hbm],
        out_specs=[hbm, vmem, vmem],
        out_shape=[whole, grad_half, grad_half],
        input_output_aliases={7: 0},
        scratch_shapes=copy_sems,
        compiler_params=params,
        name="place_blocks",
    )(info, theirs12, theirs3, own, mate, back2, back3, placed)
    return query_grad, key_grad.T, value_grad.T


def solution(mesh):
    placed = (
        P("seq", "head"),
        P("seq", None),
        P("seq", None),
        P("seq", "head"),
        P("seq", "head"),
        P("head", "seq"),
        P(),
        P(),
    )
    return jax.shard_map(
        on_device,
        mesh=mesh,
        in_specs=placed,
        out_specs=(P("seq", "head"), P("seq", "head"), P("seq", "head")),
        check_vma=False,
    )
```

time: 81.7 us -> 81.1 us (level); the launches traced: 81.3 us -> 81.5 us
  waiting for transfers between devices: 29.1 us -> 25.7 us
  starting transfers between devices: 36 us -> 39.3 us
  other arithmetic: 0.18 us -> 1.11 us
    ppermute x6 -> x4, waiting for transfers between devices: 20.6 us -> 0.01 us  [shifted(): lax.ppermute(value, axis, [(i, i + steps) for i in range(first, last)])]
    ppermute x0 -> x2, waiting for transfers between devices: none -> 17.7 us  [the longest x1 17.7 us: returns(): lax.ppermute(third, 'seq', [(i, i - 3) for i in range(4, devices, 2)])]
    ppermute x2 -> x3, starting transfers between devices: 18.5 us -> 23.6 us  [swapped(): lax.ppermute(array, axis, [(i, i ^ apart) for i in range(lax.axis_size(ax...]
    ppermute x6 -> x4, starting transfers between devices: 17.5 us -> 13.1 us  [shifted(): lax.ppermute(value, axis, [(i, i + steps) for i in range(first, last)])]
    pallas_call x1, Pallas kernels: 4.37 us -> 1.11 us  [on_device(): pl.pallas_call(functools.partial(rest_kernel, heads), in_specs=[smem] + [...]
    ppermute x0 -> x2, starting transfers between devices: none -> 2.63 us  [the longest x1 1.35 us: returns(): theirs3 = lax.ppermute(dq3, 'seq', pairs) if pairs else dq3]
    pallas_call x1 -> x3, Pallas kernels: 2.6 us -> 4.8 us  [the longest x1 2.55 us: on_device(): pl.pallas_call(finish_kernel, in_specs=[smem] + [vmem] * 6 + [hbm], out_s...]
    pallas_call x1, Pallas kernels: 5.91 us -> 6.89 us  [on_device(): pl.pallas_call(functools.partial(own_kernel, heads, half_axis), in_specs=...]
  transfers between devices with their start and end apart: 8 -> 9, of which waited for: 3 -> 2; matrix products, arithmetic and copies ran while one was open for 1% -> 1% of each run, Pallas kernels for 7% -> 11%
where the time goes in v4:
time: 81.1 us; the launch traced here: 81.5 us
  starting transfers between devices  39.3 us (48%)
  waiting for transfers between devices  25.7 us (32%)
  Pallas kernels  12.8 us (16%)
  between operations  1.56 us (2%)
  other arithmetic  1.11 us (1%)
  local copies, waits for them, and re-layouts  0.96 us (1%)
    ppermute x3, starting transfers between devices, swapped(): lax.ppermute(array, axis, [(i, i ^ apart) for i in range(lax.axis_size(ax...  23.6 us
    ppermute x1, waiting for transfers between devices, returns(): lax.ppermute(third, 'seq', [(i, i - 3) for i in range(4, devices, 2)])  17.7 us
    ppermute x4, starting transfers between devices, shifted(): lax.ppermute(value, axis, [(i, i + steps) for i in range(first, last)])  13.1 us
    ppermute x3, waiting for transfers between devices, swapped(): lax.ppermute(array, axis, [(i, i ^ apart) for i in range(lax.axis_size(ax...  7.97 us
    pallas_call x1, Pallas kernels, on_device(): pl.pallas_call(functools.partial(own_kernel, heads, half_axis), in_specs=...  6.89 us
    pallas_call x1, Pallas kernels, on_device(): pl.pallas_call(finish_kernel, in_specs=[smem] + [vmem] * 6 + [hbm], out_s...  2.55 us
  transfers between devices with their start and end apart: 9, of which 2 were waited for; matrix products, arithmetic and copies ran while one was open for 1% of the time, Pallas kernels for 11%

profile of v4, /device:TPU:1, one launch (start us, length us, event | category | flops | bytes accessed | tf_op | source)
XLA Modules:
  0.0 81.5 jit_solution(16482227993555263471)
XLA Ops:
  0.6 1.0 %constant_dynamic-slice_fusion = (bf16[384,128]{1,0:T(8,128)(2,1)S(1)}, bf16[384,128]{1,0:T(8,128)(2,1)S(1)}) fusion(bf16[384,1024]{1,0:T(8,128)(2,1)} %param.26, s32[]{:T(128)S(6)} %select_n.174, bf16[384,1024]{1,0:T(8,128)(2,1)} %param.25), kind=kLoop, calls=%fused_computation.161 | loop fusion | bytes 393220 | tf_op jit(solution)/shard_map/dynamic_slice | solution.py:266
  1.6 4.9 %collective-permute-start.79 = (bf16[384,256]{1,0:T(8,128)(2,1)S(1)}, bf16[384,256]{1,0:T(8,128)(2,1)S(1)}, u32[]{:S(2)}, u32[]{:S(2)}) collective-permute-start(bf16[384,256]{1,0:T(8,128)(2,1)S(1)} %pad_maximum_fusion.16.kv_ref), channel_id=1, source_target_pairs={{0,16},{16,32},{32,48},{48,64},{64,80},{80,96},{96,112},{112,128},... | collective-permute-start | bytes 589832 | tf_op jit(solution)/shard_map/ppermute | solution.py:22
  6.6 3.3 %collective-permute-start.81 = (bf16[384,256]{1,0:T(8,128)(2,1)S(1)}, bf16[384,256]{1,0:T(8,128)(2,1)S(1)}, u32[]{:S(2)}, u32[]{:S(2)}) collective-permute-start(bf16[384,256]{1,0:T(8,128)(2,1)S(1)} %pad_maximum_fusion.16.kv_ref), channel_id=1, source_target_pairs={{0,48},{16,64},{32,80},{48,96},{64,112},{80,128},{96,144},{112,160... | collective-permute-start | bytes 589832 | tf_op jit(solution)/shard_map/ppermute | solution.py:22
  9.9 3.5 %collective-permute-start.80 = (bf16[384,256]{1,0:T(8,128)(2,1)S(1)}, bf16[384,256]{1,0:T(8,128)(2,1)S(1)}, u32[]{:S(2)}, u32[]{:S(2)}) collective-permute-start(bf16[384,256]{1,0:T(8,128)(2,1)S(1)} %pad_maximum_fusion.16.kv_ref), channel_id=1, source_target_pairs={{0,32},{16,48},{32,64},{48,80},{64,96},{80,112},{96,128},{112,144}... | collective-permute-start | bytes 589832 | tf_op jit(solution)/shard_map/ppermute | solution.py:22
  13.4 0.0 collective-permute-done.79.kv1_ref
  13.4 6.9 %own_keys.1 = (f32[384,768]{1,0:T(8,128)S(1)}, f32[768,256]{1,0:T(8,128)S(1)}, f32[3,16,128]{2,1,0:T(8,128)S(1)}, s32[3,8,128]{2,1,0:T(8,128)S(1)}, bf16[2304,12...) custom-call(s32[30]{0:T(128)} %lengths_ref.1, s32[96]{0:T(128)} %plan_ref.1, ...), custom_call_target="tpu_custom_call" | custom-call | flops 2000000000 | bytes 4000000 | tf_op jit(solution)/shard_map/own_keys/pallas_call | solution.py:278
  20.3 0.0 collective-permute-done.81.kv3_ref
  20.4 0.0 collective-permute-done.80.kv2_ref
  20.4 1.0 %first_blocks.1 = (bf16[256,768]{1,0:T(8,128)(2,1)S(1)}, bf16[768,256]{1,0:T(8,128)(2,1)S(1)}, f32[768,256]{1,0:T(8,128)S(1)}) custom-call(s32[16]{0:T(128)S(1)} %get-tuple-element.218.info, s32[3,8,128]{2,1,0:T(8,128)S(1)} %get-tuple-element.219.starts_ref, bf16[384,256]{1,0:T(8,128)(2,1)S(1)} %collective-permute-done.80.kv2_ref, ...), custom_call_target="tpu_custom_call" | custom-call | flops 1000 | bytes 1000 | tf_op jit(solution)/shard_map/first_blocks/pallas_call | solution.py:297
  21.4 16.3 %collective-permute-start.82 = (bf16[256,768]{1,0:T(8,128)(2,1)S(1)}, bf16[256,768]{1,0:T(8,128)(2,1)S(1)}, u32[]{:S(2)}, u32[]{:S(2)}) collective-permute-start(bf16[256,768]{1,0:T(8,128)(2,1)S(1)} %get-tuple-element.224.mine12), channel_id=1, source_target_pairs={{0,256},{16,272},{32,288},{48,304},{64,320},{80,336},{96,352},{112... | collective-permute-start | bytes 1179656 | tf_op jit(solution)/shard_map/ppermute | solution.py:26
  37.6 1.1 %last_block.1 = (bf16[128,768]{1,0:T(8,128)(2,1)S(1)}, bf16[1536,128]{1,0:T(8,128)(2,1)S(1)}, bf16[1152,128]{1,0:T(8,128)(2,1)S(1)}, f32[384,128]{1,0:T(8,128)S(1)}) custom-call(s32[16]{0:T(128)S(1)} %get-tuple-element.218.info, s32[3,8,128]{2,1,0:T(8,128)S(1)} %get-tuple-element.219.starts_ref, bf16[768,256]{1,0:T(8,128)(2,1)S(1)} %get-tuple-element.226.kv_ref, ...), custom_call_target="tpu_custom_call" | custom-call | flops 1000 | bytes 1000 | tf_op jit(solution)/shard_map/last_block/pallas_call | solution.py:311
  38.8 1.3 %keep_blocks.1.placed_ref = bf16[384,768]{1,0:T(8,128)(2,1)} custom-call(s32[16]{0:T(128)S(1)} %get-tuple-element.218.info, bf16[256,768]{1,0:T(8,128)(2,1)S(1)} %get-tuple-element.224.mine12, bf16[128,768]{1,0:T(8,128)(2,1)S(1)} %get-tuple-element.232.mine3), custom_call_target="tpu_custom_call" | custom-call | tf_op jit(solution)/shard_map/keep_blocks/pallas_call | solution.py:343
  40.7 38.1 %conditional.1 = (bf16[128,768]{1,0:T(8,128)(2,1)}, f32[384,128]{1,0:T(8,128)S(1)}, bf16[768,128]{1,0:T(8,128)(2,1)}, bf16[384,128]{1,0:T(8,128)(2,1)}, bf16[384,128]{1,0:T(8,128)(2,1)}) conditional(s32[]{:T(128)} %bitcast, (bf16[1536,128]{1,0:T(8,128)(2,1)S(1)}, f32[384,128]{1,0:T(8,128)S(1)}, ...), branch_computations={%region_0.1_spmd, %region_1.2_spmd, %region_2.3_spmd, %region_3.4_... | conditional | flops 1327119 | bytes 7471495 | solution.py:338
  40.7 3.2 %collective-permute-start.10 = (bf16[1536,128]{1,0:T(8,128)(2,1)S(1)}, bf16[1536,128]{1,0:T(8,128)(2,1)S(1)}, u32[]{:S(2)}, u32[]{:S(2)}) collective-permute-start(bf16[1536,128]{1,0:T(8,128)(2,1)S(1)} %get-tuple-element.138), channel_id=1, source_target_pairs={{0,1},{1,0},{2,3},{3,2},{4,5},{5,4},{6,7},{7,6},{8,9},{9,8},{10,11... | collective-permute-start | bytes 1179656 | tf_op jit(solution)/shard_map/cond/branch_2_fun/ppermute | solution.py:26
  43.9 8.0 %collective-permute-done.10 = bf16[1536,128]{1,0:T(8,128)(2,1)S(1)} collective-permute-done((bf16[1536,128]{1,0:T(8,128)(2,1)S(1)}, bf16[1536,128]{1,0:T(8,128)(2,1)S(1)}, u32[]{:S(2)}, u32[]{:S(2)}) %collective-permute-start.10) | collective-permute-done | bytes 393248 | tf_op jit(solution)/shard_map/cond/branch_2_fun/ppermute | solution.py:26
  51.9 0.1 convert_element_type.340
  52.0 0.1 broadcast_select_fusion.2
  52.1 4.1 %collective-permute-start.11 = (bf16[768,128]{1,0:T(8,128)(2,1)S(1)}, bf16[768,128]{1,0:T(8,128)(2,1)}, u32[]{:S(2)}, u32[]{:S(2)}) collective-permute-start(bf16[768,128]{1,0:T(8,128)(2,1)S(1)} %pad_maximum_fusion.2), channel_id=1, source_target_pairs={{0,16},{16,0},{32,48},{48,32},{64,80},{80,64},{96,112},{112,96},{1... | collective-permute-start | bytes 589832 | tf_op jit(solution)/shard_map/cond/branch_2_fun/ppermute | solution.py:26
  56.2 1.4 %collective-permute-start.9 = (bf16[128,768]{1,0:T(8,128)(2,1)S(1)}, bf16[128,768]{1,0:T(8,128)(2,1)}, u32[]{:S(2)}, u32[]{:S(2)}) collective-permute-start(bf16[128,768]{1,0:T(8,128)(2,1)S(1)} %get-tuple-element.136), channel_id=1, source_target_pairs={{64,320},{80,336},{96,352},{112,368},{320,64},{336,80},{352,96},{3... | collective-permute-start | bytes 589832 | tf_op jit(solution)/shard_map/cond/branch_2_fun/ppermute | solution.py:327
  57.6 1.3 %collective-permute-start.13 = (bf16[384,128]{1,0:T(8,128)(2,1)S(1)}, bf16[384,128]{1,0:T(8,128)(2,1)}, u32[]{:S(2)}, u32[]{:S(2)}) collective-permute-start(bf16[384,128]{1,0:T(8,128)(2,1)S(1)} %get-tuple-element.248), channel_id=1, source_target_pairs={{64,16},{96,48},{128,80},{160,112},{192,144},{224,176},{256,208},{... | collective-permute-start | bytes 294920 | tf_op jit(solution)/shard_map/cond/branch_2_fun/ppermute | solution.py:333
  58.8 0.0 collective-permute-done.11
  58.9 0.9 %add_convert_fusion.2 = (bf16[384,128]{1,0:T(8,128)(2,1)S(1)}, f32[384,128]{1,0:T(8,128)S(1)}) fusion(f32[1536,128]{1,0:T(8,128)S(1)} %convert_element_type.340, bf16[768,128]{1,0:T(8,128)(2,1)} %collective-permute-done.11, bf16[1152,128]{1,0:T(8,128)(2,1)S(1)} %get-tuple-element.139, f32[384,128]{1,0:T(8,128)S(1)} %get-tuple-element.137), kind=kLoop, calls=%fused_computation.28 | loop fusion | flops 393216 | bytes 1081344 | tf_op jit(solution)/shard_map/cond/branch_2_fun/convert_element_type | solution.py:334
  59.8 1.3 %collective-permute-start.12 = (bf16[384,128]{1,0:T(8,128)(2,1)S(1)}, bf16[384,128]{1,0:T(8,128)(2,1)}, u32[]{:S(2)}, u32[]{:S(2)}) collective-permute-start(bf16[384,128]{1,0:T(8,128)(2,1)S(1)} %get-tuple-element.293), channel_id=1, source_target_pairs={{32,0},{48,16},{64,32},{80,48},{96,64},{112,80},{128,96},{144,112}... | collective-permute-start | bytes 294920 | tf_op jit(solution)/shard_map/cond/branch_2_fun/ppermute | solution.py:22
  61.1 0.0 collective-permute-done.9
  61.1 17.7 %collective-permute-done.13 = bf16[384,128]{1,0:T(8,128)(2,1)} collective-permute-done((bf16[384,128]{1,0:T(8,128)(2,1)S(1)}, bf16[384,128]{1,0:T(8,128)(2,1)}, u32[]{:S(2)}, u32[]{:S(2)}) %collective-permute-start.13) | collective-permute-done | bytes 98336 | tf_op jit(solution)/shard_map/cond/branch_2_fun/ppermute | solution.py:333
  78.8 0.0 collective-permute-done.12
  78.8 0.0 collective-permute-done.82.theirs12
  78.8 2.6 %place_blocks.1 = (bf16[384,768]{1,0:T(8,128)(2,1)}, bf16[64,384]{1,0:T(8,128)(2,1)}, bf16[64,384]{1,0:T(8,128)(2,1)}) custom-call(s32[16]{0:T(128)S(1)} %get-tuple-element.218.info, bf16[256,768]{1,0:T(8,128)(2,1)S(1)} %collective-permute-done.82.theirs12, bf16[128,768]{1,0:T(8,128)(2,1)} %get-tuple-element.233.theirs3, ...), custom_call_target="tpu_custom_call", output_to_operand_aliasing={{0}: (7, {})} | custom-call | tf_op jit(solution)/shard_map/place_blocks/pallas_call | solution.py:352
  (2 shorter events, 0.0 us)
Async XLA Ops:
  1.6 11.8 %collective-permute-start.79 = (bf16[384,256]{1,0:T(8,128)(2,1)S(1)}, bf16[384,256]{1,0:T(8,128)(2,1)S(1)}, u32[]{:S(2)}, u32[]{:S(2)}) collective-permute-start(bf16[384,256]{1,0:T(8,128)(2,1)S(1)} %pad_maximum_fusion.16.kv_ref), channel_id=1, source_target_pairs={{0,16},{16,32},{32,48},{48,64},{64,80},{80,96},{96,112},{112,128},... | collective-permute-start | bytes 589832 | tf_op jit(solution)/shard_map/ppermute | solution.py:22
  6.6 13.8 %collective-permute-start.81 = (bf16[384,256]{1,0:T(8,128)(2,1)S(1)}, bf16[384,256]{1,0:T(8,128)(2,1)S(1)}, u32[]{:S(2)}, u32[]{:S(2)}) collective-permute-start(bf16[384,256]{1,0:T(8,128)(2,1)S(1)} %pad_maximum_fusion.16.kv_ref), channel_id=1, source_target_pairs={{0,48},{16,64},{32,80},{48,96},{64,112},{80,128},{96,144},{112,160... | collective-permute-start | bytes 589832 | tf_op jit(solution)/shard_map/ppermute | solution.py:22
  9.9 10.5 %collective-permute-start.80 = (bf16[384,256]{1,0:T(8,128)(2,1)S(1)}, bf16[384,256]{1,0:T(8,128)(2,1)S(1)}, u32[]{:S(2)}, u32[]{:S(2)}) collective-permute-start(bf16[384,256]{1,0:T(8,128)(2,1)S(1)} %pad_maximum_fusion.16.kv_ref), channel_id=1, source_target_pairs={{0,32},{16,48},{32,64},{48,80},{64,96},{80,112},{96,128},{112,144}... | collective-permute-start | bytes 589832 | tf_op jit(solution)/shard_map/ppermute | solution.py:22
  21.4 57.5 %collective-permute-start.82 = (bf16[256,768]{1,0:T(8,128)(2,1)S(1)}, bf16[256,768]{1,0:T(8,128)(2,1)S(1)}, u32[]{:S(2)}, u32[]{:S(2)}) collective-permute-start(bf16[256,768]{1,0:T(8,128)(2,1)S(1)} %get-tuple-element.224.mine12), channel_id=1, source_target_pairs={{0,256},{16,272},{32,288},{48,304},{64,320},{80,336},{96,352},{112... | collective-permute-start | bytes 1179656 | tf_op jit(solution)/shard_map/ppermute | solution.py:26
  40.7 11.2 %collective-permute-start.10 = (bf16[1536,128]{1,0:T(8,128)(2,1)S(1)}, bf16[1536,128]{1,0:T(8,128)(2,1)S(1)}, u32[]{:S(2)}, u32[]{:S(2)}) collective-permute-start(bf16[1536,128]{1,0:T(8,128)(2,1)S(1)} %get-tuple-element.138), channel_id=1, source_target_pairs={{0,1},{1,0},{2,3},{3,2},{4,5},{5,4},{6,7},{7,6},{8,9},{9,8},{10,11... | collective-permute-start | bytes 1179656 | tf_op jit(solution)/shard_map/cond/branch_2_fun/ppermute | solution.py:26
  52.1 6.8 %collective-permute-start.11 = (bf16[768,128]{1,0:T(8,128)(2,1)S(1)}, bf16[768,128]{1,0:T(8,128)(2,1)}, u32[]{:S(2)}, u32[]{:S(2)}) collective-permute-start(bf16[768,128]{1,0:T(8,128)(2,1)S(1)} %pad_maximum_fusion.2), channel_id=1, source_target_pairs={{0,16},{16,0},{32,48},{48,32},{64,80},{80,64},{96,112},{112,96},{1... | collective-permute-start | bytes 589832 | tf_op jit(solution)/shard_map/cond/branch_2_fun/ppermute | solution.py:26
  56.2 4.9 %collective-permute-start.9 = (bf16[128,768]{1,0:T(8,128)(2,1)S(1)}, bf16[128,768]{1,0:T(8,128)(2,1)}, u32[]{:S(2)}, u32[]{:S(2)}) collective-permute-start(bf16[128,768]{1,0:T(8,128)(2,1)S(1)} %get-tuple-element.136), channel_id=1, source_target_pairs={{64,320},{80,336},{96,352},{112,368},{320,64},{336,80},{352,96},{3... | collective-permute-start | bytes 589832 | tf_op jit(solution)/shard_map/cond/branch_2_fun/ppermute | solution.py:327
  57.6 21.3 %collective-permute-start.13 = (bf16[384,128]{1,0:T(8,128)(2,1)S(1)}, bf16[384,128]{1,0:T(8,128)(2,1)}, u32[]{:S(2)}, u32[]{:S(2)}) collective-permute-start(bf16[384,128]{1,0:T(8,128)(2,1)S(1)} %get-tuple-element.248), channel_id=1, source_target_pairs={{64,16},{96,48},{128,80},{160,112},{192,144},{224,176},{256,208},{... | collective-permute-start | bytes 294920 | tf_op jit(solution)/shard_map/cond/branch_2_fun/ppermute | solution.py:333
  59.8 19.0 %collective-permute-start.12 = (bf16[384,128]{1,0:T(8,128)(2,1)S(1)}, bf16[384,128]{1,0:T(8,128)(2,1)}, u32[]{:S(2)}, u32[]{:S(2)}) collective-permute-start(bf16[384,128]{1,0:T(8,128)(2,1)S(1)} %get-tuple-element.293), channel_id=1, source_target_pairs={{32,0},{48,16},{64,32},{80,48},{96,64},{112,80},{128,96},{144,112}... | collective-permute-start | bytes 294920 | tf_op jit(solution)/shard_map/cond/branch_2_fun/ppermute | solution.py:22

commit v5 on v4

--- a/solution.py
+++ b/solution.py
@@ -91,13 +91,11 @@
             full = full & ((local < 0) | (local >= per_device))
         mask = mask | jnp.where(full, 1 << (pair * GROUPS // half_axis), 0)
     branch_ref[0] = mask
-    return starts
-
-
-def own_kernel(heads, half_axis, lengths_ref, plan_ref, kv_ref, kv1_ref, q_hbm, o_hbm, do_hbm, lse_ref,
-               dq_ref, dkv_ref, rows_ref, starts_ref, qs_ref, dos_ref, info_ref, branch_ref,
-               q_buf, o_buf, do_buf, sems):
-    tokens = kv_ref.shape[0]
+
+
+def prepare_kernel(heads, half_axis, lengths_ref, plan_ref, q_hbm, o_hbm, do_hbm, lse_ref,
+                   rows_ref, starts_ref, qs_ref, dos_ref, info_ref, branch_ref, q_buf, o_buf, do_buf, sems):
+    tokens = q_buf.shape[0]
     blocks = tokens // BLOCK
     feature = heads * HEAD_DIM
 
@@ -110,11 +108,9 @@
         for c in copies(j):
             c.start()
     device = lax.axis_index("seq")
-    base = device * tokens
-    dkv_ref[...] = jnp.zeros_like(dkv_ref)
-    first_starts = plan_info(info_ref, branch_ref, lengths_ref, plan_ref, device, half_axis, lax.axis_index("head") & 1, blocks)
-
-    pos = base + lax.broadcasted_iota(jnp.int32, (1, tokens), 1)
+    plan_info(info_ref, branch_ref, lengths_ref, plan_ref, device, half_axis, lax.axis_index("head") & 1, blocks)
+
+    pos = device * tokens + lax.broadcasted_iota(jnp.int32, (1, tokens), 1)
     start = jnp.zeros((1, tokens), jnp.int32)
     begin = jnp.int32(0)
     for n in range(lengths_ref.shape[0]):
@@ -125,6 +121,8 @@
     for j in range(blocks):
         rows = pl.ds(j * BLOCK, BLOCK)
         lanes = slice(j * BLOCK, (j + 1) * BLOCK)
+        starts_ref[j] = jnp.broadcast_to(start[:, lanes], (8, BLOCK))
+        rows_ref[j, 0:heads, :] = lse_ref[:, lanes].astype(jnp.float32) * LOG2E
         for c in copies(j):
             c.wait()
         for h in range(heads):
@@ -137,29 +135,25 @@
             low = (prod - high.astype(jnp.float32)).astype(jnp.bfloat16)
             row = dot_nt(ones, jnp.concatenate([high, low], axis=1))
             rows_ref[j, heads + h : heads + h + 1, :] = row[0:1, :]
-        rows_ref[j, 0:heads, :] = lse_ref[:, lanes].astype(jnp.float32) * LOG2E
-        start_row, pos_row = start[:, lanes], pos[:, lanes]
-        starts_ref[j] = jnp.broadcast_to(start_row, (8, BLOCK))
+
+
+def own_kernel(heads, info, starts_ref, kv_ref, qs_ref, dos_ref, rows_ref, dq_ref, dkv_ref):
+    tokens = kv_ref.shape[0]
+    feature = heads * HEAD_DIM
+    base = info[0] * tokens
+    dkv_ref[...] = jnp.zeros_like(dkv_ref)
+    for j in range(tokens // BLOCK):
+        rows = pl.ds(j * BLOCK, BLOCK)
         keys = slice(0, (j + 1) * BLOCK)
         queries = pl.ds(j * feature, feature)
+        pos_row = base + j * BLOCK + lax.broadcasted_iota(jnp.int32, (1, BLOCK), 1)
         key_pos = base + lax.broadcasted_iota(jnp.int32, ((j + 1) * BLOCK, BLOCK), 0)
-        allowed = (key_pos >= start_row) & (key_pos <= pos_row)
+        allowed = (key_pos >= starts_ref[j, 0:1, :]) & (key_pos <= pos_row)
         dq_t, dk, dv = tile_grads(kv_ref[keys, 0:HEAD_DIM], kv_ref[keys, HEAD_DIM : 2 * HEAD_DIM],
                                   qs_ref[queries, :], dos_ref[queries, :], rows_ref.at[j], allowed, heads)
         dq_ref[rows, :] = dq_t
-        mine = pl.ds(tokens, (j + 1) * BLOCK)
-        dkv_ref[mine, 0:HEAD_DIM] += dk
-        dkv_ref[mine, HEAD_DIM : 2 * HEAD_DIM] += dv
-
-        @pl.when(first_starts[j] < base)
-        def _(j=j, rows=rows, queries=queries, start_row=start_row):
-            key_pos = base - tokens + lax.broadcasted_iota(jnp.int32, (tokens, BLOCK), 0)
-            dq_t, dk, dv = tile_grads(kv1_ref[:, 0:HEAD_DIM], kv1_ref[:, HEAD_DIM : 2 * HEAD_DIM],
-                                      qs_ref[queries, :], dos_ref[queries, :], rows_ref.at[j],
-                                      key_pos >= start_row, heads)
-            dq_ref[rows, :] += dq_t
-            dkv_ref[pl.ds(0, tokens), 0:HEAD_DIM] += dk
-            dkv_ref[pl.ds(0, tokens), HEAD_DIM : 2 * HEAD_DIM] += dv
+        dkv_ref[keys, 0:HEAD_DIM] += dk
+        dkv_ref[keys, HEAD_DIM : 2 * HEAD_DIM] += dv
 
 
 def block_rest(i, heads, info, starts_ref, kv_ref, qs_ref, dos_ref, rows_ref, dqa_ref, dkv_ref, dq_ref, out_ref, row=0):
@@ -168,7 +162,7 @@
     blocks = tokens // BLOCK
     base = (info[0] - BACK) * tokens
     block = jnp.clip(info[2 + i], 0, blocks - 1)
-    first = jnp.clip(lax.div(info[5 + i] - base, tokens), 0, BACK - 1)
+    first = jnp.clip(lax.div(info[5 + i] - base, tokens), 0, BACK)
     queries = pl.ds(pl.multiple_of(block * feature, feature), feature)
     dq_ref[...] = dqa_ref[pl.ds(pl.multiple_of(block * BLOCK, BLOCK), BLOCK), :]
     start_row = starts_ref[block, 0:1, :]
@@ -184,18 +178,24 @@
         dkv_ref[keys, HEAD_DIM : 2 * HEAD_DIM] += dv
         return carry
 
-    lax.fori_loop(first, BACK - 1, step, 0)
+    lax.fori_loop(first, BACK, step, 0)
     for h in range(heads):
         cols = pl.ds(h * HEAD_DIM, HEAD_DIM)
         out_ref[pl.ds(row, BLOCK), cols] = (dq_ref[:, cols].T * SCALE).astype(jnp.bfloat16)
 
 
-def first_kernel(heads, info, starts_ref, kv2_ref, kv3_ref, qs_ref, dos_ref, rows_ref, dqa_ref,
+def first_kernel(heads, info, starts_ref, mate_ref, chip_ref, far_ref, qs_ref, dos_ref, rows_ref, dqa_ref,
                  out_ref, kv_ref, dkv_ref, dq_ref):
-    tokens = kv3_ref.shape[0]
+    tokens = chip_ref.shape[0]
     dkv_ref[...] = jnp.zeros_like(dkv_ref)
-    for n, ref in enumerate((kv3_ref, kv2_ref)):
-        kv_ref[pl.ds(n * tokens, tokens), :] = ref[...]
+    kv_ref[pl.ds(tokens, tokens), :] = chip_ref[...]
+    odd = lax.rem(info[0], 2)
+    for parity, (third_back, one_back) in enumerate(((far_ref, mate_ref), (mate_ref, far_ref))):
+        @pl.when(odd == parity)
+        def _(third_back=third_back, one_back=one_back):
+            kv_ref[pl.ds(0, tokens), :] = third_back[...]
+            kv_ref[pl.ds(2 * tokens, tokens), :] = one_back[...]
+
     for i in range(2):
         block_rest(i, heads, info, starts_ref, kv_ref, qs_ref, dos_ref, rows_ref, dqa_ref, dkv_ref, dq_ref, out_ref,
                    i * BLOCK)
@@ -203,7 +203,7 @@
 
 def rest_kernel(heads, info, starts_ref, kv_ref, qs_ref, dos_ref, rows_ref, dqa_ref, dkva_ref, dkvb_ref,
                 third_ref, send_ref, far_ref, own_ref, dq_ref, dkv_ref):
-    tokens = dkva_ref.shape[0] // 2
+    tokens = dkva_ref.shape[0]
     dkv_ref[...] = dkvb_ref[...]
     block_rest(2, heads, info, starts_ref, kv_ref, qs_ref, dos_ref, rows_ref, dqa_ref, dkv_ref, dq_ref, third_ref)
 
@@ -212,7 +212,7 @@
     left = lax.broadcasted_iota(jnp.int32, (tokens, HEAD_DIM), 1) < half
     for n in range(BACK + 1):
         rows = pl.ds(n * tokens, tokens)
-        ref, first = (dkv_ref, n * tokens) if n < BACK - 1 else (dkva_ref, (n - BACK + 1) * tokens)
+        ref, first = (dkv_ref, n * tokens) if n < BACK else (dkva_ref, 0)
         dk = ref[pl.ds(first, tokens), 0:HEAD_DIM] * SCALE
         dv = ref[pl.ds(first, tokens), HEAD_DIM : 2 * HEAD_DIM]
         low = jnp.where(left, dk, pltpu.roll(dv, half, 1))
@@ -225,33 +225,52 @@
             own_ref[...] = kept
 
 
-def place(info, first, pair, single, out_ref, sems, act):
-    arrays = (pair.at[pl.ds(0, BLOCK), :], pair.at[pl.ds(BLOCK, BLOCK), :], single)
+def place(info, arrays, out_ref, sems, act):
     for s in range(3):
-        for number, array in enumerate(arrays):
-            @pl.when(info[8 + s] == first + number)
+        for number, array in arrays:
+            @pl.when(info[8 + s] == number)
             def _(array=array, s=s):
                 getattr(pltpu.make_async_copy(array, out_ref.at[pl.ds(s * BLOCK, BLOCK), :], sems.at[s]), act)()
 
 
+def both_blocks(first, pair):
+    return [(first, pair.at[pl.ds(0, BLOCK), :]), (first + 1, pair.at[pl.ds(BLOCK, BLOCK), :])]
+
+
 def keep_kernel(info, mine12, mine3, out_ref, sems):
-    place(info, 0, mine12, mine3, out_ref, sems, "start")
-    place(info, 0, mine12, mine3, out_ref, sems, "wait")
-
-
-def finish_kernel(info, theirs12, theirs3, own_ref, mate_ref, r2_ref, r3_ref, placed_ref,
-                  out_ref, key_ref, value_ref, sems):
-    place(info, 3, theirs12, theirs3, out_ref, sems, "start")
+    arrays = both_blocks(0, mine12) + [(2, mine3)]
+    place(info, arrays, out_ref, sems, "start")
+    place(info, arrays, out_ref, sems, "wait")
+
+
+def finish_kernel(info, theirs12, theirs3_hbm, own_ref, mate_hbm, r2_hbm, r3_hbm, placed_ref,
+                  out_ref, key_ref, value_ref, sems, theirs3, mate_ref, r2_ref, r3_ref):
+    tokens = own_ref.shape[0]
+    pairs = ((mate_hbm.at[pl.ds(tokens, tokens), :], mate_ref), (r2_hbm, r2_ref), (r3_hbm, r3_ref))
+    loads = [pltpu.make_async_copy(a, b, sems.at[3 + n]) for n, (a, b) in enumerate(pairs)]
+    for load in loads:
+        load.start()
+    place(info, both_blocks(3, theirs12), out_ref, sems, "start")
+    has_third = (info[8] == 5) | (info[9] == 5) | (info[10] == 5)
+
+    @pl.when(has_third)
+    def _():
+        load = pltpu.make_async_copy(theirs3_hbm, theirs3, sems.at[6])
+        load.start()
+        load.wait()
+        place(info, [(5, theirs3)], out_ref, sems, "start")
+
+    for load in loads:
+        load.wait()
     total = own_ref[...] + r2_ref[...].astype(jnp.float32) + r3_ref[...].astype(jnp.float32)
-    tokens = total.shape[0]
-    total = total + jnp.where(lax.rem(info[0], 2) == 0, mate_ref[tokens:, :].astype(jnp.float32), 0.0)
+    total = total + jnp.where(lax.rem(info[0], 2) == 0, mate_ref[...].astype(jnp.float32), 0.0)
     half = HEAD_DIM // 2
     for n in range(total.shape[0] // BLOCK):
         lanes = slice(n * BLOCK, (n + 1) * BLOCK)
         turned = total[lanes, :].T.astype(jnp.bfloat16)
         key_ref[:, lanes] = turned[:half]
         value_ref[:, lanes] = turned[half:]
-    place(info, 3, theirs12, theirs3, out_ref, sems, "wait")
+    place(info, both_blocks(3, theirs12) + [(5, theirs3)], out_ref, sems, "wait")
 
 
 def on_device(queries, key_states, value_states, attn_out, grad_out, log_norm, lengths, block_plan):
@@ -265,8 +284,8 @@
         lax.dynamic_slice_in_dim(key_states, kv_group * HEAD_DIM, HEAD_DIM, 1),
         lax.dynamic_slice_in_dim(value_states, kv_group * HEAD_DIM, HEAD_DIM, 1)], axis=1)
     devices = 2 * half_axis
-    kv1, kv2, kv3 = (shifted(own_kv, "seq", n) for n in (1, 2, 3))
-    later = (BACK - 1) * tokens
+    chip_kv = shifted(own_kv, "seq", 2)
+    later = BACK * tokens
     f32, bf16, i32 = jnp.float32, jnp.bfloat16, jnp.int32
     queries, attn_out, grad_out, log_norm, lengths, block_plan = (
         pltpu.with_memory_space_constraint(a, pltpu.HBM)
@@ -274,14 +293,14 @@
     smem = pl.BlockSpec(memory_space=pltpu.SMEM)
     vmem = pl.BlockSpec(memory_space=pltpu.VMEM)
     hbm = pl.BlockSpec(memory_space=pltpu.HBM)
+    anywhere = pl.BlockSpec(memory_space=pl.ANY)
     params = pltpu.CompilerParams(vmem_limit_bytes=VMEM_LIMIT)
-    own_dq, own_dkv, rows, starts, qs, dos, info, branch = pl.pallas_call(
-        functools.partial(own_kernel, heads, half_axis),
-        in_specs=[smem, smem, vmem, vmem, hbm, hbm, hbm, vmem],
-        out_specs=[vmem] * 6 + [smem] * 2,
-        out_shape=[pltpu.VMEM((tokens, feature), f32),
-                   pltpu.VMEM((2 * tokens, 2 * HEAD_DIM), f32),
-                   pltpu.VMEM((blocks, 16, BLOCK), f32),
+    cost = pl.CostEstimate(flops=1_000, bytes_accessed=1_000, transcendentals=0)
+    rows, starts, qs, dos, info, branch = pl.pallas_call(
+        functools.partial(prepare_kernel, heads, half_axis),
+        in_specs=[smem, smem, hbm, hbm, hbm, vmem],
+        out_specs=[vmem] * 4 + [smem] * 2,
+        out_shape=[pltpu.VMEM((blocks, 16, BLOCK), f32),
                    pltpu.VMEM((blocks, 8, BLOCK), i32),
                    pltpu.VMEM((blocks * feature, HEAD_DIM), bf16),
                    pltpu.VMEM((blocks * feature, HEAD_DIM), bf16),
@@ -289,14 +308,26 @@
                    jax.ShapeDtypeStruct((1,), i32)],
         scratch_shapes=[pltpu.VMEM((tokens, feature), bf16)] * 3 + [pltpu.SemaphoreType.DMA((blocks, 3))],
         compiler_params=params,
-        cost_estimate=pl.CostEstimate(flops=2_000_000_000, bytes_accessed=4_000_000, transcendentals=600_000),
+        cost_estimate=cost,
+        name="prepare",
+    )(lengths, block_plan, queries, attn_out, grad_out, log_norm)
+
+    early_kv, chip_kv, rows = lax.optimization_barrier((own_kv, chip_kv, rows))
+    far_kv = lax.ppermute(early_kv, "seq", [(i, i + 3 if i % 2 else i + 1) for i in range(devices) if i + 3 < devices or not i % 2])
+    mate_kv = swapped(chip_kv, "seq", 1)
+    own_dq, own_dkv = pl.pallas_call(
+        functools.partial(own_kernel, heads),
+        in_specs=[smem] + [vmem] * 5,
+        out_specs=[vmem] * 2,
+        out_shape=[pltpu.VMEM((tokens, feature), f32), pltpu.VMEM((tokens, 2 * HEAD_DIM), f32)],
+        compiler_params=params,
+        cost_estimate=cost,
         name="own_keys",
-    )(lengths, block_plan, own_kv, kv1, queries, attn_out, grad_out, log_norm)
-
-    cost = pl.CostEstimate(flops=1_000, bytes_accessed=1_000, transcendentals=0)
+    )(info, starts, own_kv, qs, dos, rows)
+
     dq12, kv, dkv = pl.pallas_call(
         functools.partial(first_kernel, heads),
-        in_specs=[smem] + [vmem] * 7,
+        in_specs=[smem] + [vmem] * 8,
         out_specs=[vmem] * 3,
         out_shape=[pltpu.VMEM((2 * BLOCK, feature), bf16),
                    pltpu.VMEM((later, 2 * HEAD_DIM), bf16),
@@ -305,7 +336,7 @@
         compiler_params=params,
         cost_estimate=cost,
         name="first_blocks",
-    )(info, starts, kv2, kv3, qs, dos, rows, own_dq)
+    )(info, starts, mate_kv, chip_kv, far_kv, qs, dos, rows, own_dq)
     theirs12 = swapped(dq12, "seq", half_axis)
 
     dq3, send, far, own = pl.pallas_call(
@@ -351,11 +382,12 @@
     )(info, dq12, dq3)
     query_grad, key_grad, value_grad = pl.pallas_call(
         finish_kernel,
-        in_specs=[smem] + [vmem] * 6 + [hbm],
+        in_specs=[smem, vmem, anywhere, vmem] + [anywhere] * 3 + [hbm],
         out_specs=[hbm, vmem, vmem],
         out_shape=[whole, grad_half, grad_half],
         input_output_aliases={7: 0},
-        scratch_shapes=copy_sems,
+        scratch_shapes=[pltpu.SemaphoreType.DMA((7,)), pltpu.VMEM((BLOCK, feature), bf16)]
+        + [pltpu.VMEM((tokens, HEAD_DIM), bf16)] * 3,
         compiler_params=params,
         name="place_blocks",
     )(info, theirs12, theirs3, own, mate, back2, back3, placed)

time: 81.1 us -> 83.7 us (1.032); the launches traced: 81.5 us -> 83.2 us
  starting transfers between devices: 39.3 us -> 40.9 us
    ppermute x4 -> x2, starting transfers between devices: 13.1 us -> 5.67 us  [shifted(): lax.ppermute(value, axis, [(i, i + steps) for i in range(first, last)])]
    ppermute x0 -> x1, starting transfers between devices: none -> 7.24 us  [on_device(): lax.ppermute(early_kv, 'seq', [(i, i + 3 if i % 2 else i + 1) for i in ra...]
    ppermute x3 -> x4, waiting for transfers between devices: 7.97 us -> 5.62 us  [swapped(): lax.ppermute(array, axis, [(i, i ^ apart) for i in range(lax.axis_size(ax...]
    pallas_call x1, Pallas kernels: 0.99 us -> 3 us  [on_device(): pl.pallas_call(functools.partial(first_kernel, heads), in_specs=[smem] +...]
    ppermute x3 -> x4, starting transfers between devices: 23.6 us -> 25.4 us  [swapped(): lax.ppermute(array, axis, [(i, i ^ apart) for i in range(lax.axis_size(ax...]
    pallas_call x2 -> x3, Pallas kernels: 9.45 us -> 7.97 us  [the longest x1 3.16 us: on_device(): pl.pallas_call(functools.partial(prepare_kernel, heads, half_axis), in_sp...]
    ppermute x1, waiting for transfers between devices: 17.7 us -> 18.9 us  [returns(): lax.ppermute(third, 'seq', [(i, i - 3) for i in range(4, devices, 2)])]
  transfers between devices with their start and end apart: 9 -> 9, of which waited for: 2 -> 3; matrix products, arithmetic and copies ran while one was open for 1% -> 1% of each run, Pallas kernels for 11% -> 10%
where the time goes in v5:
time: 83.7 us; the launch traced here: 83.2 us
  starting transfers between devices  40.9 us (49%)
  waiting for transfers between devices  25.1 us (30%)
  Pallas kernels  13.4 us (16%)
  between operations  1.58 us (2%)
  other arithmetic  1.11 us (1%)
  local copies, waits for them, and re-layouts  0.96 us (1%)
    ppermute x4, starting transfers between devices, swapped(): lax.ppermute(array, axis, [(i, i ^ apart) for i in range(lax.axis_size(ax...  25.4 us
    ppermute x1, waiting for transfers between devices, returns(): lax.ppermute(third, 'seq', [(i, i - 3) for i in range(4, devices, 2)])  18.9 us
    ppermute x1, starting transfers between devices, on_device(): lax.ppermute(early_kv, 'seq', [(i, i + 3 if i % 2 else i + 1) for i in ra...  7.24 us
    ppermute x2, starting transfers between devices, shifted(): lax.ppermute(value, axis, [(i, i + steps) for i in range(first, last)])  5.67 us
    ppermute x4, waiting for transfers between devices, swapped(): lax.ppermute(array, axis, [(i, i ^ apart) for i in range(lax.axis_size(ax...  5.62 us
    pallas_call x1, Pallas kernels, on_device(): pl.pallas_call(functools.partial(prepare_kernel, heads, half_axis), in_sp...  3.16 us
    pallas_call x1, Pallas kernels, on_device(): pl.pallas_call(functools.partial(first_kernel, heads), in_specs=[smem] +...  3 us
    pallas_call x1, Pallas kernels, on_device(): pl.pallas_call(finish_kernel, in_specs=[smem, vmem, anywhere, vmem] + [an...  2.45 us
  transfers between devices with their start and end apart: 9, of which 3 were waited for; matrix products, arithmetic and copies ran while one was open for 1% of the time, Pallas kernels for 10%

profile of v5, /device:TPU:1, one launch (start us, length us, event | category | flops | bytes accessed | tf_op | source)
XLA Modules:
  0.0 83.2 jit_solution(1309285397474728704)
XLA Ops:
  0.6 1.0 %constant_dynamic-slice_fusion = (bf16[384,128]{1,0:T(8,128)(2,1)S(1)}, bf16[384,128]{1,0:T(8,128)(2,1)S(1)}) fusion(bf16[384,1024]{1,0:T(8,128)(2,1)} %param.26, s32[]{:T(128)S(6)} %select_n.174, bf16[384,1024]{1,0:T(8,128)(2,1)} %param.25), kind=kLoop, calls=%fused_computation.161 | loop fusion | bytes 393220 | tf_op jit(solution)/shard_map/dynamic_slice | solution.py:285
  1.6 4.4 %collective-permute-start.79 = (bf16[384,256]{1,0:T(8,128)(2,1)S(1)}, bf16[384,256]{1,0:T(8,128)(2,1)S(1)}, u32[]{:S(2)}, u32[]{:S(2)}) collective-permute-start(bf16[384,256]{1,0:T(8,128)(2,1)S(1)} %pad_maximum_fusion.16.kv_ref), channel_id=1, source_target_pairs={{0,32},{16,48},{32,64},{48,80},{64,96},{80,112},{96,128},{112,144}... | collective-permute-start | bytes 589832 | tf_op jit(solution)/shard_map/ppermute | solution.py:22
  6.0 3.2 %prepare.1 = (f32[3,16,128]{2,1,0:T(8,128)S(1)}, s32[3,8,128]{2,1,0:T(8,128)S(1)}, bf16[2304,128]{1,0:T(8,128)(2,1)S(1)}, bf16[2304,128]{1,0:T(8,128)(2,1)S(1)}, s32[16]{0:T(128)S(1)}, /*index=5*/s32[1]{0:T(128)}) custom-call(s32[30]{0:T(128)} %lengths_ref.1, s32[96]{0:T(128)} %plan_ref.1, bf16[384,768]{1,0:T(8,128)(2,1)} %q_hbm.1, bf16[384,768]{1,0:T(8,128)(2,1)} %o_hbm.1, ...), custom_call_target="tpu_custom_call" | custom-call | flops 1000 | bytes 1000 | tf_op jit(solution)/shard_map/prepare/pallas_call | solution.py:299
  9.2 0.0 collective-permute-done.79.chip_ref
  9.2 7.2 %collective-permute-start.81 = (bf16[384,256]{1,0:T(8,128)(2,1)S(1)}, bf16[384,256]{1,0:T(8,128)(2,1)S(1)}, u32[]{:S(2)}, u32[]{:S(2)}) collective-permute-start(bf16[384,256]{1,0:T(8,128)(2,1)S(1)} %pad_maximum_fusion.16.kv_ref), channel_id=1, source_target_pairs={{0,16},{16,64},{32,48},{48,96},{64,80},{80,128},{96,112},{112,160}... | collective-permute-start | bytes 589832 | tf_op jit(solution)/shard_map/ppermute | solution.py:316
  16.5 1.9 %collective-permute-start.80 = (bf16[384,256]{1,0:T(8,128)(2,1)S(1)}, bf16[384,256]{1,0:T(8,128)(2,1)S(1)}, u32[]{:S(2)}, u32[]{:S(2)}) collective-permute-start(bf16[384,256]{1,0:T(8,128)(2,1)S(1)} %collective-permute-done.79.chip_ref), channel_id=1, source_target_pairs={{0,16},{16,0},{32,48},{48,32},{64,80},{80,64},{96,112},{112,96},{1... | collective-permute-start | bytes 589832 | tf_op jit(solution)/shard_map/ppermute | solution.py:26
  18.4 2.4 %own_keys.1 = (f32[384,768]{1,0:T(8,128)S(1)}, f32[384,256]{1,0:T(8,128)S(1)}) custom-call(s32[16]{0:T(128)S(1)} %get-tuple-element.221.info, s32[3,8,128]{2,1,0:T(8,128)S(1)} %get-tuple-element.222.starts_ref, bf16[384,256]{1,0:T(8,128)(2,1)S(1)} %pad_maximum_fusion.16.kv_ref, bf16[2304,128]{1,0:T(8,128)(2,1)S(1)} %get-tuple-element.226.qs_ref, ...), custom_call_target="tpu_custom_call" | custom-call | flops 1000 | bytes 1000 | tf_op jit(solution)/shard_map/own_keys/pallas_call | solution.py:318
  20.8 0.0 collective-permute-done.81.far_ref
  20.8 0.0 collective-permute-done.80.mate_ref
  20.8 3.0 %first_blocks.1 = (bf16[256,768]{1,0:T(8,128)(2,1)S(1)}, bf16[1152,256]{1,0:T(8,128)(2,1)S(1)}, f32[1152,256]{1,0:T(8,128)S(1)}) custom-call(s32[16]{0:T(128)S(1)} %get-tuple-element.221.info, s32[3,8,128]{2,1,0:T(8,128)S(1)} %get-tuple-element.222.starts_ref, bf16[384,256]{1,0:T(8,128)(2,1)S(1)} %collective-permute-done.80.mate_ref, ...), custom_call_target="tpu_custom_call" | custom-call | flops 1000 | bytes 1000 | tf_op jit(solution)/shard_map/first_blocks/pallas_call | solution.py:328
  23.8 13.8 %collective-permute-start.82 = (bf16[256,768]{1,0:T(8,128)(2,1)S(1)}, bf16[256,768]{1,0:T(8,128)(2,1)S(1)}, u32[]{:S(2)}, u32[]{:S(2)}) collective-permute-start(bf16[256,768]{1,0:T(8,128)(2,1)S(1)} %get-tuple-element.230.mine12), channel_id=1, source_target_pairs={{0,256},{16,272},{32,288},{48,304},{64,320},{80,336},{96,352},{112... | collective-permute-start | bytes 1179656 | tf_op jit(solution)/shard_map/ppermute | solution.py:26
  38.2 1.1 %last_block.1 = (bf16[128,768]{1,0:T(8,128)(2,1)S(1)}, bf16[1536,128]{1,0:T(8,128)(2,1)S(1)}, bf16[1152,128]{1,0:T(8,128)(2,1)S(1)}, f32[384,128]{1,0:T(8,128)S(1)}) custom-call(s32[16]{0:T(128)S(1)} %get-tuple-element.221.info, s32[3,8,128]{2,1,0:T(8,128)S(1)} %get-tuple-element.222.starts_ref, bf16[1152,256]{1,0:T(8,128)(2,1)S(1)} %get-tuple-element.232.kv_ref, ...), custom_call_target="tpu_custom_call" | custom-call | flops 1000 | bytes 1000 | tf_op jit(solution)/shard_map/last_block/pallas_call | solution.py:342
  39.3 1.3 %keep_blocks.1.placed_ref = bf16[384,768]{1,0:T(8,128)(2,1)} custom-call(s32[16]{0:T(128)S(1)} %get-tuple-element.221.info, bf16[256,768]{1,0:T(8,128)(2,1)S(1)} %get-tuple-element.230.mine12, bf16[128,768]{1,0:T(8,128)(2,1)S(1)} %get-tuple-element.238.mine3), custom_call_target="tpu_custom_call" | custom-call | tf_op jit(solution)/shard_map/keep_blocks/pallas_call | solution.py:374
  40.7 39.9 %conditional.1 = (bf16[128,768]{1,0:T(8,128)(2,1)}, f32[384,128]{1,0:T(8,128)S(1)}, bf16[768,128]{1,0:T(8,128)(2,1)}, bf16[384,128]{1,0:T(8,128)(2,1)}, bf16[384,128]{1,0:T(8,128)(2,1)}) conditional(s32[]{:T(128)} %bitcast, (bf16[1536,128]{1,0:T(8,128)(2,1)S(1)}, f32[384,128]{1,0:T(8,128)S(1)}, ...), branch_computations={%region_0.1_spmd, %region_1.2_spmd, %region_2.3_spmd, %region_3.4_... | conditional | flops 1327119 | bytes 7471495 | solution.py:369
  40.7 3.2 %collective-permute-start.40 = (bf16[1536,128]{1,0:T(8,128)(2,1)S(1)}, bf16[1536,128]{1,0:T(8,128)(2,1)S(1)}, u32[]{:S(2)}, u32[]{:S(2)}) collective-permute-start(bf16[1536,128]{1,0:T(8,128)(2,1)S(1)} %get-tuple-element.162), channel_id=1, source_target_pairs={{0,1},{1,0},{2,3},{3,2},{4,5},{5,4},{6,7},{7,6},{8,9},{9,8},{10,11... | collective-permute-start | bytes 1179656 | tf_op jit(solution)/shard_map/cond/branch_8_fun/ppermute | solution.py:26
  43.9 5.6 %collective-permute-done.40 = bf16[1536,128]{1,0:T(8,128)(2,1)S(1)} collective-permute-done((bf16[1536,128]{1,0:T(8,128)(2,1)S(1)}, bf16[1536,128]{1,0:T(8,128)(2,1)S(1)}, u32[]{:S(2)}, u32[]{:S(2)}) %collective-permute-start.40) | collective-permute-done | bytes 393248 | tf_op jit(solution)/shard_map/cond/branch_8_fun/ppermute | solution.py:26
  49.5 0.1 convert_element_type.400
  49.6 0.1 broadcast_select_fusion.8
  49.7 6.5 %collective-permute-start.41 = (bf16[768,128]{1,0:T(8,128)(2,1)S(1)}, bf16[768,128]{1,0:T(8,128)(2,1)}, u32[]{:S(2)}, u32[]{:S(2)}) collective-permute-start(bf16[768,128]{1,0:T(8,128)(2,1)S(1)} %pad_maximum_fusion.8), channel_id=1, source_target_pairs={{0,16},{16,0},{32,48},{48,32},{64,80},{80,64},{96,112},{112,96},{1... | collective-permute-start | bytes 589832 | tf_op jit(solution)/shard_map/cond/branch_8_fun/ppermute | solution.py:26
  56.2 1.3 %collective-permute-start.39 = (bf16[128,768]{1,0:T(8,128)(2,1)S(1)}, bf16[128,768]{1,0:T(8,128)(2,1)}, u32[]{:S(2)}, u32[]{:S(2)}) collective-permute-start(bf16[128,768]{1,0:T(8,128)(2,1)S(1)} %get-tuple-element.160), channel_id=1, source_target_pairs={{192,448},{208,464},{224,480},{240,496},{448,192},{464,208},{480,2... | collective-permute-start | bytes 589832 | tf_op jit(solution)/shard_map/cond/branch_8_fun/ppermute | solution.py:358
  57.5 1.3 %collective-permute-start.43 = (bf16[384,128]{1,0:T(8,128)(2,1)S(1)}, bf16[384,128]{1,0:T(8,128)(2,1)}, u32[]{:S(2)}, u32[]{:S(2)}) collective-permute-start(bf16[384,128]{1,0:T(8,128)(2,1)S(1)} %get-tuple-element.272), channel_id=1, source_target_pairs={{64,16},{96,48},{128,80},{160,112},{192,144},{224,176},{256,208},{... | collective-permute-start | bytes 294920 | tf_op jit(solution)/shard_map/cond/branch_8_fun/ppermute | solution.py:364
  58.8 0.0 collective-permute-done.41
  58.8 0.9 %add_convert_fusion.8 = (bf16[384,128]{1,0:T(8,128)(2,1)S(1)}, f32[384,128]{1,0:T(8,128)S(1)}) fusion(f32[1536,128]{1,0:T(8,128)S(1)} %convert_element_type.400, bf16[768,128]{1,0:T(8,128)(2,1)} %collective-permute-done.41, bf16[1152,128]{1,0:T(8,128)(2,1)S(1)} %get-tuple-element.163, f32[384,128]{1,0:T(8,128)S(1)} %get-tuple-element.161), kind=kLoop, calls=%fused_computation.88 | loop fusion | flops 393216 | bytes 1081344 | tf_op jit(solution)/shard_map/cond/branch_8_fun/convert_element_type | solution.py:365
  59.8 1.3 %collective-permute-start.42 = (bf16[384,128]{1,0:T(8,128)(2,1)S(1)}, bf16[384,128]{1,0:T(8,128)(2,1)}, u32[]{:S(2)}, u32[]{:S(2)}) collective-permute-start(bf16[384,128]{1,0:T(8,128)(2,1)S(1)} %get-tuple-element.311), channel_id=1, source_target_pairs={{32,0},{48,16},{64,32},{80,48},{96,64},{112,80},{128,96},{144,112}... | collective-permute-start | bytes 294920 | tf_op jit(solution)/shard_map/cond/branch_8_fun/ppermute | solution.py:22
  61.1 0.0 collective-permute-done.39
  61.1 18.9 %collective-permute-done.43 = bf16[384,128]{1,0:T(8,128)(2,1)} collective-permute-done((bf16[384,128]{1,0:T(8,128)(2,1)S(1)}, bf16[384,128]{1,0:T(8,128)(2,1)}, u32[]{:S(2)}, u32[]{:S(2)}) %collective-permute-start.43) | collective-permute-done | bytes 98336 | tf_op jit(solution)/shard_map/cond/branch_8_fun/ppermute | solution.py:364
  80.0 0.6 collective-permute-done.42
  80.6 0.0 collective-permute-done.82.theirs12
  80.6 2.5 %place_blocks.1 = (bf16[384,768]{1,0:T(8,128)(2,1)}, bf16[64,384]{1,0:T(8,128)(2,1)}, bf16[64,384]{1,0:T(8,128)(2,1)}) custom-call(s32[16]{0:T(128)S(1)} %get-tuple-element.221.info, bf16[256,768]{1,0:T(8,128)(2,1)S(1)} %collective-permute-done.82.theirs12, bf16[128,768]{1,0:T(8,128)(2,1)} %get-tuple-element.239.theirs3_hbm, ...), custom_call_target="tpu_custom_call", output_to_operand_aliasing={{0}: (7, {})} | custom-call | tf_op jit(solution)/shard_map/place_blocks/pallas_call | solution.py:383
  (2 shorter events, 0.0 us)
Async XLA Ops:
  1.6 7.6 %collective-permute-start.79 = (bf16[384,256]{1,0:T(8,128)(2,1)S(1)}, bf16[384,256]{1,0:T(8,128)(2,1)S(1)}, u32[]{:S(2)}, u32[]{:S(2)}) collective-permute-start(bf16[384,256]{1,0:T(8,128)(2,1)S(1)} %pad_maximum_fusion.16.kv_ref), channel_id=1, source_target_pairs={{0,32},{16,48},{32,64},{48,80},{64,96},{80,112},{96,128},{112,144}... | collective-permute-start | bytes 589832 | tf_op jit(solution)/shard_map/ppermute | solution.py:22
  9.2 11.5 %collective-permute-start.81 = (bf16[384,256]{1,0:T(8,128)(2,1)S(1)}, bf16[384,256]{1,0:T(8,128)(2,1)S(1)}, u32[]{:S(2)}, u32[]{:S(2)}) collective-permute-start(bf16[384,256]{1,0:T(8,128)(2,1)S(1)} %pad_maximum_fusion.16.kv_ref), channel_id=1, source_target_pairs={{0,16},{16,64},{32,48},{48,96},{64,80},{80,128},{96,112},{112,160}... | collective-permute-start | bytes 589832 | tf_op jit(solution)/shard_map/ppermute | solution.py:316
  16.5 4.3 %collective-permute-start.80 = (bf16[384,256]{1,0:T(8,128)(2,1)S(1)}, bf16[384,256]{1,0:T(8,128)(2,1)S(1)}, u32[]{:S(2)}, u32[]{:S(2)}) collective-permute-start(bf16[384,256]{1,0:T(8,128)(2,1)S(1)} %collective-permute-done.79.chip_ref), channel_id=1, source_target_pairs={{0,16},{16,0},{32,48},{48,32},{64,80},{80,64},{96,112},{112,96},{1... | collective-permute-start | bytes 589832 | tf_op jit(solution)/shard_map/ppermute | solution.py:26
  23.8 56.8 %collective-permute-start.82 = (bf16[256,768]{1,0:T(8,128)(2,1)S(1)}, bf16[256,768]{1,0:T(8,128)(2,1)S(1)}, u32[]{:S(2)}, u32[]{:S(2)}) collective-permute-start(bf16[256,768]{1,0:T(8,128)(2,1)S(1)} %get-tuple-element.230.mine12), channel_id=1, source_target_pairs={{0,256},{16,272},{32,288},{48,304},{64,320},{80,336},{96,352},{112... | collective-permute-start | bytes 1179656 | tf_op jit(solution)/shard_map/ppermute | solution.py:26
  40.7 8.8 %collective-permute-start.40 = (bf16[1536,128]{1,0:T(8,128)(2,1)S(1)}, bf16[1536,128]{1,0:T(8,128)(2,1)S(1)}, u32[]{:S(2)}, u32[]{:S(2)}) collective-permute-start(bf16[1536,128]{1,0:T(8,128)(2,1)S(1)} %get-tuple-element.162), channel_id=1, source_target_pairs={{0,1},{1,0},{2,3},{3,2},{4,5},{5,4},{6,7},{7,6},{8,9},{9,8},{10,11... | collective-permute-start | bytes 1179656 | tf_op jit(solution)/shard_map/cond/branch_8_fun/ppermute | solution.py:26
  49.7 9.1 %collective-permute-start.41 = (bf16[768,128]{1,0:T(8,128)(2,1)S(1)}, bf16[768,128]{1,0:T(8,128)(2,1)}, u32[]{:S(2)}, u32[]{:S(2)}) collective-permute-start(bf16[768,128]{1,0:T(8,128)(2,1)S(1)} %pad_maximum_fusion.8), channel_id=1, source_target_pairs={{0,16},{16,0},{32,48},{48,32},{64,80},{80,64},{96,112},{112,96},{1... | collective-permute-start | bytes 589832 | tf_op jit(solution)/shard_map/cond/branch_8_fun/ppermute | solution.py:26
  56.2 4.9 %collective-permute-start.39 = (bf16[128,768]{1,0:T(8,128)(2,1)S(1)}, bf16[128,768]{1,0:T(8,128)(2,1)}, u32[]{:S(2)}, u32[]{:S(2)}) collective-permute-start(bf16[128,768]{1,0:T(8,128)(2,1)S(1)} %get-tuple-element.160), channel_id=1, source_target_pairs={{192,448},{208,464},{224,480},{240,496},{448,192},{464,208},{480,2... | collective-permute-start | bytes 589832 | tf_op jit(solution)/shard_map/cond/branch_8_fun/ppermute | solution.py:358
  57.5 22.4 %collective-permute-start.43 = (bf16[384,128]{1,0:T(8,128)(2,1)S(1)}, bf16[384,128]{1,0:T(8,128)(2,1)}, u32[]{:S(2)}, u32[]{:S(2)}) collective-permute-start(bf16[384,128]{1,0:T(8,128)(2,1)S(1)} %get-tuple-element.272), channel_id=1, source_target_pairs={{64,16},{96,48},{128,80},{160,112},{192,144},{224,176},{256,208},{... | collective-permute-start | bytes 294920 | tf_op jit(solution)/shard_map/cond/branch_8_fun/ppermute | solution.py:364
  59.8 20.8 %collective-permute-start.42 = (bf16[384,128]{1,0:T(8,128)(2,1)S(1)}, bf16[384,128]{1,0:T(8,128)(2,1)}, u32[]{:S(2)}, u32[]{:S(2)}) collective-permute-start(bf16[384,128]{1,0:T(8,128)(2,1)S(1)} %get-tuple-element.311), channel_id=1, source_target_pairs={{32,0},{48,16},{64,32},{80,48},{96,64},{112,80},{128,96},{144,112}... | collective-permute-start | bytes 294920 | tf_op jit(solution)/shard_map/cond/branch_8_fun/ppermute | solution.py:22

commit v6 on v5

--- a/solution.py
+++ b/solution.py
@@ -243,10 +243,9 @@
     place(info, arrays, out_ref, sems, "wait")
 
 
-def finish_kernel(info, theirs12, theirs3_hbm, own_ref, mate_hbm, r2_hbm, r3_hbm, placed_ref,
-                  out_ref, key_ref, value_ref, sems, theirs3, mate_ref, r2_ref, r3_ref):
-    tokens = own_ref.shape[0]
-    pairs = ((mate_hbm.at[pl.ds(tokens, tokens), :], mate_ref), (r2_hbm, r2_ref), (r3_hbm, r3_ref))
+def finish_kernel(info, theirs12, theirs3_hbm, own_ref, r2_hbm, r3_hbm, placed_ref,
+                  out_ref, key_ref, value_ref, sems, theirs3, r2_ref, r3_ref):
+    pairs = ((r2_hbm, r2_ref), (r3_hbm, r3_ref))
     loads = [pltpu.make_async_copy(a, b, sems.at[3 + n]) for n, (a, b) in enumerate(pairs)]
     for load in loads:
         load.start()
@@ -263,7 +262,6 @@
     for load in loads:
         load.wait()
     total = own_ref[...] + r2_ref[...].astype(jnp.float32) + r3_ref[...].astype(jnp.float32)
-    total = total + jnp.where(lax.rem(info[0], 2) == 0, mate_ref[...].astype(jnp.float32), 0.0)
     half = HEAD_DIM // 2
     for n in range(total.shape[0] // BLOCK):
         lanes = slice(n * BLOCK, (n + 1) * BLOCK)
@@ -285,6 +283,7 @@
         lax.dynamic_slice_in_dim(value_states, kv_group * HEAD_DIM, HEAD_DIM, 1)], axis=1)
     devices = 2 * half_axis
     chip_kv = shifted(own_kv, "seq", 2)
+    far_kv = lax.ppermute(own_kv, "seq", [(i, i + 3 if i % 2 else i + 1) for i in range(devices) if i + 3 < devices or not i % 2])
     later = BACK * tokens
     f32, bf16, i32 = jnp.float32, jnp.bfloat16, jnp.int32
     queries, attn_out, grad_out, log_norm, lengths, block_plan = (
@@ -312,8 +311,7 @@
         name="prepare",
     )(lengths, block_plan, queries, attn_out, grad_out, log_norm)
 
-    early_kv, chip_kv, rows = lax.optimization_barrier((own_kv, chip_kv, rows))
-    far_kv = lax.ppermute(early_kv, "seq", [(i, i + 3 if i % 2 else i + 1) for i in range(devices) if i + 3 < devices or not i % 2])
+    chip_kv, rows = lax.optimization_barrier((chip_kv, rows))
     mate_kv = swapped(chip_kv, "seq", 1)
     own_dq, own_dkv = pl.pallas_call(
         functools.partial(own_kernel, heads),
@@ -356,17 +354,23 @@
     def returns(mask, dq3, send, far, own):
         pairs = [(i, i ^ half_axis) for i in range(2 * half_axis) if mask >> (i % half_axis * GROUPS // half_axis) & 1]
         theirs3 = lax.ppermute(dq3, "seq", pairs) if pairs else dq3
-        arrived = swapped(send, "head", 1).astype(f32)
-        third, second, first = ((far[n * tokens : (n + 1) * tokens].astype(f32)
-                                 + arrived[n * tokens : (n + 1) * tokens]).astype(bf16) for n in range(BACK))
         odd = lax.axis_index("seq") % 2 == 1
-        mate = swapped(jnp.concatenate([jnp.where(odd, third, first), first], axis=0), "seq", 1)
-        back3 = lax.ppermute(third, "seq", [(i, i - 3) for i in range(4, devices, 2)])
-        back2 = shifted((second.astype(f32) + mate[:tokens].astype(f32)).astype(bf16), "seq", -2)
-        return (theirs3, own + arrived[window:], mate, back2, back3)
+        halves = jnp.concatenate([send[:window], far], axis=1)
+        third, second, first = (halves[n * tokens : (n + 1) * tokens] for n in range(BACK))
+        mate = swapped(jnp.concatenate([jnp.where(odd, third, first), first], axis=0), "seq", 1).astype(f32)
+        second = second.astype(f32) + mate[:tokens]
+        mine = jnp.where(odd, 0.0, mate[tokens:])
+        own = own + mine[:, HEAD_DIM:]
+        sent = send[window:].astype(f32) + mine[:, :HEAD_DIM]
+        arrived = swapped(jnp.concatenate([second[:, :HEAD_DIM].astype(bf16), sent.astype(bf16), send[:tokens]], axis=0),
+                          "head", 1).astype(f32)
+        back3 = lax.ppermute((far[:tokens].astype(f32) + arrived[2 * tokens :]).astype(bf16), "seq",
+                             [(i, i - 3) for i in range(4, devices, 2)])
+        back2 = shifted((second[:, HEAD_DIM:] + arrived[:tokens]).astype(bf16), "seq", -2)
+        return (theirs3, own + arrived[tokens : 2 * tokens], back2, back3)
 
     branches = [functools.partial(returns, mask) for mask in range(1 << GROUPS)]
-    theirs3, own, mate, back2, back3 = lax.switch(branch.reshape(()), branches, dq3, send, far, own)
+    theirs3, own, back2, back3 = lax.switch(branch.reshape(()), branches, dq3, send, far, own)
 
     grad_half = jax.ShapeDtypeStruct((HEAD_DIM // 2, tokens), bf16)
     whole = jax.ShapeDtypeStruct((tokens, feature), bf16)
@@ -382,15 +386,15 @@
     )(info, dq12, dq3)
     query_grad, key_grad, value_grad = pl.pallas_call(
         finish_kernel,
-        in_specs=[smem, vmem, anywhere, vmem] + [anywhere] * 3 + [hbm],
+        in_specs=[smem, vmem, anywhere, vmem] + [anywhere] * 2 + [hbm],
         out_specs=[hbm, vmem, vmem],
         out_shape=[whole, grad_half, grad_half],
-        input_output_aliases={7: 0},
+        input_output_aliases={6: 0},
         scratch_shapes=[pltpu.SemaphoreType.DMA((7,)), pltpu.VMEM((BLOCK, feature), bf16)]
-        + [pltpu.VMEM((tokens, HEAD_DIM), bf16)] * 3,
+        + [pltpu.VMEM((tokens, HEAD_DIM), bf16)] * 2,
         compiler_params=params,
         name="place_blocks",
-    )(info, theirs12, theirs3, own, mate, back2, back3, placed)
+    )(info, theirs12, theirs3, own, back2, back3, placed)
     return query_grad, key_grad.T, value_grad.T
 
 

time: 83.7 us -> 77.4 us (0.925)
  starting transfers between devices: 40.9 us -> 34.5 us
  Pallas kernels: 13.4 us -> 12.4 us
    ppermute x4, starting transfers between devices: 25.4 us -> 21.8 us  [swapped(): lax.ppermute(array, axis, [(i, i ^ apart) for i in range(lax.axis_size(ax...]
    ppermute x4, waiting for transfers between devices: 5.62 us -> 8.55 us  [swapped(): lax.ppermute(array, axis, [(i, i ^ apart) for i in range(lax.axis_size(ax...]
    ppermute x3 -> x2, starting transfers between devices: 9.87 us -> 7.02 us  [the longest x1 5.73 us: on_device(): lax.ppermute(own_kv, 'seq', [(i, i + 3 if i % 2 else i + 1) for i in rang...]
    ppermute x3 -> x2, waiting for transfers between devices: 18.9 us -> 17.1 us  [the longest x1 17.1 us: returns(): lax.ppermute((far[:tokens].astype(f32) + arrived[2 * tokens:]).astype(bf1...]
    pallas_call x1, Pallas kernels: 3 us -> 2.03 us  [on_device(): pl.pallas_call(functools.partial(first_kernel, heads), in_specs=[smem] +...]
  transfers between devices with their start and end apart: 9 -> 8, of which waited for: 3 -> 3; matrix products, arithmetic and copies ran while one was open for 1% -> 1% of each run, Pallas kernels for 10% -> 11%
where the time goes in v6:
time: 77.4 us; the launch traced here: 76.3 us
  starting transfers between devices  34.5 us (45%)
  waiting for transfers between devices  25.7 us (33%)
  Pallas kernels  12.4 us (16%)
  local copies, waits for them, and re-layouts  1.69 us (2%)
  between operations  1.56 us (2%)
    ppermute x4, starting transfers between devices, swapped(): lax.ppermute(array, axis, [(i, i ^ apart) for i in range(lax.axis_size(ax...  21.8 us
    ppermute x1, waiting for transfers between devices, returns(): lax.ppermute((far[:tokens].astype(f32) + arrived[2 * tokens:]).astype(bf1...  17.1 us
    ppermute x4, waiting for transfers between devices, swapped(): lax.ppermute(array, axis, [(i, i ^ apart) for i in range(lax.axis_size(ax...  8.55 us
    ppermute x1, starting transfers between devices, on_device(): lax.ppermute(own_kv, 'seq', [(i, i + 3 if i % 2 else i + 1) for i in rang...  5.73 us
    ppermute x2, starting transfers between devices, shifted(): lax.ppermute(value, axis, [(i, i + steps) for i in range(first, last)])  5.67 us
    pallas_call x1, Pallas kernels, on_device(): pl.pallas_call(functools.partial(prepare_kernel, heads, half_axis), in_sp...  3.16 us
    pallas_call x1, Pallas kernels, on_device(): pl.pallas_call(functools.partial(own_kernel, heads), in_specs=[smem] + [v...  2.36 us
    pallas_call x1, Pallas kernels, on_device(): pl.pallas_call(finish_kernel, in_specs=[smem, vmem, anywhere, vmem] + [an...  2.32 us
  transfers between devices with their start and end apart: 8, of which 3 were waited for; matrix products, arithmetic and copies ran while one was open for 1% of the time, Pallas kernels for 11%

profile of v6, /device:TPU:1, one launch (start us, length us, event | category | flops | bytes accessed | tf_op | source)
XLA Modules:
  0.0 76.3 jit_solution(3853667371758810847)
XLA Ops:
  0.6 1.0 %constant_dynamic-slice_fusion = (bf16[384,128]{1,0:T(8,128)(2,1)S(1)}, bf16[384,128]{1,0:T(8,128)(2,1)S(1)}) fusion(bf16[384,1024]{1,0:T(8,128)(2,1)} %param.26, s32[]{:T(128)S(6)} %select_n.240, bf16[384,1024]{1,0:T(8,128)(2,1)} %param.25), kind=kLoop, calls=%fused_computation.337 | loop fusion | bytes 393220 | tf_op jit(solution)/shard_map/dynamic_slice | solution.py:283
  1.6 4.4 %collective-permute-start.79 = (bf16[384,256]{1,0:T(8,128)(2,1)S(1)}, bf16[384,256]{1,0:T(8,128)(2,1)S(1)}, u32[]{:S(2)}, u32[]{:S(2)}) collective-permute-start(bf16[384,256]{1,0:T(8,128)(2,1)S(1)} %pad_maximum_fusion.48.kv_ref), channel_id=1, source_target_pairs={{0,32},{16,48},{32,64},{48,80},{64,96},{80,112},{96,128},{112,144}... | collective-permute-start | bytes 589832 | tf_op jit(solution)/shard_map/ppermute | solution.py:22
  6.0 5.7 %collective-permute-start.81 = (bf16[384,256]{1,0:T(8,128)(2,1)S(1)}, bf16[384,256]{1,0:T(8,128)(2,1)S(1)}, u32[]{:S(2)}, u32[]{:S(2)}) collective-permute-start(bf16[384,256]{1,0:T(8,128)(2,1)S(1)} %pad_maximum_fusion.48.kv_ref), channel_id=1, source_target_pairs={{0,16},{16,64},{32,48},{48,96},{64,80},{80,128},{96,112},{112,160}... | collective-permute-start | bytes 589832 | tf_op jit(solution)/shard_map/ppermute | solution.py:286
  11.8 3.2 %prepare.1 = (f32[3,16,128]{2,1,0:T(8,128)S(1)}, s32[3,8,128]{2,1,0:T(8,128)S(1)}, bf16[2304,128]{1,0:T(8,128)(2,1)S(1)}, bf16[2304,128]{1,0:T(8,128)(2,1)S(1)}, s32[16]{0:T(128)S(1)}, /*index=5*/s32[1]{0:T(128)}) custom-call(s32[30]{0:T(128)} %lengths_ref.1, s32[96]{0:T(128)} %plan_ref.1, bf16[384,768]{1,0:T(8,128)(2,1)} %q_hbm.1, bf16[384,768]{1,0:T(8,128)(2,1)} %o_hbm.1, ...), custom_call_target="tpu_custom_call" | custom-call | flops 1000 | bytes 1000 | tf_op jit(solution)/shard_map/prepare/pallas_call | solution.py:298
  14.9 0.0 collective-permute-done.79.chip_ref
  15.0 1.9 %collective-permute-start.80 = (bf16[384,256]{1,0:T(8,128)(2,1)S(1)}, bf16[384,256]{1,0:T(8,128)(2,1)S(1)}, u32[]{:S(2)}, u32[]{:S(2)}) collective-permute-start(bf16[384,256]{1,0:T(8,128)(2,1)S(1)} %collective-permute-done.79.chip_ref), channel_id=1, source_target_pairs={{0,16},{16,0},{32,48},{48,32},{64,80},{80,64},{96,112},{112,96},{1... | collective-permute-start | bytes 589832 | tf_op jit(solution)/shard_map/ppermute | solution.py:26
  16.9 2.4 %own_keys.1 = (f32[384,768]{1,0:T(8,128)S(1)}, f32[384,256]{1,0:T(8,128)S(1)}) custom-call(s32[16]{0:T(128)S(1)} %get-tuple-element.219.info, s32[3,8,128]{2,1,0:T(8,128)S(1)} %get-tuple-element.220.starts_ref, bf16[384,256]{1,0:T(8,128)(2,1)S(1)} %pad_maximum_fusion.48.kv_ref, bf16[2304,128]{1,0:T(8,128)(2,1)S(1)} %get-tuple-element.223.qs_ref, ...), custom_call_target="tpu_custom_call" | custom-call | flops 1000 | bytes 1000 | tf_op jit(solution)/shard_map/own_keys/pallas_call | solution.py:316
  19.2 0.0 collective-permute-done.81.far_ref
  19.3 0.0 collective-permute-done.80.mate_ref
  19.3 2.0 %first_blocks.1 = (bf16[256,768]{1,0:T(8,128)(2,1)S(1)}, bf16[1152,256]{1,0:T(8,128)(2,1)S(1)}, f32[1152,256]{1,0:T(8,128)S(1)}) custom-call(s32[16]{0:T(128)S(1)} %get-tuple-element.219.info, s32[3,8,128]{2,1,0:T(8,128)S(1)} %get-tuple-element.220.starts_ref, bf16[384,256]{1,0:T(8,128)(2,1)S(1)} %collective-permute-done.80.mate_ref, ...), custom_call_target="tpu_custom_call" | custom-call | flops 1000 | bytes 1000 | tf_op jit(solution)/shard_map/first_blocks/pallas_call | solution.py:326
  21.3 14.5 %collective-permute-start.82 = (bf16[256,768]{1,0:T(8,128)(2,1)S(1)}, bf16[256,768]{1,0:T(8,128)(2,1)S(1)}, u32[]{:S(2)}, u32[]{:S(2)}) collective-permute-start(bf16[256,768]{1,0:T(8,128)(2,1)S(1)} %get-tuple-element.227.mine12), channel_id=1, source_target_pairs={{0,256},{16,272},{32,288},{48,304},{64,320},{80,336},{96,352},{112... | collective-permute-start | bytes 1179656 | tf_op jit(solution)/shard_map/ppermute | solution.py:26
  36.5 1.1 %last_block.1 = (bf16[128,768]{1,0:T(8,128)(2,1)S(1)}, bf16[1536,128]{1,0:T(8,128)(2,1)S(1)}, bf16[1152,128]{1,0:T(8,128)(2,1)S(1)}, f32[384,128]{1,0:T(8,128)S(1)}) custom-call(s32[16]{0:T(128)S(1)} %get-tuple-element.219.info, s32[3,8,128]{2,1,0:T(8,128)S(1)} %get-tuple-element.220.starts_ref, bf16[1152,256]{1,0:T(8,128)(2,1)S(1)} %get-tuple-element.229.kv_ref, ...), custom_call_target="tpu_custom_call" | custom-call | flops 1000 | bytes 1000 | tf_op jit(solution)/shard_map/last_block/pallas_call | solution.py:340
  37.6 1.4 %keep_blocks.1.placed_ref = bf16[384,768]{1,0:T(8,128)(2,1)} custom-call(s32[16]{0:T(128)S(1)} %get-tuple-element.219.info, bf16[256,768]{1,0:T(8,128)(2,1)S(1)} %get-tuple-element.227.mine12, bf16[128,768]{1,0:T(8,128)(2,1)S(1)} %get-tuple-element.235.mine3), custom_call_target="tpu_custom_call" | custom-call | tf_op jit(solution)/shard_map/keep_blocks/pallas_call | solution.py:378
  39.0 34.8 %conditional.1 = (bf16[128,768]{1,0:T(8,128)(2,1)}, f32[384,128]{1,0:T(8,128)S(1)}, bf16[384,128]{1,0:T(8,128)(2,1)}, bf16[384,128]{1,0:T(8,128)(2,1)}) conditional(s32[]{:T(128)} %bitcast, (bf16[1536,128]{1,0:T(8,128)(2,1)S(1)}, bf16[1152,128]{1,0:T(8,128)(2,1)S(1)}, f32[384,128]{1,0:T(8,128)S(1)}, ...), branch_computations={%region_0.1_spmd, %region_1.2_spmd, %region_2.3_spmd, %region_3.4_... | conditional | flops 3981327 | bytes 13959552 | solution.py:373
  39.1 0.1 fusion.2
  39.2 2.1 %collective-permute-start = (bf16[768,256]{1,0:T(8,128)(2,1)S(1)}, bf16[768,256]{1,0:T(8,128)(2,1)S(1)}, u32[]{:S(2)}, u32[]{:S(2)}) collective-permute-start(bf16[768,256]{1,0:T(8,128)(2,1)S(1)} %pad_maximum_fusion), channel_id=1, source_target_pairs={{0,16},{16,0},{32,48},{48,32},{64,80},{80,64},{96,112},{112,96},{1... | collective-permute-start | bytes 1179656 | tf_op jit(solution)/shard_map/cond/branch_0_fun/ppermute | solution.py:26
  41.3 1.5 %collective-permute-done = bf16[768,256]{1,0:T(8,128)(2,1)S(1)} collective-permute-done((bf16[768,256]{1,0:T(8,128)(2,1)S(1)}, bf16[768,256]{1,0:T(8,128)(2,1)S(1)}, u32[]{:S(2)}, u32[]{:S(2)}) %collective-permute-start) | collective-permute-done | bytes 393248 | tf_op jit(solution)/shard_map/cond/branch_0_fun/ppermute | solution.py:26
  42.8 0.1 convert_element_type.241
  42.9 0.1 slice_add_fusion
  43.0 3.2 %collective-permute-start.1 = (bf16[1152,128]{1,0:T(8,128)(2,1)S(1)}, bf16[1152,128]{1,0:T(8,128)(2,1)S(1)}, u32[]{:S(2)}, u32[]{:S(2)}) collective-permute-start(bf16[1152,128]{1,0:T(8,128)(2,1)S(1)} %pad_maximum_fusion.1), channel_id=1, source_target_pairs={{0,1},{1,0},{2,3},{3,2},{4,5},{5,4},{6,7},{7,6},{8,9},{9,8},{10,11... | collective-permute-start | bytes 884744 | tf_op jit(solution)/shard_map/cond/branch_0_fun/ppermute | solution.py:26
  46.2 7.1 %collective-permute-done.1 = bf16[1152,128]{1,0:T(8,128)(2,1)S(1)} collective-permute-done((bf16[1152,128]{1,0:T(8,128)(2,1)S(1)}, bf16[1152,128]{1,0:T(8,128)(2,1)S(1)}, u32[]{:S(2)}, u32[]{:S(2)}) %collective-permute-start.1) | collective-permute-done | bytes 294944 | tf_op jit(solution)/shard_map/cond/branch_0_fun/ppermute | solution.py:26
  53.4 0.1 fusion.3
  53.4 1.3 %collective-permute-start.3 = (bf16[384,128]{1,0:T(8,128)(2,1)S(1)}, bf16[384,128]{1,0:T(8,128)(2,1)}, u32[]{:S(2)}, u32[]{:S(2)}) collective-permute-start(bf16[384,128]{1,0:T(8,128)(2,1)S(1)} %get-tuple-element.277), channel_id=1, source_target_pairs={{64,16},{96,48},{128,80},{160,112},{192,144},{224,176},{256,208},{... | collective-permute-start | bytes 294920 | tf_op jit(solution)/shard_map/cond/branch_0_fun/ppermute | solution.py:367
  54.7 1.3 %collective-permute-start.2 = (bf16[384,128]{1,0:T(8,128)(2,1)S(1)}, bf16[384,128]{1,0:T(8,128)(2,1)}, u32[]{:S(2)}, u32[]{:S(2)}) collective-permute-start(bf16[384,128]{1,0:T(8,128)(2,1)S(1)} %get-tuple-element.278), channel_id=1, source_target_pairs={{32,0},{48,16},{64,32},{80,48},{96,64},{112,80},{128,96},{144,112}... | collective-permute-start | bytes 294920 | tf_op jit(solution)/shard_map/cond/branch_0_fun/ppermute | solution.py:22
  56.0 0.7 copy.12
  56.7 17.1 %collective-permute-done.3 = bf16[384,128]{1,0:T(8,128)(2,1)} collective-permute-done((bf16[384,128]{1,0:T(8,128)(2,1)S(1)}, bf16[384,128]{1,0:T(8,128)(2,1)}, u32[]{:S(2)}, u32[]{:S(2)}) %collective-permute-start.3) | collective-permute-done | bytes 98336 | tf_op jit(solution)/shard_map/cond/branch_0_fun/ppermute | solution.py:367
  73.8 0.0 collective-permute-done.2
  73.9 0.0 collective-permute-done.82.theirs12
  73.9 2.3 %place_blocks.1 = (bf16[384,768]{1,0:T(8,128)(2,1)}, bf16[64,384]{1,0:T(8,128)(2,1)}, bf16[64,384]{1,0:T(8,128)(2,1)}) custom-call(s32[16]{0:T(128)S(1)} %get-tuple-element.219.info, bf16[256,768]{1,0:T(8,128)(2,1)S(1)} %collective-permute-done.82.theirs12, bf16[128,768]{1,0:T(8,128)(2,1)} %get-tuple-element.236.theirs3_hbm, ...), custom_call_target="tpu_custom_call", output_to_operand_aliasing={{0}: (6, {})} | custom-call | tf_op jit(solution)/shard_map/place_blocks/pallas_call | solution.py:387
  (8 shorter events, 0.2 us)
Async XLA Ops:
  1.6 13.3 %collective-permute-start.79 = (bf16[384,256]{1,0:T(8,128)(2,1)S(1)}, bf16[384,256]{1,0:T(8,128)(2,1)S(1)}, u32[]{:S(2)}, u32[]{:S(2)}) collective-permute-start(bf16[384,256]{1,0:T(8,128)(2,1)S(1)} %pad_maximum_fusion.48.kv_ref), channel_id=1, source_target_pairs={{0,32},{16,48},{32,64},{48,80},{64,96},{80,112},{96,128},{112,144}... | collective-permute-start | bytes 589832 | tf_op jit(solution)/shard_map/ppermute | solution.py:22
  6.0 13.2 %collective-permute-start.81 = (bf16[384,256]{1,0:T(8,128)(2,1)S(1)}, bf16[384,256]{1,0:T(8,128)(2,1)S(1)}, u32[]{:S(2)}, u32[]{:S(2)}) collective-permute-start(bf16[384,256]{1,0:T(8,128)(2,1)S(1)} %pad_maximum_fusion.48.kv_ref), channel_id=1, source_target_pairs={{0,16},{16,64},{32,48},{48,96},{64,80},{80,128},{96,112},{112,160}... | collective-permute-start | bytes 589832 | tf_op jit(solution)/shard_map/ppermute | solution.py:286
  15.0 4.3 %collective-permute-start.80 = (bf16[384,256]{1,0:T(8,128)(2,1)S(1)}, bf16[384,256]{1,0:T(8,128)(2,1)S(1)}, u32[]{:S(2)}, u32[]{:S(2)}) collective-permute-start(bf16[384,256]{1,0:T(8,128)(2,1)S(1)} %collective-permute-done.79.chip_ref), channel_id=1, source_target_pairs={{0,16},{16,0},{32,48},{48,32},{64,80},{80,64},{96,112},{112,96},{1... | collective-permute-start | bytes 589832 | tf_op jit(solution)/shard_map/ppermute | solution.py:26
  21.3 52.5 %collective-permute-start.82 = (bf16[256,768]{1,0:T(8,128)(2,1)S(1)}, bf16[256,768]{1,0:T(8,128)(2,1)S(1)}, u32[]{:S(2)}, u32[]{:S(2)}) collective-permute-start(bf16[256,768]{1,0:T(8,128)(2,1)S(1)} %get-tuple-element.227.mine12), channel_id=1, source_target_pairs={{0,256},{16,272},{32,288},{48,304},{64,320},{80,336},{96,352},{112... | collective-permute-start | bytes 1179656 | tf_op jit(solution)/shard_map/ppermute | solution.py:26
  39.2 3.6 %collective-permute-start = (bf16[768,256]{1,0:T(8,128)(2,1)S(1)}, bf16[768,256]{1,0:T(8,128)(2,1)S(1)}, u32[]{:S(2)}, u32[]{:S(2)}) collective-permute-start(bf16[768,256]{1,0:T(8,128)(2,1)S(1)} %pad_maximum_fusion), channel_id=1, source_target_pairs={{0,16},{16,0},{32,48},{48,32},{64,80},{80,64},{96,112},{112,96},{1... | collective-permute-start | bytes 1179656 | tf_op jit(solution)/shard_map/cond/branch_0_fun/ppermute | solution.py:26
  43.0 10.3 %collective-permute-start.1 = (bf16[1152,128]{1,0:T(8,128)(2,1)S(1)}, bf16[1152,128]{1,0:T(8,128)(2,1)S(1)}, u32[]{:S(2)}, u32[]{:S(2)}) collective-permute-start(bf16[1152,128]{1,0:T(8,128)(2,1)S(1)} %pad_maximum_fusion.1), channel_id=1, source_target_pairs={{0,1},{1,0},{2,3},{3,2},{4,5},{5,4},{6,7},{7,6},{8,9},{9,8},{10,11... | collective-permute-start | bytes 884744 | tf_op jit(solution)/shard_map/cond/branch_0_fun/ppermute | solution.py:26
  53.4 20.4 %collective-permute-start.3 = (bf16[384,128]{1,0:T(8,128)(2,1)S(1)}, bf16[384,128]{1,0:T(8,128)(2,1)}, u32[]{:S(2)}, u32[]{:S(2)}) collective-permute-start(bf16[384,128]{1,0:T(8,128)(2,1)S(1)} %get-tuple-element.277), channel_id=1, source_target_pairs={{64,16},{96,48},{128,80},{160,112},{192,144},{224,176},{256,208},{... | collective-permute-start | bytes 294920 | tf_op jit(solution)/shard_map/cond/branch_0_fun/ppermute | solution.py:367
  54.7 19.1 %collective-permute-start.2 = (bf16[384,128]{1,0:T(8,128)(2,1)S(1)}, bf16[384,128]{1,0:T(8,128)(2,1)}, u32[]{:S(2)}, u32[]{:S(2)}) collective-permute-start(bf16[384,128]{1,0:T(8,128)(2,1)S(1)} %get-tuple-element.278), channel_id=1, source_target_pairs={{32,0},{48,16},{64,32},{80,48},{96,64},{112,80},{128,96},{144,112}... | collective-permute-start | bytes 294920 | tf_op jit(solution)/shard_map/cond/branch_0_fun/ppermute | solution.py:22

commit v7 on v6

--- a/solution.py
+++ b/solution.py
@@ -201,11 +201,25 @@
                    i * BLOCK)
 
 
+def place(info, arrays, out_ref, sems, act):
+    for s in range(3):
+        for number, array in arrays:
+            @pl.when(info[8 + s] == number)
+            def _(array=array, s=s):
+                getattr(pltpu.make_async_copy(array, out_ref.at[pl.ds(s * BLOCK, BLOCK), :], sems.at[s]), act)()
+
+
+def both_blocks(first, pair):
+    return [(first, pair.at[pl.ds(0, BLOCK), :]), (first + 1, pair.at[pl.ds(BLOCK, BLOCK), :])]
+
+
 def rest_kernel(heads, info, starts_ref, kv_ref, qs_ref, dos_ref, rows_ref, dqa_ref, dkva_ref, dkvb_ref,
-                third_ref, send_ref, far_ref, own_ref, dq_ref, dkv_ref):
+                mine12, third_ref, send_ref, far_ref, own_ref, placed_ref, dq_ref, dkv_ref, sems):
     tokens = dkva_ref.shape[0]
+    place(info, both_blocks(0, mine12), placed_ref, sems, "start")
     dkv_ref[...] = dkvb_ref[...]
     block_rest(2, heads, info, starts_ref, kv_ref, qs_ref, dos_ref, rows_ref, dqa_ref, dkv_ref, dq_ref, third_ref)
+    place(info, [(2, third_ref)], placed_ref, sems, "start")
 
     side = info[1]
     half = HEAD_DIM // 2
@@ -223,28 +237,11 @@
             far_ref[rows, :] = kept.astype(jnp.bfloat16)
         else:
             own_ref[...] = kept
-
-
-def place(info, arrays, out_ref, sems, act):
-    for s in range(3):
-        for number, array in arrays:
-            @pl.when(info[8 + s] == number)
-            def _(array=array, s=s):
-                getattr(pltpu.make_async_copy(array, out_ref.at[pl.ds(s * BLOCK, BLOCK), :], sems.at[s]), act)()
-
-
-def both_blocks(first, pair):
-    return [(first, pair.at[pl.ds(0, BLOCK), :]), (first + 1, pair.at[pl.ds(BLOCK, BLOCK), :])]
-
-
-def keep_kernel(info, mine12, mine3, out_ref, sems):
-    arrays = both_blocks(0, mine12) + [(2, mine3)]
-    place(info, arrays, out_ref, sems, "start")
-    place(info, arrays, out_ref, sems, "wait")
+    place(info, both_blocks(0, mine12) + [(2, third_ref)], placed_ref, sems, "wait")
 
 
 def finish_kernel(info, theirs12, theirs3_hbm, own_ref, r2_hbm, r3_hbm, placed_ref,
-                  out_ref, key_ref, value_ref, sems, theirs3, r2_ref, r3_ref):
+                  out_ref, key_hbm, value_hbm, sems, theirs3, r2_ref, r3_ref, key_ref, value_ref):
     pairs = ((r2_hbm, r2_ref), (r3_hbm, r3_ref))
     loads = [pltpu.make_async_copy(a, b, sems.at[3 + n]) for n, (a, b) in enumerate(pairs)]
     for load in loads:
@@ -268,7 +265,13 @@
         turned = total[lanes, :].T.astype(jnp.bfloat16)
         key_ref[:, lanes] = turned[:half]
         value_ref[:, lanes] = turned[half:]
+    stores = [pltpu.make_async_copy(a, b, sems.at[7 + n])
+              for n, (a, b) in enumerate(((key_ref, key_hbm), (value_ref, value_hbm)))]
+    for store in stores:
+        store.start()
     place(info, both_blocks(3, theirs12) + [(5, theirs3)], out_ref, sems, "wait")
+    for store in stores:
+        store.wait()
 
 
 def on_device(queries, key_states, value_states, attn_out, grad_out, log_norm, lengths, block_plan):
@@ -337,19 +340,20 @@
     )(info, starts, mate_kv, chip_kv, far_kv, qs, dos, rows, own_dq)
     theirs12 = swapped(dq12, "seq", half_axis)
 
-    dq3, send, far, own = pl.pallas_call(
+    dq3, send, far, own, placed = pl.pallas_call(
         functools.partial(rest_kernel, heads),
-        in_specs=[smem] + [vmem] * 8,
-        out_specs=[vmem] * 4,
+        in_specs=[smem] + [vmem] * 9,
+        out_specs=[vmem] * 4 + [hbm],
         out_shape=[pltpu.VMEM((BLOCK, feature), bf16),
                    pltpu.VMEM((window + tokens, HEAD_DIM), bf16),
                    pltpu.VMEM((window, HEAD_DIM), bf16),
-                   pltpu.VMEM((tokens, HEAD_DIM), f32)],
-        scratch_shapes=[pltpu.VMEM((BLOCK, feature), f32), pltpu.VMEM((later, 2 * HEAD_DIM), f32)],
+                   pltpu.VMEM((tokens, HEAD_DIM), f32),
+                   jax.ShapeDtypeStruct((tokens, feature), bf16)],
+        scratch_shapes=[pltpu.VMEM((BLOCK, feature), f32), pltpu.VMEM((later, 2 * HEAD_DIM), f32), pltpu.SemaphoreType.DMA((3,))],
         compiler_params=params,
         cost_estimate=cost,
         name="last_block",
-    )(info, starts, kv, qs, dos, rows, own_dq, own_dkv, dkv)
+    )(info, starts, kv, qs, dos, rows, own_dq, own_dkv, dkv, dq12)
 
     def returns(mask, dq3, send, far, own):
         pairs = [(i, i ^ half_axis) for i in range(2 * half_axis) if mask >> (i % half_axis * GROUPS // half_axis) & 1]
@@ -374,24 +378,14 @@
 
     grad_half = jax.ShapeDtypeStruct((HEAD_DIM // 2, tokens), bf16)
     whole = jax.ShapeDtypeStruct((tokens, feature), bf16)
-    copy_sems = [pltpu.SemaphoreType.DMA((3,))]
-    placed = pl.pallas_call(
-        keep_kernel,
-        in_specs=[smem, vmem, vmem],
-        out_specs=hbm,
-        out_shape=whole,
-        scratch_shapes=copy_sems,
-        compiler_params=params,
-        name="keep_blocks",
-    )(info, dq12, dq3)
     query_grad, key_grad, value_grad = pl.pallas_call(
         finish_kernel,
         in_specs=[smem, vmem, anywhere, vmem] + [anywhere] * 2 + [hbm],
-        out_specs=[hbm, vmem, vmem],
+        out_specs=[hbm, hbm, hbm],
         out_shape=[whole, grad_half, grad_half],
         input_output_aliases={6: 0},
-        scratch_shapes=[pltpu.SemaphoreType.DMA((7,)), pltpu.VMEM((BLOCK, feature), bf16)]
-        + [pltpu.VMEM((tokens, HEAD_DIM), bf16)] * 2,
+        scratch_shapes=[pltpu.SemaphoreType.DMA((9,)), pltpu.VMEM((BLOCK, feature), bf16)]
+        + [pltpu.VMEM((tokens, HEAD_DIM), bf16)] * 2 + [pltpu.VMEM((HEAD_DIM // 2, tokens), bf16)] * 2,
         compiler_params=params,
         name="place_blocks",
     )(info, theirs12, theirs3, own, back2, back3, placed)

time: 77.4 us -> 83.2 us (1.075)
  waiting for transfers between devices: 25.7 us -> 30.4 us
  Pallas kernels: 12.4 us -> 13.7 us
    ppermute x0 -> x1, waiting for transfers between devices: none -> 23.5 us  [returns(): theirs3 = lax.ppermute(dq3, 'seq', pairs) if pairs else dq3]
    ppermute x1, waiting for transfers between devices: 17.1 us -> 0.01 us  [returns(): lax.ppermute((far[:tokens].astype(f32) + arrived[2 * tokens:]).astype(bf1...]
    ppermute x0 -> x1, starting transfers between devices: none -> 1.92 us  [returns(): theirs3 = lax.ppermute(dq3, 'seq', pairs) if pairs else dq3]
    ppermute x4, waiting for transfers between devices: 8.55 us -> 6.9 us  [swapped(): lax.ppermute(array, axis, [(i, i ^ apart) for i in range(lax.axis_size(ax...]
    pallas_call x1, Pallas kernels: 1.12 us -> 2.73 us  [on_device(): pl.pallas_call(functools.partial(rest_kernel, heads), in_specs=[smem] + [...]
    pallas_call x1 -> x0, Pallas kernels: 1.38 us -> none  [on_device(): pl.pallas_call(keep_kernel, in_specs=[smem, vmem, vmem], out_specs=hbm, o...]
    ppermute x4, starting transfers between devices: 21.8 us -> 20.6 us  [swapped(): lax.ppermute(array, axis, [(i, i ^ apart) for i in range(lax.axis_size(ax...]
    pallas_call x1, Pallas kernels: 2.03 us -> 3.02 us  [on_device(): pl.pallas_call(functools.partial(first_kernel, heads), in_specs=[smem] +...]
  transfers between devices with their start and end apart: 8 -> 9, of which waited for: 3 -> 3; matrix products, arithmetic and copies ran while one was open for 1% -> 1% of each run, Pallas kernels for 11% -> 10%
where the time goes in v7:
time: 83.2 us; the launch traced here: 82.7 us
  starting transfers between devices  35.2 us (42%)
  waiting for transfers between devices  30.4 us (37%)
  Pallas kernels  13.7 us (16%)
  between operations  1.57 us (2%)
  local copies, waits for them, and re-layouts  1.02 us (1%)
    ppermute x1, waiting for transfers between devices, returns(): theirs3 = lax.ppermute(dq3, 'seq', pairs) if pairs else dq3  23.5 us
    ppermute x4, starting transfers between devices, swapped(): lax.ppermute(array, axis, [(i, i ^ apart) for i in range(lax.axis_size(ax...  20.6 us
    ppermute x4, waiting for transfers between devices, swapped(): lax.ppermute(array, axis, [(i, i ^ apart) for i in range(lax.axis_size(ax...  6.9 us
    ppermute x1, starting transfers between devices, on_device(): lax.ppermute(own_kv, 'seq', [(i, i + 3 if i % 2 else i + 1) for i in rang...  5.73 us
    ppermute x2, starting transfers between devices, shifted(): lax.ppermute(value, axis, [(i, i + steps) for i in range(first, last)])  5.67 us
    pallas_call x1, Pallas kernels, on_device(): pl.pallas_call(functools.partial(prepare_kernel, heads, half_axis), in_sp...  3.16 us
    pallas_call x1, Pallas kernels, on_device(): pl.pallas_call(functools.partial(first_kernel, heads), in_specs=[smem] +...  3.02 us
    pallas_call x1, Pallas kernels, on_device(): pl.pallas_call(functools.partial(rest_kernel, heads), in_specs=[smem] + [...  2.73 us
  transfers between devices with their start and end apart: 9, of which 3 were waited for; matrix products, arithmetic and copies ran while one was open for 1% of the time, Pallas kernels for 10%

profile of v7, /device:TPU:1, one launch (start us, length us, event | category | flops | bytes accessed | tf_op | source)
XLA Modules:
  0.0 82.7 jit_solution(16871555669912232936)
XLA Ops:
  0.6 1.0 %constant_dynamic-slice_fusion = (bf16[384,128]{1,0:T(8,128)(2,1)S(1)}, bf16[384,128]{1,0:T(8,128)(2,1)S(1)}) fusion(bf16[384,1024]{1,0:T(8,128)(2,1)} %param.26, s32[]{:T(128)S(6)} %select_n.240, bf16[384,1024]{1,0:T(8,128)(2,1)} %param.25), kind=kLoop, calls=%fused_computation.337 | loop fusion | bytes 393220 | tf_op jit(solution)/shard_map/dynamic_slice | solution.py:286
  1.6 4.4 %collective-permute-start.79 = (bf16[384,256]{1,0:T(8,128)(2,1)S(1)}, bf16[384,256]{1,0:T(8,128)(2,1)S(1)}, u32[]{:S(2)}, u32[]{:S(2)}) collective-permute-start(bf16[384,256]{1,0:T(8,128)(2,1)S(1)} %pad_maximum_fusion.48.kv_ref), channel_id=1, source_target_pairs={{0,32},{16,48},{32,64},{48,80},{64,96},{80,112},{96,128},{112,144}... | collective-permute-start | bytes 589832 | tf_op jit(solution)/shard_map/ppermute | solution.py:22
  6.0 5.7 %collective-permute-start.81 = (bf16[384,256]{1,0:T(8,128)(2,1)S(1)}, bf16[384,256]{1,0:T(8,128)(2,1)S(1)}, u32[]{:S(2)}, u32[]{:S(2)}) collective-permute-start(bf16[384,256]{1,0:T(8,128)(2,1)S(1)} %pad_maximum_fusion.48.kv_ref), channel_id=1, source_target_pairs={{0,16},{16,64},{32,48},{48,96},{64,80},{80,128},{96,112},{112,160}... | collective-permute-start | bytes 589832 | tf_op jit(solution)/shard_map/ppermute | solution.py:289
  11.8 3.2 %prepare.1 = (f32[3,16,128]{2,1,0:T(8,128)S(1)}, s32[3,8,128]{2,1,0:T(8,128)S(1)}, bf16[2304,128]{1,0:T(8,128)(2,1)S(1)}, bf16[2304,128]{1,0:T(8,128)(2,1)S(1)}, s32[16]{0:T(128)S(1)}, /*index=5*/s32[1]{0:T(128)}) custom-call(s32[30]{0:T(128)} %lengths_ref.1, s32[96]{0:T(128)} %plan_ref.1, bf16[384,768]{1,0:T(8,128)(2,1)} %q_hbm.1, bf16[384,768]{1,0:T(8,128)(2,1)} %o_hbm.1, ...), custom_call_target="tpu_custom_call" | custom-call | flops 1000 | bytes 1000 | tf_op jit(solution)/shard_map/prepare/pallas_call | solution.py:301
  14.9 0.0 collective-permute-done.79.chip_ref
  15.0 1.9 %collective-permute-start.80 = (bf16[384,256]{1,0:T(8,128)(2,1)S(1)}, bf16[384,256]{1,0:T(8,128)(2,1)S(1)}, u32[]{:S(2)}, u32[]{:S(2)}) collective-permute-start(bf16[384,256]{1,0:T(8,128)(2,1)S(1)} %collective-permute-done.79.chip_ref), channel_id=1, source_target_pairs={{0,16},{16,0},{32,48},{48,32},{64,80},{80,64},{96,112},{112,96},{1... | collective-permute-start | bytes 589832 | tf_op jit(solution)/shard_map/ppermute | solution.py:26
  16.9 2.4 %own_keys.1 = (f32[384,768]{1,0:T(8,128)S(1)}, f32[384,256]{1,0:T(8,128)S(1)}) custom-call(s32[16]{0:T(128)S(1)} %get-tuple-element.220.info, s32[3,8,128]{2,1,0:T(8,128)S(1)} %get-tuple-element.221.starts_ref, bf16[384,256]{1,0:T(8,128)(2,1)S(1)} %pad_maximum_fusion.48.kv_ref, bf16[2304,128]{1,0:T(8,128)(2,1)S(1)} %get-tuple-element.224.qs_ref, ...), custom_call_target="tpu_custom_call" | custom-call | flops 1000 | bytes 1000 | tf_op jit(solution)/shard_map/own_keys/pallas_call | solution.py:319
  19.2 0.0 collective-permute-done.81.far_ref
  19.3 0.0 collective-permute-done.80.mate_ref
  19.3 3.0 %first_blocks.1 = (bf16[256,768]{1,0:T(8,128)(2,1)S(1)}, bf16[1152,256]{1,0:T(8,128)(2,1)S(1)}, f32[1152,256]{1,0:T(8,128)S(1)}) custom-call(s32[16]{0:T(128)S(1)} %get-tuple-element.220.info, s32[3,8,128]{2,1,0:T(8,128)S(1)} %get-tuple-element.221.starts_ref, bf16[384,256]{1,0:T(8,128)(2,1)S(1)} %collective-permute-done.80.mate_ref, ...), custom_call_target="tpu_custom_call" | custom-call | flops 1000 | bytes 1000 | tf_op jit(solution)/shard_map/first_blocks/pallas_call | solution.py:329
  22.3 13.6 %collective-permute-start.82 = (bf16[256,768]{1,0:T(8,128)(2,1)S(1)}, bf16[256,768]{1,0:T(8,128)(2,1)S(1)}, u32[]{:S(2)}, u32[]{:S(2)}) collective-permute-start(bf16[256,768]{1,0:T(8,128)(2,1)S(1)} %get-tuple-element.228.mine12), channel_id=1, source_target_pairs={{0,256},{16,272},{32,288},{48,304},{64,320},{80,336},{96,352},{112... | collective-permute-start | bytes 1179656 | tf_op jit(solution)/shard_map/ppermute | solution.py:26
  36.5 2.7 %last_block.1 = (bf16[128,768]{1,0:T(8,128)(2,1)S(1)}, bf16[1536,128]{1,0:T(8,128)(2,1)S(1)}, bf16[1152,128]{1,0:T(8,128)(2,1)S(1)}, f32[384,128]{1,0:T(8,128)S(1)}, bf16[384,768]{1,0:T(8,128)(2,1)}) custom-call(s32[16]{0:T(128)S(1)} %get-tuple-element.220.info, s32[3,8,128]{2,1,0:T(8,128)S(1)} %get-tuple-element.221.starts_ref, ...), custom_call_target="tpu_custom_call" | custom-call | flops 1000 | bytes 1000 | tf_op jit(solution)/shard_map/last_block/pallas_call | solution.py:343
  39.2 40.8 %conditional.1 = (bf16[128,768]{1,0:T(8,128)(2,1)S(1)}, f32[384,128]{1,0:T(8,128)S(1)}, bf16[384,128]{1,0:T(8,128)(2,1)}, bf16[384,128]{1,0:T(8,128)(2,1)}) conditional(s32[]{:T(128)} %bitcast, (bf16[1536,128]{1,0:T(8,128)(2,1)S(1)}, bf16[1152,128]{1,0:T(8,128)(2,1)S(1)}, f32[384,128]{1,0:T(8,128)S(1)}, ...), branch_computations={%region_0.1_spmd, %region_1.2_spmd, %region_2.3_spmd, %region_3.4_... | conditional | flops 3981327 | bytes 14352768 | solution.py:377
  39.3 0.1 fusion.8
  39.4 1.9 %collective-permute-start.5 = (bf16[768,256]{1,0:T(8,128)(2,1)S(1)}, bf16[768,256]{1,0:T(8,128)(2,1)S(1)}, u32[]{:S(2)}, u32[]{:S(2)}) collective-permute-start(bf16[768,256]{1,0:T(8,128)(2,1)S(1)} %pad_maximum_fusion.3), channel_id=1, source_target_pairs={{0,16},{16,0},{32,48},{48,32},{64,80},{80,64},{96,112},{112,96},{1... | collective-permute-start | bytes 1179656 | tf_op jit(solution)/shard_map/cond/branch_1_fun/ppermute | solution.py:26
  41.4 1.7 %collective-permute-done.5 = bf16[768,256]{1,0:T(8,128)(2,1)S(1)} collective-permute-done((bf16[768,256]{1,0:T(8,128)(2,1)S(1)}, bf16[768,256]{1,0:T(8,128)(2,1)S(1)}, u32[]{:S(2)}, u32[]{:S(2)}) %collective-permute-start.5) | collective-permute-done | bytes 393248 | tf_op jit(solution)/shard_map/cond/branch_1_fun/ppermute | solution.py:26
  43.1 0.1 convert_element_type.271
  43.1 0.1 slice_add_fusion.6
  43.3 3.2 %collective-permute-start.6 = (bf16[1152,128]{1,0:T(8,128)(2,1)S(1)}, bf16[1152,128]{1,0:T(8,128)(2,1)S(1)}, u32[]{:S(2)}, u32[]{:S(2)}) collective-permute-start(bf16[1152,128]{1,0:T(8,128)(2,1)S(1)} %pad_maximum_fusion.4), channel_id=1, source_target_pairs={{0,1},{1,0},{2,3},{3,2},{4,5},{5,4},{6,7},{7,6},{8,9},{9,8},{10,11... | collective-permute-start | bytes 884744 | tf_op jit(solution)/shard_map/cond/branch_1_fun/ppermute | solution.py:26
  46.5 1.9 %collective-permute-start.4 = (bf16[128,768]{1,0:T(8,128)(2,1)S(1)}, bf16[128,768]{1,0:T(8,128)(2,1)S(1)}, u32[]{:S(2)}, u32[]{:S(2)}) collective-permute-start(bf16[128,768]{1,0:T(8,128)(2,1)S(1)} %get-tuple-element.132), channel_id=1, source_target_pairs={{0,256},{16,272},{32,288},{48,304},{256,0},{272,16},{288,32},{304,... | collective-permute-start | bytes 589832 | tf_op jit(solution)/shard_map/cond/branch_1_fun/ppermute | solution.py:360
  48.4 5.2 %collective-permute-done.6 = bf16[1152,128]{1,0:T(8,128)(2,1)S(1)} collective-permute-done((bf16[1152,128]{1,0:T(8,128)(2,1)S(1)}, bf16[1152,128]{1,0:T(8,128)(2,1)S(1)}, u32[]{:S(2)}, u32[]{:S(2)}) %collective-permute-start.6) | collective-permute-done | bytes 294944 | tf_op jit(solution)/shard_map/cond/branch_1_fun/ppermute | solution.py:26
  53.7 0.1 fusion.9
  53.8 1.3 %collective-permute-start.8 = (bf16[384,128]{1,0:T(8,128)(2,1)S(1)}, bf16[384,128]{1,0:T(8,128)(2,1)}, u32[]{:S(2)}, u32[]{:S(2)}) collective-permute-start(bf16[384,128]{1,0:T(8,128)(2,1)S(1)} %get-tuple-element.284), channel_id=1, source_target_pairs={{64,16},{96,48},{128,80},{160,112},{192,144},{224,176},{256,208},{... | collective-permute-start | bytes 294920 | tf_op jit(solution)/shard_map/cond/branch_1_fun/ppermute | solution.py:371
  55.1 1.3 %collective-permute-start.7 = (bf16[384,128]{1,0:T(8,128)(2,1)S(1)}, bf16[384,128]{1,0:T(8,128)(2,1)}, u32[]{:S(2)}, u32[]{:S(2)}) collective-permute-start(bf16[384,128]{1,0:T(8,128)(2,1)S(1)} %get-tuple-element.285), channel_id=1, source_target_pairs={{32,0},{48,16},{64,32},{80,48},{96,64},{112,80},{128,96},{144,112}... | collective-permute-start | bytes 294920 | tf_op jit(solution)/shard_map/cond/branch_1_fun/ppermute | solution.py:22
  56.4 23.5 %collective-permute-done.4 = bf16[128,768]{1,0:T(8,128)(2,1)S(1)} collective-permute-done((bf16[128,768]{1,0:T(8,128)(2,1)S(1)}, bf16[128,768]{1,0:T(8,128)(2,1)S(1)}, u32[]{:S(2)}, u32[]{:S(2)}) %collective-permute-start.4) | collective-permute-done | bytes 196640 | tf_op jit(solution)/shard_map/cond/branch_1_fun/ppermute | solution.py:360
  79.9 0.0 collective-permute-done.8
  79.9 0.0 collective-permute-done.7
  80.1 0.0 collective-permute-done.82.theirs12
  80.1 2.4 %place_blocks.1 = (bf16[384,768]{1,0:T(8,128)(2,1)}, bf16[64,384]{1,0:T(8,128)(2,1)}, bf16[64,384]{1,0:T(8,128)(2,1)}) custom-call(s32[16]{0:T(128)S(1)} %get-tuple-element.220.info, bf16[256,768]{1,0:T(8,128)(2,1)S(1)} %collective-permute-done.82.theirs12, bf16[128,768]{1,0:T(8,128)(2,1)S(1)} %get-tuple-element.237.theirs3_hbm, ...), custom_call_target="tpu_custom_call", output_to_operand_aliasing={{0}: (6, {})} | custom-call | tf_op jit(solution)/shard_map/place_blocks/pallas_call | solution.py:381
  (9 shorter events, 0.2 us)
Async XLA Ops:
  1.6 13.3 %collective-permute-start.79 = (bf16[384,256]{1,0:T(8,128)(2,1)S(1)}, bf16[384,256]{1,0:T(8,128)(2,1)S(1)}, u32[]{:S(2)}, u32[]{:S(2)}) collective-permute-start(bf16[384,256]{1,0:T(8,128)(2,1)S(1)} %pad_maximum_fusion.48.kv_ref), channel_id=1, source_target_pairs={{0,32},{16,48},{32,64},{48,80},{64,96},{80,112},{96,128},{112,144}... | collective-permute-start | bytes 589832 | tf_op jit(solution)/shard_map/ppermute | solution.py:22
  6.0 13.2 %collective-permute-start.81 = (bf16[384,256]{1,0:T(8,128)(2,1)S(1)}, bf16[384,256]{1,0:T(8,128)(2,1)S(1)}, u32[]{:S(2)}, u32[]{:S(2)}) collective-permute-start(bf16[384,256]{1,0:T(8,128)(2,1)S(1)} %pad_maximum_fusion.48.kv_ref), channel_id=1, source_target_pairs={{0,16},{16,64},{32,48},{48,96},{64,80},{80,128},{96,112},{112,160}... | collective-permute-start | bytes 589832 | tf_op jit(solution)/shard_map/ppermute | solution.py:289
  15.0 4.3 %collective-permute-start.80 = (bf16[384,256]{1,0:T(8,128)(2,1)S(1)}, bf16[384,256]{1,0:T(8,128)(2,1)S(1)}, u32[]{:S(2)}, u32[]{:S(2)}) collective-permute-start(bf16[384,256]{1,0:T(8,128)(2,1)S(1)} %collective-permute-done.79.chip_ref), channel_id=1, source_target_pairs={{0,16},{16,0},{32,48},{48,32},{64,80},{80,64},{96,112},{112,96},{1... | collective-permute-start | bytes 589832 | tf_op jit(solution)/shard_map/ppermute | solution.py:26
  22.3 57.8 %collective-permute-start.82 = (bf16[256,768]{1,0:T(8,128)(2,1)S(1)}, bf16[256,768]{1,0:T(8,128)(2,1)S(1)}, u32[]{:S(2)}, u32[]{:S(2)}) collective-permute-start(bf16[256,768]{1,0:T(8,128)(2,1)S(1)} %get-tuple-element.228.mine12), channel_id=1, source_target_pairs={{0,256},{16,272},{32,288},{48,304},{64,320},{80,336},{96,352},{112... | collective-permute-start | bytes 1179656 | tf_op jit(solution)/shard_map/ppermute | solution.py:26
  39.4 3.6 %collective-permute-start.5 = (bf16[768,256]{1,0:T(8,128)(2,1)S(1)}, bf16[768,256]{1,0:T(8,128)(2,1)S(1)}, u32[]{:S(2)}, u32[]{:S(2)}) collective-permute-start(bf16[768,256]{1,0:T(8,128)(2,1)S(1)} %pad_maximum_fusion.3), channel_id=1, source_target_pairs={{0,16},{16,0},{32,48},{48,32},{64,80},{80,64},{96,112},{112,96},{1... | collective-permute-start | bytes 1179656 | tf_op jit(solution)/shard_map/cond/branch_1_fun/ppermute | solution.py:26
  43.3 10.4 %collective-permute-start.6 = (bf16[1152,128]{1,0:T(8,128)(2,1)S(1)}, bf16[1152,128]{1,0:T(8,128)(2,1)S(1)}, u32[]{:S(2)}, u32[]{:S(2)}) collective-permute-start(bf16[1152,128]{1,0:T(8,128)(2,1)S(1)} %pad_maximum_fusion.4), channel_id=1, source_target_pairs={{0,1},{1,0},{2,3},{3,2},{4,5},{5,4},{6,7},{7,6},{8,9},{9,8},{10,11... | collective-permute-start | bytes 884744 | tf_op jit(solution)/shard_map/cond/branch_1_fun/ppermute | solution.py:26
  46.5 33.4 %collective-permute-start.4 = (bf16[128,768]{1,0:T(8,128)(2,1)S(1)}, bf16[128,768]{1,0:T(8,128)(2,1)S(1)}, u32[]{:S(2)}, u32[]{:S(2)}) collective-permute-start(bf16[128,768]{1,0:T(8,128)(2,1)S(1)} %get-tuple-element.132), channel_id=1, source_target_pairs={{0,256},{16,272},{32,288},{48,304},{256,0},{272,16},{288,32},{304,... | collective-permute-start | bytes 589832 | tf_op jit(solution)/shard_map/cond/branch_1_fun/ppermute | solution.py:360
  53.8 26.1 %collective-permute-start.8 = (bf16[384,128]{1,0:T(8,128)(2,1)S(1)}, bf16[384,128]{1,0:T(8,128)(2,1)}, u32[]{:S(2)}, u32[]{:S(2)}) collective-permute-start(bf16[384,128]{1,0:T(8,128)(2,1)S(1)} %get-tuple-element.284), channel_id=1, source_target_pairs={{64,16},{96,48},{128,80},{160,112},{192,144},{224,176},{256,208},{... | collective-permute-start | bytes 294920 | tf_op jit(solution)/shard_map/cond/branch_1_fun/ppermute | solution.py:371
  55.1 24.8 %collective-permute-start.7 = (bf16[384,128]{1,0:T(8,128)(2,1)S(1)}, bf16[384,128]{1,0:T(8,128)(2,1)}, u32[]{:S(2)}, u32[]{:S(2)}) collective-permute-start(bf16[384,128]{1,0:T(8,128)(2,1)S(1)} %get-tuple-element.285), channel_id=1, source_target_pairs={{32,0},{48,16},{64,32},{80,48},{96,64},{112,80},{128,96},{144,112}... | collective-permute-start | bytes 294920 | tf_op jit(solution)/shard_map/cond/branch_1_fun/ppermute | solution.py:22
